TPU v7x, 256 devices: a whole 4x4x8 slice. The times are simulated.
256 devices in a mesh: rows: 64 (over z, y, core), help: 4 (over x).
Axes of the slice: x: 4, y: 4, z: 8, core: 2. Of those that a mesh axis runs over, the one named last changes fastest.
Arguments:
- panel: bfloat16 [32, 262144], P(None, ('rows', 'help')), may hold values from -6 to 6
- tiles: bfloat16 [2, 2048, 16, 128, 128], P(None, ('rows', 'help')), may hold values from -0.125 to 0.125
- tile_cols: int32 [2048, 16], P(('rows', 'help')), may hold values from 0 to 63
- tile_count: int32 [2048], P(('rows', 'help')), may hold values from 4 to 16
- row_assign: int32 [2048], P('rows'), may hold values from 0 to 31, as said below
- send_lists: int32 [64, 2, 16], P('rows'), may hold values from 0 to 31, as said below
- centers: float32 [2], replicated, may hold values from -0.5 to 0.5
- half_widths: float32 [2], replicated, may hold values from 0.6 to 1.5
Outputs:
- filtered: bfloat16 [2, 32, 262144], P(None, None, ('rows', 'help'))
- gram: float32 [2, 2, 32, 32], replicated
Inputs may be any that keep to these rules, and one draw needn't show every extreme that they name: `row_assign`: each aligned group of 32 entries (one slab) is a permutation of 0 to 31. `send_lists`: the 16 entries of each list are distinct tile rows of the slab.
All inputs are finite; a program needn't handle non-finite values.
Results may differ from a plain program's by a relative error of at most 0.0042.
Values may be sent and summed in bfloat16 or wider, within the bound.
No kernel may reach another device: no remote copies, remote signals or barrier semaphores. Data moves between devices by JAX's collectives and lax.ppermute only.
A program may use at most 64 MiB of HBM per device.

v0:
```python
import jax
import jax.numpy as jnp
from jax import lax
from jax.sharding import PartitionSpec as P


def passed_along(value, axis, steps):
    count = lax.axis_size(axis)
    pairs = [(source, (source + steps) % count) for source in range(count)]
    return lax.ppermute(value, axis, pairs)


def multiply(extended, tiles, tile_cols, live_mask):
    picked = extended[:, :, tile_cols, :]
    picked = jnp.where(live_mask[None, None, :, :, None], picked, jnp.zeros((), picked.dtype))
    if picked.shape[0] == 1:
        return jnp.einsum("pjkc,vjkrc->vpjr", picked[0], tiles, preferred_element_type=jnp.float32)
    return jnp.einsum("vpjkc,vjkrc->vpjr", picked, tiles, preferred_element_type=jnp.float32)


def per_device(panel, tiles, tile_cols, tile_count, row_assign, send_lists, centers, half_widths):
    helpers = lax.axis_size("help")
    help_index = lax.axis_index("help")
    volumes = tiles.shape[0]
    row_tiles = tiles.shape[1]
    slot_count = tiles.shape[2]
    tile_side = tiles.shape[3]
    vectors = panel.shape[0]
    slab_size = row_tiles * helpers
    total_rows = row_tiles * tile_side * helpers * lax.axis_size("rows")
    mine = lax.dynamic_slice_in_dim(row_assign, help_index * row_tiles, row_tiles)
    onehot_full = row_assign[:, None] == jnp.arange(slab_size, dtype=jnp.int32)[None, :]
    live_mask = jnp.arange(slot_count, dtype=jnp.int32)[None, :] < tile_count[:, None]
    centre = centers[:, None, None, None]
    spread = half_widths[:, None, None, None]

    def gather_slab(shard):
        whole = lax.all_gather(shard, "help", axis=2, tiled=True)
        return whole.reshape(shard.shape[0], vectors, slab_size, tile_side)

    def extend(blocks):
        to_next = blocks[:, :, send_lists[0, 1], :]
        to_prev = blocks[:, :, send_lists[0, 0], :]
        from_left = passed_along(to_next, "rows", 1)
        from_right = passed_along(to_prev, "rows", -1)
        return jnp.concatenate([blocks, from_left, from_right], axis=2)

    def to_natural(stored, need_blocks):
        onehot_mine = lax.dynamic_slice_in_dim(
            onehot_full, help_index * row_tiles, row_tiles, 0
        ).astype(jnp.bfloat16)
        placed = jnp.einsum(
            "vpjr,jt->vptr", stored, onehot_mine, preferred_element_type=jnp.float32
        )
        placed = placed.reshape(volumes, vectors, slab_size * tile_side)
        shard = lax.psum_scatter(
            placed.astype(jnp.bfloat16), "help", scatter_dimension=2, tiled=True
        )
        blocks = gather_slab(shard) if need_blocks else None
        return (shard, blocks)

    slab_panel = gather_slab(panel[None])
    x_store = slab_panel[0][:, mine, :].astype(jnp.float32)
    first_h = multiply(extend(slab_panel), tiles, tile_cols, live_mask)
    first = ((first_h - centre * x_store[None]) / spread).astype(jnp.bfloat16)
    gram_one = jnp.einsum("vpjr,vqjr->vpq", first, first, preferred_element_type=jnp.float32)
    summed_one = lax.psum(gram_one, ("rows", "help"))
    unused_shard, first_blocks = to_natural(first, True)
    second_h = multiply(extend(first_blocks), tiles, tile_cols, live_mask)
    second = (
        2.0 * (second_h - centre * first.astype(jnp.float32)) / spread - x_store[None]
    ).astype(jnp.bfloat16)
    gram_two = jnp.einsum("vpjr,vqjr->vpq", second, second, preferred_element_type=jnp.float32)
    filtered, unused_blocks = to_natural(second, False)
    summed_two = lax.psum(gram_two, ("rows", "help"))
    gram = jnp.stack([summed_one, summed_two], axis=1) / total_rows
    return (filtered, gram)


def solution(mesh):
    placed = (
        P(None, ("rows", "help")),
        P(None, ("rows", "help"), None, None, None),
        P(("rows", "help"), None),
        P(("rows", "help")),
        P("rows"),
        P("rows", None, None),
        P(),
        P(),
    )
    return jax.shard_map(
        per_device,
        mesh=mesh,
        in_specs=placed,
        out_specs=(P(None, None, ("rows", "help")), P()),
        check_vma=False,
    )
```

profile of v0, /device:TPU:1, one launch (start us, length us, event | category | flops | bytes accessed | tf_op | source)
XLA Modules:
  0.0 177.7 jit_solution(13371522743271903468)
XLA Ops:
  7.2 0.0 reduce-scatter.3.cloned.1.call-start
  7.2 0.8 fusion.62
  8.0 11.2 %all-gather = bf16[32,4096]{1,0:T(8,128)(2,1)S(1)} all-gather(bf16[32,1024]{1,0:T(8,128)(2,1)} %param.8), channel_id=2, replica_groups=mesh['rows'=64,'help'=4] {'help'}, dimensions={1}, use_global_device_ids=true | all-gather | bytes 327680 | tf_op jit(solution)/shard_map/all_gather | solution.py:38
  19.2 0.6 gather_fusion
  19.8 4.4 %collective-permute-start = (bf16[1,32,16,128]{3,1,2,0:T(8,128)(2,1)S(1)}, bf16[1,32,16,128]{3,1,2,0:T(8,128)(2,1)S(1)}, u32[]{:S(2)}, u32[]{:S(2)}) collective-permute-start(bf16[1,32,16,128]{3,1,2,0:T(8,128)(2,1)S(1)} %bitcast.113), channel_id=1, source_target_pairs={{0,4},{4,8},{8,12},{12,16},{16,20},{20,24},{24,28},{28,32},{32,36}... | collective-permute-start | bytes 393224 | tf_op jit(solution)/shard_map/ppermute | solution.py:10
  24.2 0.6 gather_fusion.1
  24.8 0.4 collective-permute-start.1
  25.2 0.7 compare_select_fusion
  25.9 0.7 compare_select_fusion.1
  26.6 0.6 gather_fusion.3
  27.2 0.7 iota_compare_fusion.1
  27.9 0.0 copy-start.3
  27.9 0.0 copy-start
  27.9 0.0 copy-start.1
  28.0 0.1 copy.34
  28.1 0.1 reshape.120
  28.2 0.0 collective-permute-done
  28.2 1.0 collective-permute-done.1
  29.2 0.1 maximum_bitcast_fusion
  29.3 0.8 gather_fusion.2
  30.1 0.0 copy-done.3
  30.1 0.0 copy-done
  30.1 0.0 copy-done.1
  30.1 4.9 %fusion.32 = bf16[2,32,8,128]{3,1,0,2:T(8,128)(2,1)S(1)} fusion(bf16[2,8,16,128,128]{4,3,2,1,0:T(8,128)(2,1)} %param.9, bf16[8,16,32,128]{3,2,1,0:T(8,128)(2,1)S(1)} %bitcast.109, pred[8,16]{1,0:T(8,128)(4,1)S(1)} %iota_compare_fusion.1, f32[2]{0:T(128)S(1)} %copy-done, f32[32,8,128]{2,0,1:T(8,128)S(1)} %convert_bitcast_fusion, f32[2]{0:T(128)S(1)} %copy-done.1), kind=kOutput, calls=%fused_computation.26 | convolution fusion | flops 269221888 | bytes 9699472 | tf_op jit(solution)/shard_map/pjkc,vjkrc->vpjr/dot_general | solution.py:17
  35.0 0.4 fusion.6
  35.5 1.0 convert_element_type.40
  36.5 0.0 reduce-scatter.3.cloned.1.call-update
  36.5 0.0 reduce-scatter.5.cloned.1.call-start
  36.5 26.0 %reduce-scatter.3.cloned.1.call-done = bf16[2,32,1024]{2,1,0:T(8,128)(2,1)} async-done(((bf16[2,32,4096]{2,1,0:T(8,128)(2,1)}), bf16[2,32,1024]{2,1,0:T(8,128)(2,1)}) %reduce-scatter.3.cloned.1.call-update) | async-done | bytes 131088 | tf_op jit(solution)/shard_map/reduce_scatter | solution.py:56
  62.6 11.2 %all_gather.7 = bf16[2,32,4096]{2,1,0:T(8,128)(2,1)S(1)} all-gather(bf16[2,32,1024]{2,1,0:T(8,128)(2,1)} %reduce-scatter.3.cloned.1.call-done), channel_id=1, replica_groups=mesh['rows'=64,'help'=4] {'help'}, dimensions={2}, use_global_device_ids=true | all-gather | bytes 655360 | tf_op jit(solution)/shard_map/all_gather | solution.py:38
  73.8 0.1 copy_bitcast_fusion
  73.9 0.6 gather_fusion.5
  74.5 0.6 gather_fusion.4
  75.1 4.2 %collective-permute-start.3 = (bf16[2,32,16,128]{3,1,0,2:T(8,128)(2,1)S(1)}, bf16[2,32,16,128]{3,1,0,2:T(8,128)(2,1)S(1)}, u32[]{:S(2)}, u32[]{:S(2)}) collective-permute-start(bf16[2,32,16,128]{3,1,0,2:T(8,128)(2,1)S(1)} %bitcast.112), channel_id=1, source_target_pairs={{0,252},{4,0},{8,4},{12,8},{16,12},{20,16},{24,20},{28,24},{32,28}... | collective-permute-start | bytes 786440 | tf_op jit(solution)/shard_map/ppermute | solution.py:10
  79.3 1.2 collective-permute-start.2
  80.5 4.0 %collective-permute-done.3 = bf16[2,32,16,128]{3,1,0,2:T(8,128)(2,1)S(1)} collective-permute-done((bf16[2,32,16,128]{3,1,0,2:T(8,128)(2,1)S(1)}, bf16[2,32,16,128]{3,1,0,2:T(8,128)(2,1)S(1)}, u32[]{:S(2)}, u32[]{:S(2)}) %collective-permute-start.3) | collective-permute-done | bytes 262176 | tf_op jit(solution)/shard_map/ppermute | solution.py:10
  84.5 0.0 collective-permute-done.2
  84.5 0.1 pad_maximum_fusion
  84.5 0.0 copy-start.2
  84.5 0.0 copy-start.4
  84.6 1.0 gather_fusion.6
  85.5 0.0 copy-done.2
  85.5 0.0 copy-done.4
  85.5 5.4 %fusion.45 = bf16[2,32,8,128]{3,1,0,2:T(8,128)(2,1)S(1)} fusion(bf16[2,8,16,128,128]{4,3,2,1,0:T(8,128)(2,1)} %param.9, bf16[8,16,2,32,128]{4,3,2,1,0:T(8,128)(2,1)S(1)} %bitcast.108, pred[8,16]{1,0:T(8,128)(4,1)S(1)} %copy-done.4, bf16[2,32,8,128]{3,1,0,2:T(8,128)(2,1)S(1)} %fusion.32, f32[2]{0:T(128)S(1)} %copy-done, ...), kind=kOutput, calls=%fused_computation.29 | convolution fusion | flops 269942784 | bytes 10879120 | tf_op jit(solution)/shard_map/vpjkc,vjkrc->vpjr/dot_general | solution.py:18
  90.9 0.4 fusion.7
  91.4 1.0 convert_element_type.45
  92.4 0.0 reduce-scatter.5.cloned.1.call-update
  92.4 0.1 convolution_bitcast_fusion.1
  92.5 0.2 convolution_bitcast_fusion
  92.7 77.5 %all-reduce = (f32[2,1,32,32]{3,2,0,1:T(8,128)S(1)}, f32[2,1,32,32]{3,2,0,1:T(8,128)S(1)}) all-reduce(f32[2,1,32,32]{3,2,0,1:T(8,128)S(1)} %convolution_bitcast_fusion, f32[2,1,32,32]{3,2,0,1:T(8,128)S(1)} %convolution_bitcast_fusion.1), channel_id=1, replica_groups=mesh['rows'=64,'help'=4] {'rows','help'}, use_global_device_ids=true, to_apply=%region_3.4 | all-reduce | flops 4096 | bytes 32768 | tf_op jit(solution)/shard_map/psum | solution.py:75
  170.2 0.6 copy.46
  170.8 0.0 reduce-scatter.5.cloned.1.call-done
  (7 shorter events, 0.1 us)
Async XLA Ops:
  7.2 55.4 %reduce-scatter.3.cloned.1.call-start = ((), (), s32[]{:S(2)}) async-start(), calls=%async_computation.2 | async-start | bytes 655360 | tf_op jit(solution)/shard_map/reduce_scatter | solution.py:56
  19.8 8.4 %collective-permute-start = (bf16[1,32,16,128]{3,1,2,0:T(8,128)(2,1)S(1)}, bf16[1,32,16,128]{3,1,2,0:T(8,128)(2,1)S(1)}, u32[]{:S(2)}, u32[]{:S(2)}) collective-permute-start(bf16[1,32,16,128]{3,1,2,0:T(8,128)(2,1)S(1)} %bitcast.113), channel_id=1, source_target_pairs={{0,4},{4,8},{8,12},{12,16},{16,20},{20,24},{24,28},{28,32},{32,36}... | collective-permute-start | bytes 393224 | tf_op jit(solution)/shard_map/ppermute | solution.py:10
  24.8 4.5 %collective-permute-start.1 = (bf16[1,32,16,128]{3,1,2,0:T(8,128)(2,1)S(1)}, bf16[1,32,16,128]{3,1,2,0:T(8,128)(2,1)S(1)}, u32[]{:S(2)}, u32[]{:S(2)}) collective-permute-start(bf16[1,32,16,128]{3,1,2,0:T(8,128)(2,1)S(1)} %bitcast.114), channel_id=1, source_target_pairs={{0,252},{4,0},{8,4},{12,8},{16,12},{20,16},{24,20},{28,24},{32,28}... | collective-permute-start | bytes 393224 | tf_op jit(solution)/shard_map/ppermute | solution.py:10
  27.9 2.1 %copy-start.3 = (pred[8,16]{1,0:T(8,128)(4,1)}, pred[8,16]{1,0:T(8,128)(4,1)S(1)}, u32[]{:S(2)}) copy-start(pred[8,16]{1,0:T(8,128)(4,1)S(1)} %iota_compare_fusion.1) | copy-start | bytes 388
  27.9 2.1 %copy-start = (f32[2]{0:T(128)S(1)}, f32[2]{0:T(128)}, u32[]{:S(2)}) copy-start(f32[2]{0:T(128)} %param.15) | copy-start | bytes 28
  27.9 2.2 %copy-start.1 = (f32[2]{0:T(128)S(1)}, f32[2]{0:T(128)}, u32[]{:S(2)}) copy-start(f32[2]{0:T(128)} %param.14) | copy-start | bytes 28
  36.5 134.3 %reduce-scatter.5.cloned.1.call-start = ((), (), s32[]{:S(2)}) async-start(), calls=%async_computation.3 | async-start | bytes 655360 | tf_op jit(solution)/shard_map/reduce_scatter | solution.py:56
  75.1 9.3 %collective-permute-start.3 = (bf16[2,32,16,128]{3,1,0,2:T(8,128)(2,1)S(1)}, bf16[2,32,16,128]{3,1,0,2:T(8,128)(2,1)S(1)}, u32[]{:S(2)}, u32[]{:S(2)}) collective-permute-start(bf16[2,32,16,128]{3,1,0,2:T(8,128)(2,1)S(1)} %bitcast.112), channel_id=1, source_target_pairs={{0,252},{4,0},{8,4},{12,8},{16,12},{20,16},{24,20},{28,24},{32,28}... | collective-permute-start | bytes 786440 | tf_op jit(solution)/shard_map/ppermute | solution.py:10
  79.3 5.1 %collective-permute-start.2 = (bf16[2,32,16,128]{3,1,0,2:T(8,128)(2,1)S(1)}, bf16[2,32,16,128]{3,1,0,2:T(8,128)(2,1)S(1)}, u32[]{:S(2)}, u32[]{:S(2)}) collective-permute-start(bf16[2,32,16,128]{3,1,0,2:T(8,128)(2,1)S(1)} %bitcast.111), channel_id=1, source_target_pairs={{0,4},{4,8},{8,12},{12,16},{16,20},{20,24},{24,28},{28,32},{32,36}... | collective-permute-start | bytes 786440 | tf_op jit(solution)/shard_map/ppermute | solution.py:10
  84.5 1.0 copy-start.2
  84.5 1.0 copy-start.4
Sparse Core Ops, SparseCore 0:
  36.6 25.9 reduce-scatter.2
  92.5 22.9 reduce-scatter.4
where the time goes:
time: 178 us
  blocking collectives  99.9 us (56%)
  waiting for transfers between devices  31.1 us (17%)
  between operations  14.2 us (8%)
  matrix products  11.5 us (6%)
  starting transfers between devices  10.2 us (6%)
  local copies, waits for them, and re-layouts  7.67 us (4%)
  other arithmetic  3.08 us (2%)
    psum x1, blocking collectives, per_device(): summed_two = lax.psum(gram_two, ('rows', 'help'))  77.5 us
    reduce_scatter x2, waiting for transfers between devices, to_natural(): lax.psum_scatter(placed.astype(jnp.bfloat16), 'help', scatter_dimension=2...  26 us
    all_gather x2, blocking collectives, gather_slab(): whole = lax.all_gather(shard, 'help', axis=2, tiled=True)  22.4 us
    ppermute x4, starting transfers between devices, passed_along(): return lax.ppermute(value, axis, pairs)  10.1 us
    dot_general x1, matrix products, multiply(): jnp.einsum('vpjkc,vjkrc->vpjr', picked, tiles, preferred_element_type=jnp...  5.38 us
    ppermute x4, waiting for transfers between devices, passed_along(): return lax.ppermute(value, axis, pairs)  5.01 us
    dot_general x1, matrix products, multiply(): jnp.einsum('pjkc,vjkrc->vpjr', picked[0], tiles, preferred_element_type=j...  4.94 us
  transfers between devices with their start and end apart: 6, of which 3 were waited for; matrix products, arithmetic and copies ran while one was open for 3% of the time, Pallas kernels for 0%

commit v1 on v0

v1 whole, which is shorter than its diff:
```python
import functools

import jax
import jax.numpy as jnp
from jax import lax
from jax.experimental import pallas as pl
from jax.experimental.pallas import tpu as pltpu
from jax.sharding import PartitionSpec as P

CORES = 2
SIDE_CHIPS = 4
NT = (((1,), (1,)), ((), ()))
VMEM = pl.BlockSpec(memory_space=pltpu.VMEM)
SMEM = pl.BlockSpec(memory_space=pltpu.SMEM)


def spread_panel(helpers, lists, *refs):
    shards, (slab, to_pair, to_cross) = refs[:helpers], refs[helpers:]
    me = lax.axis_index("help")
    odd = lax.rem(lax.axis_index("rows"), 2)
    side = slab.shape[2]
    row_tiles = slab.shape[0] // helpers
    for d in range(helpers):
        base = (me ^ d) * row_tiles
        for j in range(row_tiles):
            slab[base + j] = shards[d][:, j * side:(j + 1) * side]
    for g in range(to_pair.shape[0]):
        to_pair[g] = slab[lists[0, 1 - odd, g]]
        to_cross[g] = slab[lists[0, odd, g]]


def spread_field(helpers, lists, assign, *refs):
    shards, (slab, to_pair, to_cross) = refs[:helpers], refs[helpers:]
    me = lax.axis_index("help")
    odd = lax.rem(lax.axis_index("rows"), 2)
    row_tiles = slab.shape[1] // helpers
    for d in range(helpers):
        base = (me ^ d) * row_tiles
        for j in range(row_tiles):
            slab[:, assign[base + j]] = shards[d][:, j]
    for g in range(to_pair.shape[1]):
        to_pair[:, g] = slab[:, lists[0, 1 - odd, g]]
        to_cross[:, g] = slab[:, lists[0, odd, g]]


def place_field(helpers, assign, *refs):
    shards, (out, natural) = refs[:helpers], refs[helpers:]
    me = lax.axis_index("help")
    row_tiles = natural.shape[1] // helpers
    side = natural.shape[3]
    for d in range(helpers):
        base = (me ^ d) * row_tiles
        for j in range(row_tiles):
            natural[:, assign[base + j]] = shards[d][:, j]
    for j in range(row_tiles):
        out[:, :, j * side:(j + 1) * side] = natural[:, me * row_tiles + j]


def tile_pair(tiles, j, k):
    return jnp.concatenate(
        [jnp.concatenate([tiles[v, j, k], tiles[v, j, k + 1]], axis=1) for v in range(tiles.shape[0])],
        axis=0,
    )


def apply_first(cols, count, assign, centers, widths, slab, pair, cross, tiles, first, gram, ext):
    volumes, row_tiles, slots, side, _ = tiles.shape
    slab_size = slab.shape[0]
    ghosts = pair.shape[0]
    vectors = slab.shape[1]
    me = lax.axis_index("help")
    odd = lax.rem(lax.axis_index("rows"), 2)
    ext[pl.ds(0, slab_size)] = slab[...]
    ext[pl.ds(slab_size + (1 - odd) * ghosts, ghosts)] = pair[...]
    ext[pl.ds(slab_size + odd * ghosts, ghosts)] = cross[...]
    for j in range(row_tiles):
        total = jnp.zeros((vectors, volumes * side), jnp.float32)
        for k in range(0, slots, 2):
            left = jnp.concatenate(
                [jnp.where(q < count[j], ext[cols[j, q]], 0).astype(ext.dtype) for q in (k, k + 1)], axis=1
            )
            total += lax.dot_general(left, tile_pair(tiles, j, k), NT, preferred_element_type=jnp.float32)
        stored = slab[assign[me * row_tiles + j]].astype(jnp.float32)
        for v in range(volumes):
            h = total[:, v * side:(v + 1) * side]
            first[v, j] = ((h - centers[v] * stored) / widths[v]).astype(first.dtype)
    for v in range(volumes):
        field = jnp.concatenate([first[v, j] for j in range(row_tiles)], axis=1)
        gram[v] = lax.dot_general(field, field, NT, preferred_element_type=jnp.float32)


def apply_second(
    cols, count, assign, centers, widths, base, slab, pair, cross, tiles, first, gram_one, second, gram, ext
):
    volumes, row_tiles, slots, side, _ = tiles.shape
    slab_size = slab.shape[1]
    ghosts = pair.shape[1]
    vectors = slab.shape[2]
    me = lax.axis_index("help")
    odd = lax.rem(lax.axis_index("rows"), 2)
    ext[:, pl.ds(0, slab_size)] = slab[...]
    ext[:, pl.ds(slab_size + (1 - odd) * ghosts, ghosts)] = pair[...]
    ext[:, pl.ds(slab_size + odd * ghosts, ghosts)] = cross[...]
    for j in range(row_tiles):
        total = jnp.zeros((volumes * vectors, volumes * side), jnp.float32)
        for k in range(0, slots, 2):
            left = jnp.concatenate(
                [
                    jnp.concatenate(
                        [
                            jnp.where(q < count[j], ext[v, cols[j, q]], 0).astype(ext.dtype)
                            for q in (k, k + 1)
                        ],
                        axis=1,
                    )
                    for v in range(volumes)
                ],
                axis=0,
            )
            total += lax.dot_general(left, tile_pair(tiles, j, k), NT, preferred_element_type=jnp.float32)
        stored = base[assign[me * row_tiles + j]].astype(jnp.float32)
        for v in range(volumes):
            h = total[v * vectors:(v + 1) * vectors, v * side:(v + 1) * side]
            inner = h - centers[v] * first[v, j].astype(jnp.float32)
            second[v, j] = (2.0 * inner / widths[v] - stored).astype(second.dtype)
    parts = [gram_one[v] for v in range(volumes)]
    for v in range(volumes):
        field = jnp.concatenate([second[v, j] for j in range(row_tiles)], axis=1)
        parts.append(lax.dot_general(field, field, NT, preferred_element_type=jnp.float32))
    gram[...] = jnp.concatenate(parts, axis=1)


def swapped(value, pairs):
    return lax.ppermute(value, ("rows", "help"), pairs)


def per_device(panel, tiles, tile_cols, tile_count, row_assign, send_lists, centers, half_widths):
    helpers = lax.axis_size("help")
    rows = lax.axis_size("rows")
    volumes, row_tiles, slots, side, _ = tiles.shape
    vectors = panel.shape[0]
    ghosts = send_lists.shape[2]
    slab_size = row_tiles * helpers
    bf16 = panel.dtype
    depth = rows // (SIDE_CHIPS * CORES)

    def at(z, y, core, x):
        return ((z * SIDE_CHIPS + y) * CORES + core) * helpers + x

    def shape(*dims):
        return jax.ShapeDtypeStruct(dims, bf16)

    def gathered(shard):
        others = [
            lax.ppermute(shard, "help", [(i, i ^ d) for i in range(helpers)]) for d in range(1, helpers)
        ]
        return [shard] + others

    def exchanged(to_pair, to_cross):
        cross_pairs = [(s, (s + 1) % rows if s % 2 else (s - 1) % rows) for s in range(rows)]
        cross = lax.ppermute(to_cross, "rows", cross_pairs)
        pair = lax.ppermute(to_pair, "rows", [(s, s ^ 1) for s in range(rows)])
        return pair, cross

    params = pltpu.CompilerParams(vmem_limit_bytes=24 * 1024 * 1024)

    base, to_pair, to_cross = pl.pallas_call(
        functools.partial(spread_panel, helpers),
        out_shape=[shape(slab_size, vectors, side)] + [shape(ghosts, vectors, side)] * 2,
        in_specs=[SMEM] + [VMEM] * helpers,
        out_specs=[VMEM] * 3,
        compiler_params=params,
        name="spread_panel",
    )(send_lists, *gathered(panel))
    pair, cross = exchanged(to_pair, to_cross)
    first, gram_one = pl.pallas_call(
        apply_first,
        out_shape=[
            shape(volumes, row_tiles, vectors, side),
            jax.ShapeDtypeStruct((volumes, vectors, vectors), jnp.float32),
        ],
        in_specs=[SMEM] * 5 + [VMEM] * 4,
        out_specs=[VMEM] * 2,
        scratch_shapes=[pltpu.VMEM((slab_size + 2 * ghosts, vectors, side), bf16)],
        compiler_params=params,
        name="apply_first",
    )(tile_cols, tile_count, row_assign, centers, half_widths, base, pair, cross, tiles)
    slab, to_pair, to_cross = pl.pallas_call(
        functools.partial(spread_field, helpers),
        out_shape=[shape(volumes, slab_size, vectors, side)] + [shape(volumes, ghosts, vectors, side)] * 2,
        in_specs=[SMEM] * 2 + [VMEM] * helpers,
        out_specs=[VMEM] * 3,
        compiler_params=params,
        name="spread_field",
    )(send_lists, row_assign, *gathered(first))
    pair, cross = exchanged(to_pair, to_cross)
    second, gram = pl.pallas_call(
        apply_second,
        out_shape=[
            shape(volumes, row_tiles, vectors, side),
            jax.ShapeDtypeStruct((vectors, 2 * volumes * vectors), jnp.float32),
        ],
        in_specs=[SMEM] * 5 + [VMEM] * 7,
        out_specs=[VMEM] * 2,
        scratch_shapes=[pltpu.VMEM((volumes, slab_size + 2 * ghosts, vectors, side), bf16)],
        compiler_params=params,
        name="apply_second",
    )(tile_cols, tile_count, row_assign, centers, half_widths, base, slab, pair, cross, tiles, first, gram_one)

    every = [(z, y, x) for z in range(depth) for y in range(SIDE_CHIPS) for x in range(helpers)]
    gram = gram + swapped(gram, [(at(z, y, 0, x), at(z, y, 1, x)) for z, y, x in every])
    gram = gram + sum(
        swapped(gram, [(at(z, y, 1, d), at(z, y, 1, 0)) for z in range(depth) for y in range(SIDE_CHIPS)])
        for d in range(1, helpers)
    )
    gram = gram + sum(
        swapped(gram, [(at(z, d, 1, 0), at(z, 0, 1, 0)) for z in range(depth)]) for d in range(1, SIDE_CHIPS)
    )
    gram = gram + sum(swapped(gram, [(at(d, 0, 1, 0), at(0, 0, 1, 0))]) for d in range(1, depth))

    second, gram = lax.optimization_barrier((second, gram))
    shards = gathered(second)

    own = lax.axis_index("rows") * helpers + lax.axis_index("help")
    gram = jnp.where(own == at(0, 0, 1, 0), gram, 0.0)
    gram = gram + sum(swapped(gram, [(at(0, 0, 1, 0), at(d, 0, 1, 0))]) for d in range(1, depth))
    gram = gram + sum(
        swapped(gram, [(at(z, 0, 1, 0), at(z, d, 1, 0)) for z in range(depth)]) for d in range(1, SIDE_CHIPS)
    )
    gram = gram + sum(
        swapped(gram, [(at(z, y, 1, 0), at(z, y, 1, d)) for z in range(depth) for y in range(SIDE_CHIPS)])
        for d in range(1, helpers)
    )
    gram = gram + swapped(gram, [(at(z, y, 1, x), at(z, y, 0, x)) for z, y, x in every])

    filtered = pl.pallas_call(
        functools.partial(place_field, helpers),
        out_shape=shape(volumes, vectors, row_tiles * side),
        in_specs=[SMEM] + [VMEM] * helpers,
        out_specs=VMEM,
        scratch_shapes=[pltpu.VMEM((volumes, slab_size, vectors, side), bf16)],
        compiler_params=params,
        name="place_field",
    )(row_assign, *shards)
    gram = gram.reshape(vectors, 2, volumes, vectors).transpose(2, 1, 0, 3)
    return filtered, gram / (row_tiles * side * helpers * rows)


def solution(mesh):
    placed = (
        P(None, ("rows", "help")),
        P(None, ("rows", "help"), None, None, None),
        P(("rows", "help"), None),
        P(("rows", "help")),
        P("rows"),
        P("rows", None, None),
        P(),
        P(),
    )
    return jax.shard_map(
        per_device,
        mesh=mesh,
        in_specs=placed,
        out_specs=(P(None, None, ("rows", "help")), P()),
        check_vma=False,
    )
```

time: 178 us -> 121 us (0.68)
  blocking collectives: 99.9 us -> 0 us
  starting transfers between devices: 10.2 us -> 58.8 us
  between operations: 14.2 us -> 1.07 us
  matrix products: 11.5 us -> 0 us
  waiting for transfers between devices: 31.1 us -> 42.2 us
  Pallas kernels: 0 us -> 9.33 us
  other arithmetic: 3.08 us -> 0.07 us
    psum x1 -> x0, blocking collectives: 77.5 us -> none  [per_device(): summed_two = lax.psum(gram_two, ('rows', 'help'))]
    ppermute x4 -> x41, starting transfers between devices: 10.1 us -> 58.8 us  [the longest x28 36.1 us: swapped(): return lax.ppermute(value, ('rows', 'help'), pairs)]
    ppermute x4 -> x41, waiting for transfers between devices: 5.01 us -> 42.2 us  [the longest x28 19.4 us: swapped(): return lax.ppermute(value, ('rows', 'help'), pairs)]
    reduce_scatter x2 -> x0, waiting for transfers between devices: 26 us -> none  [to_natural(): lax.psum_scatter(placed.astype(jnp.bfloat16), 'help', scatter_dimension=2...]
    all_gather x2 -> x0, blocking collectives: 22.4 us -> none  [gather_slab(): whole = lax.all_gather(shard, 'help', axis=2, tiled=True)]
    dot_general x6 -> x0, matrix products: 11.5 us -> none  [the longest x1 5.38 us: multiply(): jnp.einsum('vpjkc,vjkrc->vpjr', picked, tiles, preferred_element_type=jnp...]
    pallas_call x0 -> x5, Pallas kernels: none -> 9.33 us  [the longest x1 3.5 us: per_device(): pl.pallas_call(apply_second, out_shape=[shape(volumes, row_tiles, vectors...]
    unnamed x12 -> x26, local copies, waits for them, and re-layouts: 0.7 us -> 8.22 us
  transfers between devices with their start and end apart: 6 -> 41, of which waited for: 3 -> 23; matrix products, arithmetic and copies ran while one was open for 3% -> 1% of each run, Pallas kernels for 0% -> 0%
where the time goes in v1:
time: 121 us
  starting transfers between devices  58.8 us (49%)
  waiting for transfers between devices  42.2 us (35%)
  Pallas kernels  9.33 us (8%)
  local copies, waits for them, and re-layouts  8.97 us (7%)
    ppermute x28, starting transfers between devices, swapped(): return lax.ppermute(value, ('rows', 'help'), pairs)  36.1 us
    ppermute x28, waiting for transfers between devices, swapped(): return lax.ppermute(value, ('rows', 'help'), pairs)  19.4 us
    ppermute x9, waiting for transfers between devices, gathered(): lax.ppermute(shard, 'help', [(i, i ^ d) for i in range(helpers)])  13.6 us
    ppermute x9, starting transfers between devices, gathered(): lax.ppermute(shard, 'help', [(i, i ^ d) for i in range(helpers)])  12.7 us
    ppermute x2, starting transfers between devices, exchanged(): pair = lax.ppermute(to_pair, 'rows', [(s, s ^ 1) for s in range(rows)])  8.77 us
    unnamed x26, local copies, waits for them, and re-layouts  8.22 us
    ppermute x2, waiting for transfers between devices, exchanged(): cross = lax.ppermute(to_cross, 'rows', cross_pairs)  8.04 us
    pallas_call x1, Pallas kernels, per_device(): pl.pallas_call(apply_second, out_shape=[shape(volumes, row_tiles, vectors...  3.5 us
  transfers between devices with their start and end apart: 41, of which 23 were waited for; matrix products, arithmetic and copies ran while one was open for 1% of the time, Pallas kernels for 0%

profile of v1, /device:TPU:1, one launch (start us, length us, event | category | flops | bytes accessed | tf_op | source)
XLA Modules:
  0.0 120.5 jit_solution(2600307943288586472)
XLA Ops:
  0.6 2.1 %collective-permute-start = (bf16[32,1024]{1,0:T(8,128)(2,1)}, bf16[32,1024]{1,0:T(8,128)(2,1)S(1)}, u32[]{:S(2)}, u32[]{:S(2)}) collective-permute-start(bf16[32,1024]{1,0:T(8,128)(2,1)} %refs_0_.1), channel_id=1, source_target_pairs={{0,1},{1,0},{2,3},{3,2},{4,5},{5,4},{6,7},{7,6},{8,9},{9,8},{10,11... | collective-permute-start | bytes 196616 | tf_op jit(solution)/shard_map/ppermute | solution.py:155
  2.8 2.5 %collective-permute-start.1 = (bf16[32,1024]{1,0:T(8,128)(2,1)}, bf16[32,1024]{1,0:T(8,128)(2,1)S(1)}, u32[]{:S(2)}, u32[]{:S(2)}) collective-permute-start(bf16[32,1024]{1,0:T(8,128)(2,1)} %refs_0_.1), channel_id=1, source_target_pairs={{0,2},{1,3},{2,0},{3,1},{4,6},{5,7},{6,4},{7,5},{8,10},{9,11},{10,... | collective-permute-start | bytes 196616 | tf_op jit(solution)/shard_map/ppermute | solution.py:155
  5.3 2.8 %collective-permute-done.1.refs_2_ = bf16[32,1024]{1,0:T(8,128)(2,1)S(1)} collective-permute-done((bf16[32,1024]{1,0:T(8,128)(2,1)}, bf16[32,1024]{1,0:T(8,128)(2,1)S(1)}, u32[]{:S(2)}, u32[]{:S(2)}) %collective-permute-start.1) | collective-permute-done | bytes 65568 | tf_op jit(solution)/shard_map/ppermute | solution.py:155
  8.0 2.0 %collective-permute-done.2.refs_3_ = bf16[32,1024]{1,0:T(8,128)(2,1)S(1)} collective-permute-done((bf16[32,1024]{1,0:T(8,128)(2,1)}, bf16[32,1024]{1,0:T(8,128)(2,1)S(1)}, u32[]{:S(2)}, u32[]{:S(2)}) %collective-permute-start.2) | collective-permute-done | bytes 65568 | tf_op jit(solution)/shard_map/ppermute | solution.py:155
  10.1 0.8 copy-done.2
  10.9 0.7 copy-done.6
  12.2 2.2 %collective-permute-start.3 = (bf16[16,32,128]{2,1,0:T(8,128)(2,1)S(1)}, bf16[16,32,128]{2,1,0:T(8,128)(2,1)S(1)}, u32[]{:S(2)}, u32[]{:S(2)}) collective-permute-start(bf16[16,32,128]{2,1,0:T(8,128)(2,1)S(1)} %get-tuple-element.15), channel_id=1, source_target_pairs={{0,4},{4,0},{8,12},{12,8},{16,20},{20,16},{24,28},{28,24},{32,36},... | collective-permute-start | bytes 393224 | tf_op jit(solution)/shard_map/ppermute | solution.py:162
  14.4 1.3 %collective-permute-start.4 = (bf16[16,32,128]{2,1,0:T(8,128)(2,1)S(1)}, bf16[16,32,128]{2,1,0:T(8,128)(2,1)S(1)}, u32[]{:S(2)}, u32[]{:S(2)}) collective-permute-start(bf16[16,32,128]{2,1,0:T(8,128)(2,1)S(1)} %get-tuple-element.16), channel_id=1, source_target_pairs={{0,252},{4,8},{8,4},{12,16},{16,12},{20,24},{24,20},{28,32},{32,28... | collective-permute-start | bytes 393224 | tf_op jit(solution)/shard_map/ppermute | solution.py:161
  15.7 3.1 %collective-permute-done.4.cross = bf16[16,32,128]{2,1,0:T(8,128)(2,1)S(1)} collective-permute-done((bf16[16,32,128]{2,1,0:T(8,128)(2,1)S(1)}, bf16[16,32,128]{2,1,0:T(8,128)(2,1)S(1)}, u32[]{:S(2)}, u32[]{:S(2)}) %collective-permute-start.4) | collective-permute-done | bytes 131104 | tf_op jit(solution)/shard_map/ppermute | solution.py:161
  18.8 3.4 %copy-done = bf16[2,8,16,128,128]{4,3,2,1,0:T(8,128)(2,1)S(1)} copy-done((bf16[2,8,16,128,128]{4,3,2,1,0:T(8,128)(2,1)S(1)}, bf16[2,8,16,128,128]{4,3,2,1,0:T(8,128)(2,1)}, u32[]{:S(2)}) %copy-start) | copy-done | bytes 8388632
  22.2 0.7 copy-done.3
  22.9 0.7 copy-done.4
  23.5 0.7 copy-done.7
  24.2 0.7 copy-done.9
  25.5 3.3 %apply_first.1 = (bf16[2,8,32,128]{3,2,1,0:T(8,128)(2,1)S(1)}, f32[2,32,32]{2,1,0:T(8,128)S(1)}) custom-call(s32[8,16]{1,0:T(8,128)S(1)} %copy-done.3, s32[8]{0:T(128)S(1)} %copy-done.7, s32[32]{0:T(128)S(1)} %copy-done.4, f32[2]{0:T(128)S(1)} %copy-done.9, f32[2]{0:T(128)S(1)} %copy-done.11, bf16[32,32,128]{2,1,0:T(8,128)(2,1)S(1)} %get-tuple-element.14.slab.base, ...), custom_call_target="tpu_custom_call" | custom-call | tf_op jit(solution)/shard_map/apply_first/pallas_call | solution.py:176
  28.8 3.1 %collective-permute-start.6 = (bf16[2,8,32,128]{3,2,1,0:T(8,128)(2,1)S(1)}, bf16[2,8,32,128]{3,2,1,0:T(8,128)(2,1)S(1)}, u32[]{:S(2)}, u32[]{:S(2)}) collective-permute-start(bf16[2,8,32,128]{3,2,1,0:T(8,128)(2,1)S(1)} %get-tuple-element.17.refs_0_.first), channel_id=1, source_target_pairs={{0,2},{1,3},{2,0},{3,1},{4,6},{5,7},{6,4},{7,5},{8,10},{9,11},{10,... | collective-permute-start | bytes 393224 | tf_op jit(solution)/shard_map/ppermute | solution.py:155
  31.9 0.7 collective-permute-start.7
  32.7 3.0 %collective-permute-done.6.refs_2_ = bf16[2,8,32,128]{3,2,1,0:T(8,128)(2,1)S(1)} collective-permute-done((bf16[2,8,32,128]{3,2,1,0:T(8,128)(2,1)S(1)}, bf16[2,8,32,128]{3,2,1,0:T(8,128)(2,1)S(1)}, u32[]{:S(2)}, u32[]{:S(2)}) %collective-permute-start.6) | collective-permute-done | bytes 131104 | tf_op jit(solution)/shard_map/ppermute | solution.py:155
  35.7 1.4 %collective-permute-done.7.refs_3_ = bf16[2,8,32,128]{3,2,1,0:T(8,128)(2,1)S(1)} collective-permute-done((bf16[2,8,32,128]{3,2,1,0:T(8,128)(2,1)S(1)}, bf16[2,8,32,128]{3,2,1,0:T(8,128)(2,1)S(1)}, u32[]{:S(2)}, u32[]{:S(2)}) %collective-permute-start.7) | collective-permute-done | bytes 131104 | tf_op jit(solution)/shard_map/ppermute | solution.py:155
  37.7 6.6 %collective-permute-start.8 = (bf16[2,16,32,128]{3,2,1,0:T(8,128)(2,1)S(1)}, bf16[2,16,32,128]{3,2,1,0:T(8,128)(2,1)S(1)}, u32[]{:S(2)}, u32[]{:S(2)}) collective-permute-start(bf16[2,16,32,128]{3,2,1,0:T(8,128)(2,1)S(1)} %get-tuple-element.19), channel_id=1, source_target_pairs={{0,4},{4,0},{8,12},{12,8},{16,20},{20,16},{24,28},{28,24},{32,36},... | collective-permute-start | bytes 786440 | tf_op jit(solution)/shard_map/ppermute | solution.py:162
  44.3 1.2 collective-permute-done.8.pair
  45.5 4.9 %collective-permute-done.9.cross = bf16[2,16,32,128]{3,2,1,0:T(8,128)(2,1)S(1)} collective-permute-done((bf16[2,16,32,128]{3,2,1,0:T(8,128)(2,1)S(1)}, bf16[2,16,32,128]{3,2,1,0:T(8,128)(2,1)S(1)}, u32[]{:S(2)}, u32[]{:S(2)}) %collective-permute-start.9) | collective-permute-done | bytes 262176 | tf_op jit(solution)/shard_map/ppermute | solution.py:161
  50.4 3.5 %apply_second.1 = (bf16[2,8,32,128]{3,2,1,0:T(8,128)(2,1)S(1)}, f32[32,128]{1,0:T(8,128)S(1)}) custom-call(s32[8,16]{1,0:T(8,128)S(1)} %copy-done.3, s32[8]{0:T(128)S(1)} %copy-done.8, s32[32]{0:T(128)S(1)} %copy-done.5, f32[2]{0:T(128)S(1)} %copy-done.10, f32[2]{0:T(128)S(1)} %copy-done.12, bf16[32,32,128]{2,1,0:T(8,128)(2,1)S(1)} %get-tuple-element.14.slab.base, ...), custom_call_target="tpu_custom_call" | custom-call | tf_op jit(solution)/shard_map/apply_second/pallas_call | solution.py:197
  53.9 1.3 %collective-permute-start.10 = (f32[32,128]{1,0:T(8,128)S(1)}, f32[32,128]{1,0:T(8,128)S(1)}, u32[]{:S(2)}, u32[]{:S(2)}) collective-permute-start(f32[32,128]{1,0:T(8,128)S(1)} %get-tuple-element.23), channel_id=1, source_target_pairs={{0,4},{1,5},{2,6},{3,7},{8,12},{9,13},{10,14},{11,15},{16,20},{17,... | collective-permute-start | bytes 49160 | tf_op jit(solution)/shard_map/ppermute | solution.py:134
  55.2 3.8 %collective-permute-done.10 = f32[32,128]{1,0:T(8,128)S(1)} collective-permute-done((f32[32,128]{1,0:T(8,128)S(1)}, f32[32,128]{1,0:T(8,128)S(1)}, u32[]{:S(2)}, u32[]{:S(2)}) %collective-permute-start.10) | collective-permute-done | bytes 16416 | tf_op jit(solution)/shard_map/ppermute | solution.py:134
  59.0 1.3 %collective-permute-start.11 = (f32[32,128]{1,0:T(8,128)S(1)}, f32[32,128]{1,0:T(8,128)S(1)}, u32[]{:S(2)}, u32[]{:S(2)}) collective-permute-start(f32[32,128]{1,0:T(8,128)S(1)} %add.87), channel_id=1, source_target_pairs={{5,4},{13,12},{21,20},{29,28},{37,36},{45,44},{53,52},{61,60},{69,... | collective-permute-start | bytes 49160 | tf_op jit(solution)/shard_map/ppermute | solution.py:134
  60.3 1.3 %collective-permute-start.12 = (f32[32,128]{1,0:T(8,128)S(1)}, f32[32,128]{1,0:T(8,128)S(1)}, u32[]{:S(2)}, u32[]{:S(2)}) collective-permute-start(f32[32,128]{1,0:T(8,128)S(1)} %add.87), channel_id=1, source_target_pairs={{6,4},{14,12},{22,20},{30,28},{38,36},{46,44},{54,52},{62,60},{70,... | collective-permute-start | bytes 49160 | tf_op jit(solution)/shard_map/ppermute | solution.py:134
  61.6 1.3 %collective-permute-start.13 = (f32[32,128]{1,0:T(8,128)S(1)}, f32[32,128]{1,0:T(8,128)S(1)}, u32[]{:S(2)}, u32[]{:S(2)}) collective-permute-start(f32[32,128]{1,0:T(8,128)S(1)} %add.87), channel_id=1, source_target_pairs={{7,4},{15,12},{23,20},{31,28},{39,36},{47,44},{55,52},{63,60},{71,... | collective-permute-start | bytes 49160 | tf_op jit(solution)/shard_map/ppermute | solution.py:134
  63.5 2.8 %collective-permute-done.12 = f32[32,128]{1,0:T(8,128)S(1)} collective-permute-done((f32[32,128]{1,0:T(8,128)S(1)}, f32[32,128]{1,0:T(8,128)S(1)}, u32[]{:S(2)}, u32[]{:S(2)}) %collective-permute-start.12) | collective-permute-done | bytes 16416 | tf_op jit(solution)/shard_map/ppermute | solution.py:134
  66.3 1.0 collective-permute-done.13
  67.3 1.3 %collective-permute-start.14 = (f32[32,128]{1,0:T(8,128)S(1)}, f32[32,128]{1,0:T(8,128)S(1)}, u32[]{:S(2)}, u32[]{:S(2)}) collective-permute-start(f32[32,128]{1,0:T(8,128)S(1)} %add_add_fusion.5), channel_id=1, source_target_pairs={{12,4},{44,36},{76,68},{108,100},{140,132},{172,164},{204,196},{23... | collective-permute-start | bytes 49160 | tf_op jit(solution)/shard_map/ppermute | solution.py:134
  68.6 1.3 %collective-permute-start.15 = (f32[32,128]{1,0:T(8,128)S(1)}, f32[32,128]{1,0:T(8,128)S(1)}, u32[]{:S(2)}, u32[]{:S(2)}) collective-permute-start(f32[32,128]{1,0:T(8,128)S(1)} %add_add_fusion.5), channel_id=1, source_target_pairs={{20,4},{52,36},{84,68},{116,100},{148,132},{180,164},{212,196},{24... | collective-permute-start | bytes 49160 | tf_op jit(solution)/shard_map/ppermute | solution.py:134
  69.9 1.3 %collective-permute-start.16 = (f32[32,128]{1,0:T(8,128)S(1)}, f32[32,128]{1,0:T(8,128)S(1)}, u32[]{:S(2)}, u32[]{:S(2)}) collective-permute-start(f32[32,128]{1,0:T(8,128)S(1)} %add_add_fusion.5), channel_id=1, source_target_pairs={{28,4},{60,36},{92,68},{124,100},{156,132},{188,164},{220,196},{25... | collective-permute-start | bytes 49160 | tf_op jit(solution)/shard_map/ppermute | solution.py:134
  71.8 2.8 %collective-permute-done.15 = f32[32,128]{1,0:T(8,128)S(1)} collective-permute-done((f32[32,128]{1,0:T(8,128)S(1)}, f32[32,128]{1,0:T(8,128)S(1)}, u32[]{:S(2)}, u32[]{:S(2)}) %collective-permute-start.15) | collective-permute-done | bytes 16416 | tf_op jit(solution)/shard_map/ppermute | solution.py:134
  74.6 1.0 collective-permute-done.16
  75.6 1.3 %collective-permute-start.17 = (f32[32,128]{1,0:T(8,128)S(1)}, f32[32,128]{1,0:T(8,128)S(1)}, u32[]{:S(2)}, u32[]{:S(2)}) collective-permute-start(f32[32,128]{1,0:T(8,128)S(1)} %add_add_fusion.4), channel_id=1, source_target_pairs={{36,4}} | collective-permute-start | bytes 49160 | tf_op jit(solution)/shard_map/ppermute | solution.py:134
  76.9 1.3 %collective-permute-start.18 = (f32[32,128]{1,0:T(8,128)S(1)}, f32[32,128]{1,0:T(8,128)S(1)}, u32[]{:S(2)}, u32[]{:S(2)}) collective-permute-start(f32[32,128]{1,0:T(8,128)S(1)} %add_add_fusion.4), channel_id=1, source_target_pairs={{68,4}} | collective-permute-start | bytes 49160 | tf_op jit(solution)/shard_map/ppermute | solution.py:134
  78.2 1.3 %collective-permute-start.19 = (f32[32,128]{1,0:T(8,128)S(1)}, f32[32,128]{1,0:T(8,128)S(1)}, u32[]{:S(2)}, u32[]{:S(2)}) collective-permute-start(f32[32,128]{1,0:T(8,128)S(1)} %add_add_fusion.4), channel_id=1, source_target_pairs={{100,4}} | collective-permute-start | bytes 49160 | tf_op jit(solution)/shard_map/ppermute | solution.py:134
  79.5 1.3 %collective-permute-start.20 = (f32[32,128]{1,0:T(8,128)S(1)}, f32[32,128]{1,0:T(8,128)S(1)}, u32[]{:S(2)}, u32[]{:S(2)}) collective-permute-start(f32[32,128]{1,0:T(8,128)S(1)} %add_add_fusion.4), channel_id=1, source_target_pairs={{132,4}} | collective-permute-start | bytes 49160 | tf_op jit(solution)/shard_map/ppermute | solution.py:134
  80.8 1.3 %collective-permute-start.21 = (f32[32,128]{1,0:T(8,128)S(1)}, f32[32,128]{1,0:T(8,128)S(1)}, u32[]{:S(2)}, u32[]{:S(2)}) collective-permute-start(f32[32,128]{1,0:T(8,128)S(1)} %add_add_fusion.4), channel_id=1, source_target_pairs={{164,4}} | collective-permute-start | bytes 49160 | tf_op jit(solution)/shard_map/ppermute | solution.py:134
  82.1 1.3 %collective-permute-start.22 = (f32[32,128]{1,0:T(8,128)S(1)}, f32[32,128]{1,0:T(8,128)S(1)}, u32[]{:S(2)}, u32[]{:S(2)}) collective-permute-start(f32[32,128]{1,0:T(8,128)S(1)} %add_add_fusion.4), channel_id=1, source_target_pairs={{196,4}} | collective-permute-start | bytes 49160 | tf_op jit(solution)/shard_map/ppermute | solution.py:134
  83.4 1.3 %collective-permute-start.23 = (f32[32,128]{1,0:T(8,128)S(1)}, f32[32,128]{1,0:T(8,128)S(1)}, u32[]{:S(2)}, u32[]{:S(2)}) collective-permute-start(f32[32,128]{1,0:T(8,128)S(1)} %add_add_fusion.4), channel_id=1, source_target_pairs={{228,4}} | collective-permute-start | bytes 49160 | tf_op jit(solution)/shard_map/ppermute | solution.py:134
  84.7 3.2 %collective-permute-done.20 = f32[32,128]{1,0:T(8,128)S(1)} collective-permute-done((f32[32,128]{1,0:T(8,128)S(1)}, f32[32,128]{1,0:T(8,128)S(1)}, u32[]{:S(2)}, u32[]{:S(2)}) %collective-permute-start.20) | collective-permute-done | bytes 16416 | tf_op jit(solution)/shard_map/ppermute | solution.py:134
  89.1 1.3 %collective-permute-start.27 = (f32[32,128]{1,0:T(8,128)S(1)}, f32[32,128]{1,0:T(8,128)S(1)}, u32[]{:S(2)}, u32[]{:S(2)}) collective-permute-start(f32[32,128]{1,0:T(8,128)S(1)} %broadcast_select_fusion), channel_id=1, source_target_pairs={{4,36}} | collective-permute-start | bytes 49160 | tf_op jit(solution)/shard_map/ppermute | solution.py:134
  90.4 1.3 %collective-permute-start.28 = (f32[32,128]{1,0:T(8,128)S(1)}, f32[32,128]{1,0:T(8,128)S(1)}, u32[]{:S(2)}, u32[]{:S(2)}) collective-permute-start(f32[32,128]{1,0:T(8,128)S(1)} %broadcast_select_fusion), channel_id=1, source_target_pairs={{4,68}} | collective-permute-start | bytes 49160 | tf_op jit(solution)/shard_map/ppermute | solution.py:134
  91.7 1.3 %collective-permute-start.29 = (f32[32,128]{1,0:T(8,128)S(1)}, f32[32,128]{1,0:T(8,128)S(1)}, u32[]{:S(2)}, u32[]{:S(2)}) collective-permute-start(f32[32,128]{1,0:T(8,128)S(1)} %broadcast_select_fusion), channel_id=1, source_target_pairs={{4,100}} | collective-permute-start | bytes 49160 | tf_op jit(solution)/shard_map/ppermute | solution.py:134
  93.0 1.3 %collective-permute-start.30 = (f32[32,128]{1,0:T(8,128)S(1)}, f32[32,128]{1,0:T(8,128)S(1)}, u32[]{:S(2)}, u32[]{:S(2)}) collective-permute-start(f32[32,128]{1,0:T(8,128)S(1)} %broadcast_select_fusion), channel_id=1, source_target_pairs={{4,132}} | collective-permute-start | bytes 49160 | tf_op jit(solution)/shard_map/ppermute | solution.py:134
  94.3 1.3 %collective-permute-start.31 = (f32[32,128]{1,0:T(8,128)S(1)}, f32[32,128]{1,0:T(8,128)S(1)}, u32[]{:S(2)}, u32[]{:S(2)}) collective-permute-start(f32[32,128]{1,0:T(8,128)S(1)} %broadcast_select_fusion), channel_id=1, source_target_pairs={{4,164}} | collective-permute-start | bytes 49160 | tf_op jit(solution)/shard_map/ppermute | solution.py:134
  95.6 1.3 %collective-permute-start.32 = (f32[32,128]{1,0:T(8,128)S(1)}, f32[32,128]{1,0:T(8,128)S(1)}, u32[]{:S(2)}, u32[]{:S(2)}) collective-permute-start(f32[32,128]{1,0:T(8,128)S(1)} %broadcast_select_fusion), channel_id=1, source_target_pairs={{4,196}} | collective-permute-start | bytes 49160 | tf_op jit(solution)/shard_map/ppermute | solution.py:134
  96.9 1.3 %collective-permute-start.33 = (f32[32,128]{1,0:T(8,128)S(1)}, f32[32,128]{1,0:T(8,128)S(1)}, u32[]{:S(2)}, u32[]{:S(2)}) collective-permute-start(f32[32,128]{1,0:T(8,128)S(1)} %broadcast_select_fusion), channel_id=1, source_target_pairs={{4,228}} | collective-permute-start | bytes 49160 | tf_op jit(solution)/shard_map/ppermute | solution.py:134
  98.3 0.8 collective-permute-done.33
  99.1 1.3 %collective-permute-start.34 = (f32[32,128]{1,0:T(8,128)S(1)}, f32[32,128]{1,0:T(8,128)S(1)}, u32[]{:S(2)}, u32[]{:S(2)}) collective-permute-start(f32[32,128]{1,0:T(8,128)S(1)} %add_add_fusion.2), channel_id=1, source_target_pairs={{4,12},{36,44},{68,76},{100,108},{132,140},{164,172},{196,204},{22... | collective-permute-start | bytes 49160 | tf_op jit(solution)/shard_map/ppermute | solution.py:134
  100.4 1.3 %collective-permute-start.35 = (f32[32,128]{1,0:T(8,128)S(1)}, f32[32,128]{1,0:T(8,128)S(1)}, u32[]{:S(2)}, u32[]{:S(2)}) collective-permute-start(f32[32,128]{1,0:T(8,128)S(1)} %add_add_fusion.2), channel_id=1, source_target_pairs={{4,20},{36,52},{68,84},{100,116},{132,148},{164,180},{196,212},{22... | collective-permute-start | bytes 49160 | tf_op jit(solution)/shard_map/ppermute | solution.py:134
  101.7 1.3 %collective-permute-start.36 = (f32[32,128]{1,0:T(8,128)S(1)}, f32[32,128]{1,0:T(8,128)S(1)}, u32[]{:S(2)}, u32[]{:S(2)}) collective-permute-start(f32[32,128]{1,0:T(8,128)S(1)} %add_add_fusion.2), channel_id=1, source_target_pairs={{4,28},{36,60},{68,92},{100,124},{132,156},{164,188},{196,220},{22... | collective-permute-start | bytes 49160 | tf_op jit(solution)/shard_map/ppermute | solution.py:134
  103.0 0.8 collective-permute-done.36
  103.9 1.3 %collective-permute-start.37 = (f32[32,128]{1,0:T(8,128)S(1)}, f32[32,128]{1,0:T(8,128)S(1)}, u32[]{:S(2)}, u32[]{:S(2)}) collective-permute-start(f32[32,128]{1,0:T(8,128)S(1)} %add_add_fusion.1), channel_id=1, source_target_pairs={{4,5},{12,13},{20,21},{28,29},{36,37},{44,45},{52,53},{60,61},{68,... | collective-permute-start | bytes 49160 | tf_op jit(solution)/shard_map/ppermute | solution.py:134
  105.1 1.3 %collective-permute-start.38 = (f32[32,128]{1,0:T(8,128)S(1)}, f32[32,128]{1,0:T(8,128)S(1)}, u32[]{:S(2)}, u32[]{:S(2)}) collective-permute-start(f32[32,128]{1,0:T(8,128)S(1)} %add_add_fusion.1), channel_id=1, source_target_pairs={{4,6},{12,14},{20,22},{28,30},{36,38},{44,46},{52,54},{60,62},{68,... | collective-permute-start | bytes 49160 | tf_op jit(solution)/shard_map/ppermute | solution.py:134
  106.4 1.3 %collective-permute-start.39 = (f32[32,128]{1,0:T(8,128)S(1)}, f32[32,128]{1,0:T(8,128)S(1)}, u32[]{:S(2)}, u32[]{:S(2)}) collective-permute-start(f32[32,128]{1,0:T(8,128)S(1)} %add_add_fusion.1), channel_id=1, source_target_pairs={{4,7},{12,15},{20,23},{28,31},{36,39},{44,47},{52,55},{60,63},{68,... | collective-permute-start | bytes 49160 | tf_op jit(solution)/shard_map/ppermute | solution.py:134
  107.8 0.8 collective-permute-done.39
  108.6 1.3 %collective-permute-start.40 = (f32[32,128]{1,0:T(8,128)S(1)}, f32[32,128]{1,0:T(8,128)S(1)}, u32[]{:S(2)}, u32[]{:S(2)}) collective-permute-start(f32[32,128]{1,0:T(8,128)S(1)} %add_add_fusion), channel_id=1, source_target_pairs={{4,0},{5,1},{6,2},{7,3},{12,8},{13,9},{14,10},{15,11},{20,16},{21,... | collective-permute-start | bytes 49160 | tf_op jit(solution)/shard_map/ppermute | solution.py:134
  110.0 4.1 %collective-permute-start.25 = (bf16[2,8,32,128]{3,2,1,0:T(8,128)(2,1)S(1)}, bf16[2,8,32,128]{3,2,1,0:T(8,128)(2,1)S(1)}, u32[]{:S(2)}, u32[]{:S(2)}) collective-permute-start(bf16[2,8,32,128]{3,2,1,0:T(8,128)(2,1)S(1)} %get-tuple-element.24.refs_0_), channel_id=1, source_target_pairs={{0,2},{1,3},{2,0},{3,1},{4,6},{5,7},{6,4},{7,5},{8,10},{9,11},{10,... | collective-permute-start | bytes 393224 | tf_op jit(solution)/shard_map/ppermute | solution.py:155
  114.9 3.0 %collective-permute-done.25.refs_2_ = bf16[2,8,32,128]{3,2,1,0:T(8,128)(2,1)S(1)} collective-permute-done((bf16[2,8,32,128]{3,2,1,0:T(8,128)(2,1)S(1)}, bf16[2,8,32,128]{3,2,1,0:T(8,128)(2,1)S(1)}, u32[]{:S(2)}, u32[]{:S(2)}) %collective-permute-start.25) | collective-permute-done | bytes 131104 | tf_op jit(solution)/shard_map/ppermute | solution.py:155
  117.9 1.4 %collective-permute-done.26.refs_3_ = bf16[2,8,32,128]{3,2,1,0:T(8,128)(2,1)S(1)} collective-permute-done((bf16[2,8,32,128]{3,2,1,0:T(8,128)(2,1)S(1)}, bf16[2,8,32,128]{3,2,1,0:T(8,128)(2,1)S(1)}, u32[]{:S(2)}, u32[]{:S(2)}) %collective-permute-start.26) | collective-permute-done | bytes 131104 | tf_op jit(solution)/shard_map/ppermute | solution.py:155
  119.2 1.3 %place_field.1 = bf16[2,32,1024]{2,1,0:T(8,128)(2,1)} custom-call(s32[32]{0:T(128)S(1)} %copy-done.5, bf16[2,8,32,128]{3,2,1,0:T(8,128)(2,1)S(1)} %get-tuple-element.24.refs_0_, bf16[2,8,32,128]{3,2,1,0:T(8,128)(2,1)S(1)} %collective-permute-done.24.refs_1_, bf16[2,8,32,128]{3,2,1,0:T(8,128)(2,1)S(1)} %collective-permute-done.25.refs_2_, ...), custom_call_target="tpu_custom_call" | custom-call | tf_op jit(solution)/shard_map/place_field/pallas_call | solution.py:236
  (60 shorter events, 5.4 us)
Async XLA Ops:
  0.6 4.6 %collective-permute-start = (bf16[32,1024]{1,0:T(8,128)(2,1)}, bf16[32,1024]{1,0:T(8,128)(2,1)S(1)}, u32[]{:S(2)}, u32[]{:S(2)}) collective-permute-start(bf16[32,1024]{1,0:T(8,128)(2,1)} %refs_0_.1), channel_id=1, source_target_pairs={{0,1},{1,0},{2,3},{3,2},{4,5},{5,4},{6,7},{7,6},{8,9},{9,8},{10,11... | collective-permute-start | bytes 196616 | tf_op jit(solution)/shard_map/ppermute | solution.py:155
  2.8 5.3 %collective-permute-start.1 = (bf16[32,1024]{1,0:T(8,128)(2,1)}, bf16[32,1024]{1,0:T(8,128)(2,1)S(1)}, u32[]{:S(2)}, u32[]{:S(2)}) collective-permute-start(bf16[32,1024]{1,0:T(8,128)(2,1)} %refs_0_.1), channel_id=1, source_target_pairs={{0,2},{1,3},{2,0},{3,1},{4,6},{5,7},{6,4},{7,5},{8,10},{9,11},{10,... | collective-permute-start | bytes 196616 | tf_op jit(solution)/shard_map/ppermute | solution.py:155
  5.2 4.8 %collective-permute-start.2 = (bf16[32,1024]{1,0:T(8,128)(2,1)}, bf16[32,1024]{1,0:T(8,128)(2,1)S(1)}, u32[]{:S(2)}, u32[]{:S(2)}) collective-permute-start(bf16[32,1024]{1,0:T(8,128)(2,1)} %refs_0_.1), channel_id=1, source_target_pairs={{0,3},{1,2},{2,1},{3,0},{4,7},{5,6},{6,5},{7,4},{8,11},{9,10},{10,... | collective-permute-start | bytes 196616 | tf_op jit(solution)/shard_map/ppermute | solution.py:155
  10.1 0.8 copy-start.2
  10.9 0.7 copy-start.6
  11.6 25.5 %copy-start.5 = (s32[32]{0:T(128)S(1)}, s32[32]{0:T(128)}, u32[]{:S(2)}) copy-start(s32[32]{0:T(128)} %assign.7) | copy-start | bytes 388
  11.6 38.8 %copy-start.8 = (s32[8]{0:T(128)S(1)}, s32[8]{0:T(128)}, u32[]{:S(2)}) copy-start(s32[8]{0:T(128)} %count.3) | copy-start | bytes 100
  11.6 38.8 %copy-start.10 = (f32[2]{0:T(128)S(1)}, f32[2]{0:T(128)}, u32[]{:S(2)}) copy-start(f32[2]{0:T(128)} %centers.3) | copy-start | bytes 28
  11.6 38.8 %copy-start.12 = (f32[2]{0:T(128)S(1)}, f32[2]{0:T(128)}, u32[]{:S(2)}) copy-start(f32[2]{0:T(128)} %widths.3) | copy-start | bytes 28
  12.2 3.5 %collective-permute-start.3 = (bf16[16,32,128]{2,1,0:T(8,128)(2,1)S(1)}, bf16[16,32,128]{2,1,0:T(8,128)(2,1)S(1)}, u32[]{:S(2)}, u32[]{:S(2)}) collective-permute-start(bf16[16,32,128]{2,1,0:T(8,128)(2,1)S(1)} %get-tuple-element.15), channel_id=1, source_target_pairs={{0,4},{4,0},{8,12},{12,8},{16,20},{20,16},{24,28},{28,24},{32,36},... | collective-permute-start | bytes 393224 | tf_op jit(solution)/shard_map/ppermute | solution.py:162
  14.4 4.4 %collective-permute-start.4 = (bf16[16,32,128]{2,1,0:T(8,128)(2,1)S(1)}, bf16[16,32,128]{2,1,0:T(8,128)(2,1)S(1)}, u32[]{:S(2)}, u32[]{:S(2)}) collective-permute-start(bf16[16,32,128]{2,1,0:T(8,128)(2,1)S(1)} %get-tuple-element.16), channel_id=1, source_target_pairs={{0,252},{4,8},{8,4},{12,16},{16,12},{20,24},{24,20},{28,32},{32,28... | collective-permute-start | bytes 393224 | tf_op jit(solution)/shard_map/ppermute | solution.py:161
  18.8 3.4 %copy-start = (bf16[2,8,16,128,128]{4,3,2,1,0:T(8,128)(2,1)S(1)}, bf16[2,8,16,128,128]{4,3,2,1,0:T(8,128)(2,1)}, u32[]{:S(2)}) copy-start(bf16[2,8,16,128,128]{4,3,2,1,0:T(8,128)(2,1)} %tiles.3) | copy-start | bytes 25165828
  22.2 0.7 copy-start.3
  22.9 0.7 copy-start.4
  23.5 0.7 copy-start.7
  24.2 0.7 copy-start.9
  24.8 0.7 copy-start.11
  25.5 24.9 %copy-start.1 = (bf16[2,8,16,128,128]{4,3,2,1,0:T(8,128)(2,1)S(1)}, bf16[2,8,16,128,128]{4,3,2,1,0:T(8,128)(2,1)}, u32[]{:S(2)}) copy-start(bf16[2,8,16,128,128]{4,3,2,1,0:T(8,128)(2,1)} %tiles.3) | copy-start | bytes 25165828
  28.8 3.9 %collective-permute-start.5 = (bf16[2,8,32,128]{3,2,1,0:T(8,128)(2,1)S(1)}, bf16[2,8,32,128]{3,2,1,0:T(8,128)(2,1)S(1)}, u32[]{:S(2)}, u32[]{:S(2)}) collective-permute-start(bf16[2,8,32,128]{3,2,1,0:T(8,128)(2,1)S(1)} %get-tuple-element.17.refs_0_.first), channel_id=1, source_target_pairs={{0,1},{1,0},{2,3},{3,2},{4,5},{5,4},{6,7},{7,6},{8,9},{9,8},{10,11... | collective-permute-start | bytes 393224 | tf_op jit(solution)/shard_map/ppermute | solution.py:155
  28.8 6.9 %collective-permute-start.6 = (bf16[2,8,32,128]{3,2,1,0:T(8,128)(2,1)S(1)}, bf16[2,8,32,128]{3,2,1,0:T(8,128)(2,1)S(1)}, u32[]{:S(2)}, u32[]{:S(2)}) collective-permute-start(bf16[2,8,32,128]{3,2,1,0:T(8,128)(2,1)S(1)} %get-tuple-element.17.refs_0_.first), channel_id=1, source_target_pairs={{0,2},{1,3},{2,0},{3,1},{4,6},{5,7},{6,4},{7,5},{8,10},{9,11},{10,... | collective-permute-start | bytes 393224 | tf_op jit(solution)/shard_map/ppermute | solution.py:155
  31.9 5.2 %collective-permute-start.7 = (bf16[2,8,32,128]{3,2,1,0:T(8,128)(2,1)S(1)}, bf16[2,8,32,128]{3,2,1,0:T(8,128)(2,1)S(1)}, u32[]{:S(2)}, u32[]{:S(2)}) collective-permute-start(bf16[2,8,32,128]{3,2,1,0:T(8,128)(2,1)S(1)} %get-tuple-element.17.refs_0_.first), channel_id=1, source_target_pairs={{0,3},{1,2},{2,1},{3,0},{4,7},{5,6},{6,5},{7,4},{8,11},{9,10},{10,... | collective-permute-start | bytes 393224 | tf_op jit(solution)/shard_map/ppermute | solution.py:155
  37.7 7.8 %collective-permute-start.8 = (bf16[2,16,32,128]{3,2,1,0:T(8,128)(2,1)S(1)}, bf16[2,16,32,128]{3,2,1,0:T(8,128)(2,1)S(1)}, u32[]{:S(2)}, u32[]{:S(2)}) collective-permute-start(bf16[2,16,32,128]{3,2,1,0:T(8,128)(2,1)S(1)} %get-tuple-element.19), channel_id=1, source_target_pairs={{0,4},{4,0},{8,12},{12,8},{16,20},{20,16},{24,28},{28,24},{32,36},... | collective-permute-start | bytes 786440 | tf_op jit(solution)/shard_map/ppermute | solution.py:162
  44.3 6.1 %collective-permute-start.9 = (bf16[2,16,32,128]{3,2,1,0:T(8,128)(2,1)S(1)}, bf16[2,16,32,128]{3,2,1,0:T(8,128)(2,1)S(1)}, u32[]{:S(2)}, u32[]{:S(2)}) collective-permute-start(bf16[2,16,32,128]{3,2,1,0:T(8,128)(2,1)S(1)} %get-tuple-element.20), channel_id=1, source_target_pairs={{0,252},{4,8},{8,4},{12,16},{16,12},{20,24},{24,20},{28,32},{32,28... | collective-permute-start | bytes 786440 | tf_op jit(solution)/shard_map/ppermute | solution.py:161
  53.9 5.1 %collective-permute-start.10 = (f32[32,128]{1,0:T(8,128)S(1)}, f32[32,128]{1,0:T(8,128)S(1)}, u32[]{:S(2)}, u32[]{:S(2)}) collective-permute-start(f32[32,128]{1,0:T(8,128)S(1)} %get-tuple-element.23), channel_id=1, source_target_pairs={{0,4},{1,5},{2,6},{3,7},{8,12},{9,13},{10,14},{11,15},{16,20},{17,... | collective-permute-start | bytes 49160 | tf_op jit(solution)/shard_map/ppermute | solution.py:134
  59.0 4.5 %collective-permute-start.11 = (f32[32,128]{1,0:T(8,128)S(1)}, f32[32,128]{1,0:T(8,128)S(1)}, u32[]{:S(2)}, u32[]{:S(2)}) collective-permute-start(f32[32,128]{1,0:T(8,128)S(1)} %add.87), channel_id=1, source_target_pairs={{5,4},{13,12},{21,20},{29,28},{37,36},{45,44},{53,52},{61,60},{69,... | collective-permute-start | bytes 49160 | tf_op jit(solution)/shard_map/ppermute | solution.py:134
  60.3 6.0 %collective-permute-start.12 = (f32[32,128]{1,0:T(8,128)S(1)}, f32[32,128]{1,0:T(8,128)S(1)}, u32[]{:S(2)}, u32[]{:S(2)}) collective-permute-start(f32[32,128]{1,0:T(8,128)S(1)} %add.87), channel_id=1, source_target_pairs={{6,4},{14,12},{22,20},{30,28},{38,36},{46,44},{54,52},{62,60},{70,... | collective-permute-start | bytes 49160 | tf_op jit(solution)/shard_map/ppermute | solution.py:134
  61.6 5.7 %collective-permute-start.13 = (f32[32,128]{1,0:T(8,128)S(1)}, f32[32,128]{1,0:T(8,128)S(1)}, u32[]{:S(2)}, u32[]{:S(2)}) collective-permute-start(f32[32,128]{1,0:T(8,128)S(1)} %add.87), channel_id=1, source_target_pairs={{7,4},{15,12},{23,20},{31,28},{39,36},{47,44},{55,52},{63,60},{71,... | collective-permute-start | bytes 49160 | tf_op jit(solution)/shard_map/ppermute | solution.py:134
  67.3 4.5 %collective-permute-start.14 = (f32[32,128]{1,0:T(8,128)S(1)}, f32[32,128]{1,0:T(8,128)S(1)}, u32[]{:S(2)}, u32[]{:S(2)}) collective-permute-start(f32[32,128]{1,0:T(8,128)S(1)} %add_add_fusion.5), channel_id=1, source_target_pairs={{12,4},{44,36},{76,68},{108,100},{140,132},{172,164},{204,196},{23... | collective-permute-start | bytes 49160 | tf_op jit(solution)/shard_map/ppermute | solution.py:134
  68.6 6.0 %collective-permute-start.15 = (f32[32,128]{1,0:T(8,128)S(1)}, f32[32,128]{1,0:T(8,128)S(1)}, u32[]{:S(2)}, u32[]{:S(2)}) collective-permute-start(f32[32,128]{1,0:T(8,128)S(1)} %add_add_fusion.5), channel_id=1, source_target_pairs={{20,4},{52,36},{84,68},{116,100},{148,132},{180,164},{212,196},{24... | collective-permute-start | bytes 49160 | tf_op jit(solution)/shard_map/ppermute | solution.py:134
  69.9 5.7 %collective-permute-start.16 = (f32[32,128]{1,0:T(8,128)S(1)}, f32[32,128]{1,0:T(8,128)S(1)}, u32[]{:S(2)}, u32[]{:S(2)}) collective-permute-start(f32[32,128]{1,0:T(8,128)S(1)} %add_add_fusion.5), channel_id=1, source_target_pairs={{28,4},{60,36},{92,68},{124,100},{156,132},{188,164},{220,196},{25... | collective-permute-start | bytes 49160 | tf_op jit(solution)/shard_map/ppermute | solution.py:134
  75.6 6.5 %collective-permute-start.17 = (f32[32,128]{1,0:T(8,128)S(1)}, f32[32,128]{1,0:T(8,128)S(1)}, u32[]{:S(2)}, u32[]{:S(2)}) collective-permute-start(f32[32,128]{1,0:T(8,128)S(1)} %add_add_fusion.4), channel_id=1, source_target_pairs={{36,4}} | collective-permute-start | bytes 49160 | tf_op jit(solution)/shard_map/ppermute | solution.py:134
  76.9 6.5 %collective-permute-start.18 = (f32[32,128]{1,0:T(8,128)S(1)}, f32[32,128]{1,0:T(8,128)S(1)}, u32[]{:S(2)}, u32[]{:S(2)}) collective-permute-start(f32[32,128]{1,0:T(8,128)S(1)} %add_add_fusion.4), channel_id=1, source_target_pairs={{68,4}} | collective-permute-start | bytes 49160 | tf_op jit(solution)/shard_map/ppermute | solution.py:134
  78.2 6.5 %collective-permute-start.19 = (f32[32,128]{1,0:T(8,128)S(1)}, f32[32,128]{1,0:T(8,128)S(1)}, u32[]{:S(2)}, u32[]{:S(2)}) collective-permute-start(f32[32,128]{1,0:T(8,128)S(1)} %add_add_fusion.4), channel_id=1, source_target_pairs={{100,4}} | collective-permute-start | bytes 49160 | tf_op jit(solution)/shard_map/ppermute | solution.py:134
  79.5 8.4 %collective-permute-start.20 = (f32[32,128]{1,0:T(8,128)S(1)}, f32[32,128]{1,0:T(8,128)S(1)}, u32[]{:S(2)}, u32[]{:S(2)}) collective-permute-start(f32[32,128]{1,0:T(8,128)S(1)} %add_add_fusion.4), channel_id=1, source_target_pairs={{132,4}} | collective-permute-start | bytes 49160 | tf_op jit(solution)/shard_map/ppermute | solution.py:134
  80.8 7.5 %collective-permute-start.21 = (f32[32,128]{1,0:T(8,128)S(1)}, f32[32,128]{1,0:T(8,128)S(1)}, u32[]{:S(2)}, u32[]{:S(2)}) collective-permute-start(f32[32,128]{1,0:T(8,128)S(1)} %add_add_fusion.4), channel_id=1, source_target_pairs={{164,4}} | collective-permute-start | bytes 49160 | tf_op jit(solution)/shard_map/ppermute | solution.py:134
  82.1 6.6 %collective-permute-start.22 = (f32[32,128]{1,0:T(8,128)S(1)}, f32[32,128]{1,0:T(8,128)S(1)}, u32[]{:S(2)}, u32[]{:S(2)}) collective-permute-start(f32[32,128]{1,0:T(8,128)S(1)} %add_add_fusion.4), channel_id=1, source_target_pairs={{196,4}} | collective-permute-start | bytes 49160 | tf_op jit(solution)/shard_map/ppermute | solution.py:134
  83.4 5.7 %collective-permute-start.23 = (f32[32,128]{1,0:T(8,128)S(1)}, f32[32,128]{1,0:T(8,128)S(1)}, u32[]{:S(2)}, u32[]{:S(2)}) collective-permute-start(f32[32,128]{1,0:T(8,128)S(1)} %add_add_fusion.4), channel_id=1, source_target_pairs={{228,4}} | collective-permute-start | bytes 49160 | tf_op jit(solution)/shard_map/ppermute | solution.py:134
  89.1 6.5 %collective-permute-start.27 = (f32[32,128]{1,0:T(8,128)S(1)}, f32[32,128]{1,0:T(8,128)S(1)}, u32[]{:S(2)}, u32[]{:S(2)}) collective-permute-start(f32[32,128]{1,0:T(8,128)S(1)} %broadcast_select_fusion), channel_id=1, source_target_pairs={{4,36}} | collective-permute-start | bytes 49160 | tf_op jit(solution)/shard_map/ppermute | solution.py:134
  90.4 6.5 %collective-permute-start.28 = (f32[32,128]{1,0:T(8,128)S(1)}, f32[32,128]{1,0:T(8,128)S(1)}, u32[]{:S(2)}, u32[]{:S(2)}) collective-permute-start(f32[32,128]{1,0:T(8,128)S(1)} %broadcast_select_fusion), channel_id=1, source_target_pairs={{4,68}} | collective-permute-start | bytes 49160 | tf_op jit(solution)/shard_map/ppermute | solution.py:134
  91.7 6.5 %collective-permute-start.29 = (f32[32,128]{1,0:T(8,128)S(1)}, f32[32,128]{1,0:T(8,128)S(1)}, u32[]{:S(2)}, u32[]{:S(2)}) collective-permute-start(f32[32,128]{1,0:T(8,128)S(1)} %broadcast_select_fusion), channel_id=1, source_target_pairs={{4,100}} | collective-permute-start | bytes 49160 | tf_op jit(solution)/shard_map/ppermute | solution.py:134
  93.0 5.2 %collective-permute-start.30 = (f32[32,128]{1,0:T(8,128)S(1)}, f32[32,128]{1,0:T(8,128)S(1)}, u32[]{:S(2)}, u32[]{:S(2)}) collective-permute-start(f32[32,128]{1,0:T(8,128)S(1)} %broadcast_select_fusion), channel_id=1, source_target_pairs={{4,132}} | collective-permute-start | bytes 49160 | tf_op jit(solution)/shard_map/ppermute | solution.py:134
  94.3 3.9 %collective-permute-start.31 = (f32[32,128]{1,0:T(8,128)S(1)}, f32[32,128]{1,0:T(8,128)S(1)}, u32[]{:S(2)}, u32[]{:S(2)}) collective-permute-start(f32[32,128]{1,0:T(8,128)S(1)} %broadcast_select_fusion), channel_id=1, source_target_pairs={{4,164}} | collective-permute-start | bytes 49160 | tf_op jit(solution)/shard_map/ppermute | solution.py:134
  95.6 2.6 %collective-permute-start.32 = (f32[32,128]{1,0:T(8,128)S(1)}, f32[32,128]{1,0:T(8,128)S(1)}, u32[]{:S(2)}, u32[]{:S(2)}) collective-permute-start(f32[32,128]{1,0:T(8,128)S(1)} %broadcast_select_fusion), channel_id=1, source_target_pairs={{4,196}} | collective-permute-start | bytes 49160 | tf_op jit(solution)/shard_map/ppermute | solution.py:134
  96.9 2.1 %collective-permute-start.33 = (f32[32,128]{1,0:T(8,128)S(1)}, f32[32,128]{1,0:T(8,128)S(1)}, u32[]{:S(2)}, u32[]{:S(2)}) collective-permute-start(f32[32,128]{1,0:T(8,128)S(1)} %broadcast_select_fusion), channel_id=1, source_target_pairs={{4,228}} | collective-permute-start | bytes 49160 | tf_op jit(solution)/shard_map/ppermute | solution.py:134
  99.1 3.9 %collective-permute-start.34 = (f32[32,128]{1,0:T(8,128)S(1)}, f32[32,128]{1,0:T(8,128)S(1)}, u32[]{:S(2)}, u32[]{:S(2)}) collective-permute-start(f32[32,128]{1,0:T(8,128)S(1)} %add_add_fusion.2), channel_id=1, source_target_pairs={{4,12},{36,44},{68,76},{100,108},{132,140},{164,172},{196,204},{22... | collective-permute-start | bytes 49160 | tf_op jit(solution)/shard_map/ppermute | solution.py:134
  100.4 2.6 %collective-permute-start.35 = (f32[32,128]{1,0:T(8,128)S(1)}, f32[32,128]{1,0:T(8,128)S(1)}, u32[]{:S(2)}, u32[]{:S(2)}) collective-permute-start(f32[32,128]{1,0:T(8,128)S(1)} %add_add_fusion.2), channel_id=1, source_target_pairs={{4,20},{36,52},{68,84},{100,116},{132,148},{164,180},{196,212},{22... | collective-permute-start | bytes 49160 | tf_op jit(solution)/shard_map/ppermute | solution.py:134
  101.7 2.1 %collective-permute-start.36 = (f32[32,128]{1,0:T(8,128)S(1)}, f32[32,128]{1,0:T(8,128)S(1)}, u32[]{:S(2)}, u32[]{:S(2)}) collective-permute-start(f32[32,128]{1,0:T(8,128)S(1)} %add_add_fusion.2), channel_id=1, source_target_pairs={{4,28},{36,60},{68,92},{100,124},{132,156},{164,188},{196,220},{22... | collective-permute-start | bytes 49160 | tf_op jit(solution)/shard_map/ppermute | solution.py:134
  103.9 3.9 %collective-permute-start.37 = (f32[32,128]{1,0:T(8,128)S(1)}, f32[32,128]{1,0:T(8,128)S(1)}, u32[]{:S(2)}, u32[]{:S(2)}) collective-permute-start(f32[32,128]{1,0:T(8,128)S(1)} %add_add_fusion.1), channel_id=1, source_target_pairs={{4,5},{12,13},{20,21},{28,29},{36,37},{44,45},{52,53},{60,61},{68,... | collective-permute-start | bytes 49160 | tf_op jit(solution)/shard_map/ppermute | solution.py:134
  105.1 2.6 %collective-permute-start.38 = (f32[32,128]{1,0:T(8,128)S(1)}, f32[32,128]{1,0:T(8,128)S(1)}, u32[]{:S(2)}, u32[]{:S(2)}) collective-permute-start(f32[32,128]{1,0:T(8,128)S(1)} %add_add_fusion.1), channel_id=1, source_target_pairs={{4,6},{12,14},{20,22},{28,30},{36,38},{44,46},{52,54},{60,62},{68,... | collective-permute-start | bytes 49160 | tf_op jit(solution)/shard_map/ppermute | solution.py:134
  106.4 2.1 %collective-permute-start.39 = (f32[32,128]{1,0:T(8,128)S(1)}, f32[32,128]{1,0:T(8,128)S(1)}, u32[]{:S(2)}, u32[]{:S(2)}) collective-permute-start(f32[32,128]{1,0:T(8,128)S(1)} %add_add_fusion.1), channel_id=1, source_target_pairs={{4,7},{12,15},{20,23},{28,31},{36,39},{44,47},{52,55},{60,63},{68,... | collective-permute-start | bytes 49160 | tf_op jit(solution)/shard_map/ppermute | solution.py:134
  108.6 5.5 %collective-permute-start.40 = (f32[32,128]{1,0:T(8,128)S(1)}, f32[32,128]{1,0:T(8,128)S(1)}, u32[]{:S(2)}, u32[]{:S(2)}) collective-permute-start(f32[32,128]{1,0:T(8,128)S(1)} %add_add_fusion), channel_id=1, source_target_pairs={{4,0},{5,1},{6,2},{7,3},{12,8},{13,9},{14,10},{15,11},{20,16},{21,... | collective-permute-start | bytes 49160 | tf_op jit(solution)/shard_map/ppermute | solution.py:134
  109.9 5.0 %collective-permute-start.24 = (bf16[2,8,32,128]{3,2,1,0:T(8,128)(2,1)S(1)}, bf16[2,8,32,128]{3,2,1,0:T(8,128)(2,1)S(1)}, u32[]{:S(2)}, u32[]{:S(2)}) collective-permute-start(bf16[2,8,32,128]{3,2,1,0:T(8,128)(2,1)S(1)} %get-tuple-element.24.refs_0_), channel_id=1, source_target_pairs={{0,1},{1,0},{2,3},{3,2},{4,5},{5,4},{6,7},{7,6},{8,9},{9,8},{10,11... | collective-permute-start | bytes 393224 | tf_op jit(solution)/shard_map/ppermute | solution.py:155
  110.0 7.9 %collective-permute-start.25 = (bf16[2,8,32,128]{3,2,1,0:T(8,128)(2,1)S(1)}, bf16[2,8,32,128]{3,2,1,0:T(8,128)(2,1)S(1)}, u32[]{:S(2)}, u32[]{:S(2)}) collective-permute-start(bf16[2,8,32,128]{3,2,1,0:T(8,128)(2,1)S(1)} %get-tuple-element.24.refs_0_), channel_id=1, source_target_pairs={{0,2},{1,3},{2,0},{3,1},{4,6},{5,7},{6,4},{7,5},{8,10},{9,11},{10,... | collective-permute-start | bytes 393224 | tf_op jit(solution)/shard_map/ppermute | solution.py:155
  114.1 5.2 %collective-permute-start.26 = (bf16[2,8,32,128]{3,2,1,0:T(8,128)(2,1)S(1)}, bf16[2,8,32,128]{3,2,1,0:T(8,128)(2,1)S(1)}, u32[]{:S(2)}, u32[]{:S(2)}) collective-permute-start(bf16[2,8,32,128]{3,2,1,0:T(8,128)(2,1)S(1)} %get-tuple-element.24.refs_0_), channel_id=1, source_target_pairs={{0,3},{1,2},{2,1},{3,0},{4,7},{5,6},{6,5},{7,4},{8,11},{9,10},{10,... | collective-permute-start | bytes 393224 | tf_op jit(solution)/shard_map/ppermute | solution.py:155

commit v2 on v1

v2 whole, which is shorter than its diff:
```python
import functools

import jax
import jax.numpy as jnp
from jax import lax
from jax.experimental import pallas as pl
from jax.experimental.pallas import tpu as pltpu
from jax.sharding import PartitionSpec as P

CORES = 2
LANES = 128
SIDE_CHIPS = 4
NT = (((1,), (1,)), ((), ()))
VMEM = pl.BlockSpec(memory_space=pltpu.VMEM)
SMEM = pl.BlockSpec(memory_space=pltpu.SMEM)


def own_blocks(panel, tiles, blocks):
    side = blocks.shape[2]
    for j in range(blocks.shape[0]):
        blocks[j] = panel[:, j * side:(j + 1) * side]


def spread_panel(helpers, ints, *refs):
    shards, (slab, to_pair, to_cross) = refs[:helpers], refs[helpers:]
    me = lax.axis_index("help")
    odd = lax.rem(lax.axis_index("rows"), 2)
    side = slab.shape[2]
    row_tiles = slab.shape[0] // helpers
    for d in range(helpers):
        base = (me ^ d) * row_tiles
        for j in range(row_tiles):
            slab[base + j] = shards[d][:, j * side:(j + 1) * side] if d else shards[0][j]
    for g in range(to_pair.shape[0]):
        to_pair[g] = slab[ints[row_tiles + 3 - odd, g]]
        to_cross[g] = slab[ints[row_tiles + 2 + odd, g]]


def spread_field(helpers, ints, *refs):
    shards, (slab, to_pair, to_cross) = refs[:helpers], refs[helpers:]
    me = lax.axis_index("help")
    odd = lax.rem(lax.axis_index("rows"), 2)
    row_tiles = slab.shape[1] // helpers
    for d in range(helpers):
        base = (me ^ d) * row_tiles
        for j in range(row_tiles):
            slab[:, ints[row_tiles + 1, base + j]] = shards[d][:, j]
    for g in range(to_pair.shape[1]):
        to_pair[:, g] = slab[:, ints[row_tiles + 3 - odd, g]]
        to_cross[:, g] = slab[:, ints[row_tiles + 2 + odd, g]]


def finish(scale, ints, parts, near, far, out, gram, inverse):
    me = lax.axis_index("help")
    volumes, steps, vectors, _ = gram.shape
    row_tiles, side = near.shape[2], near.shape[4]
    for q in range(inverse.shape[0]):
        inverse[ints[row_tiles + 1, q]] = q
    for j in range(row_tiles):
        slot = inverse[me * row_tiles + j]
        held = lax.rem(slot, row_tiles)
        step = lax.div(slot, row_tiles) ^ me
        pairs = [(near, 0), (near, 1), (far, 1), (far, 0)]
        block = near[0, :, held]
        for d, (ref, half) in enumerate(pairs):
            block = jnp.where(step == d, ref[half, :, held], block)
        out[:, :, j * side:(j + 1) * side] = block
    total = jnp.sum(parts[...].astype(jnp.float32), axis=0) * scale
    for step in range(steps):
        for v in range(volumes):
            at = (step * volumes + v) * vectors
            gram[v, step] = total[:, at:at + vectors]


def tile_pair(tiles, j, k):
    return jnp.concatenate(
        [jnp.concatenate([tiles[v, j, k], tiles[v, j, k + 1]], axis=1) for v in range(tiles.shape[0])],
        axis=0,
    )


def apply_first(ints, coefs, slab, pair, cross, tiles, first, gram, ext):
    volumes, row_tiles, slots, side, _ = tiles.shape
    slab_size = slab.shape[0]
    ghosts = pair.shape[0]
    vectors = slab.shape[1]
    me = lax.axis_index("help")
    odd = lax.rem(lax.axis_index("rows"), 2)
    ext[pl.ds(0, slab_size)] = slab[...]
    ext[pl.ds(slab_size + (1 - odd) * ghosts, ghosts)] = pair[...]
    ext[pl.ds(slab_size + odd * ghosts, ghosts)] = cross[...]
    for j in range(row_tiles):
        total = jnp.zeros((vectors, volumes * side), jnp.float32)
        for k in range(0, slots, 2):
            left = jnp.concatenate(
                [jnp.where(q < ints[row_tiles, j], ext[ints[j, q]], 0).astype(ext.dtype) for q in (k, k + 1)], axis=1
            )
            total += lax.dot_general(left, tile_pair(tiles, j, k), NT, preferred_element_type=jnp.float32)
        stored = slab[ints[row_tiles + 1, me * row_tiles + j]].astype(jnp.float32)
        for v in range(volumes):
            h = total[:, v * side:(v + 1) * side]
            first[v, j] = ((h - coefs[v] * stored) / coefs[volumes + v]).astype(first.dtype)
    for v in range(volumes):
        field = jnp.concatenate([first[v, j] for j in range(row_tiles)], axis=1)
        gram[v] = lax.dot_general(field, field, NT, preferred_element_type=jnp.float32)


def apply_second(
    ints, coefs, base, slab, pair, cross, tiles, first, gram_one, second, gram, ext
):
    volumes, row_tiles, slots, side, _ = tiles.shape
    slab_size = slab.shape[1]
    ghosts = pair.shape[1]
    vectors = slab.shape[2]
    me = lax.axis_index("help")
    odd = lax.rem(lax.axis_index("rows"), 2)
    ext[:, pl.ds(0, slab_size)] = slab[...]
    ext[:, pl.ds(slab_size + (1 - odd) * ghosts, ghosts)] = pair[...]
    ext[:, pl.ds(slab_size + odd * ghosts, ghosts)] = cross[...]
    for j in range(row_tiles):
        total = jnp.zeros((volumes * vectors, volumes * side), jnp.float32)
        for k in range(0, slots, 2):
            left = jnp.concatenate(
                [
                    jnp.concatenate(
                        [
                            jnp.where(q < ints[row_tiles, j], ext[v, ints[j, q]], 0).astype(ext.dtype)
                            for q in (k, k + 1)
                        ],
                        axis=1,
                    )
                    for v in range(volumes)
                ],
                axis=0,
            )
            total += lax.dot_general(left, tile_pair(tiles, j, k), NT, preferred_element_type=jnp.float32)
        stored = base[ints[row_tiles + 1, me * row_tiles + j]].astype(jnp.float32)
        for v in range(volumes):
            h = total[v * vectors:(v + 1) * vectors, v * side:(v + 1) * side]
            inner = h - coefs[v] * first[v, j].astype(jnp.float32)
            second[v, j] = (2.0 * inner / coefs[volumes + v] - stored).astype(second.dtype)
    parts = [gram_one[v] for v in range(volumes)]
    for v in range(volumes):
        field = jnp.concatenate([second[v, j] for j in range(row_tiles)], axis=1)
        parts.append(lax.dot_general(field, field, NT, preferred_element_type=jnp.float32))
    gram[...] = jnp.concatenate(parts, axis=1)


def summed_parts(value, groups):
    parts = jnp.broadcast_to(value.astype(jnp.bfloat16)[None], (len(groups[0]),) + value.shape)
    return lax.all_to_all(parts, ("rows", "help"), 0, 0, axis_index_groups=groups)


def per_device(panel, tiles, tile_cols, tile_count, row_assign, send_lists, centers, half_widths):
    helpers = lax.axis_size("help")
    rows = lax.axis_size("rows")
    volumes, row_tiles, slots, side, _ = tiles.shape
    vectors = panel.shape[0]
    ghosts = send_lists.shape[2]
    slab_size = row_tiles * helpers
    bf16 = panel.dtype
    depth = rows // (SIDE_CHIPS * CORES)

    def at(z, y, core, x):
        return ((z * SIDE_CHIPS + y) * CORES + core) * helpers + x

    def shape(*dims):
        return jax.ShapeDtypeStruct(dims, bf16)

    def gathered(shard):
        others = [
            lax.ppermute(shard, "help", [(i, i ^ d) for i in range(helpers)]) for d in range(1, helpers)
        ]
        return [shard] + others

    def exchanged(to_pair, to_cross):
        cross_pairs = [(s, (s + 1) % rows if s % 2 else (s - 1) % rows) for s in range(rows)]
        cross = lax.ppermute(to_cross, "rows", cross_pairs)
        pair = lax.ppermute(to_pair, "rows", [(s, s ^ 1) for s in range(rows)])
        return pair, cross

    params = pltpu.CompilerParams(vmem_limit_bytes=24 * 1024 * 1024)

    ints = jnp.concatenate(
        [
            jnp.pad(tile_cols, ((0, 0), (0, LANES - slots))),
            jnp.pad(tile_count[None], ((0, 0), (0, LANES - row_tiles))),
            jnp.pad(row_assign[None], ((0, 0), (0, LANES - slab_size))),
            jnp.pad(send_lists[0], ((0, 0), (0, LANES - ghosts))),
        ],
        axis=0,
    )
    coefs = jnp.concatenate([centers, half_widths])
    own_panel = pl.pallas_call(
        own_blocks,
        out_shape=shape(row_tiles, vectors, side),
        in_specs=[VMEM] * 2,
        out_specs=VMEM,
        compiler_params=params,
        name="own_blocks",
    )(panel, tiles)
    base, to_pair, to_cross = pl.pallas_call(
        functools.partial(spread_panel, helpers),
        out_shape=[shape(slab_size, vectors, side)] + [shape(ghosts, vectors, side)] * 2,
        in_specs=[SMEM] + [VMEM] * helpers,
        out_specs=[VMEM] * 3,
        compiler_params=params,
        name="spread_panel",
    )(ints, own_panel, *gathered(panel)[1:])
    pair, cross = exchanged(to_pair, to_cross)
    first, gram_one = pl.pallas_call(
        apply_first,
        out_shape=[
            shape(volumes, row_tiles, vectors, side),
            jax.ShapeDtypeStruct((volumes, vectors, vectors), jnp.float32),
        ],
        in_specs=[SMEM] * 2 + [VMEM] * 4,
        out_specs=[VMEM] * 2,
        scratch_shapes=[pltpu.VMEM((slab_size + 2 * ghosts, vectors, side), bf16)],
        compiler_params=params,
        name="apply_first",
    )(ints, coefs, base, pair, cross, tiles)
    slab, to_pair, to_cross = pl.pallas_call(
        functools.partial(spread_field, helpers),
        out_shape=[shape(volumes, slab_size, vectors, side)] + [shape(volumes, ghosts, vectors, side)] * 2,
        in_specs=[SMEM] + [VMEM] * helpers,
        out_specs=[VMEM] * 3,
        compiler_params=params,
        name="spread_field",
    )(ints, *gathered(first))
    pair, cross = exchanged(to_pair, to_cross)
    second, gram = pl.pallas_call(
        apply_second,
        out_shape=[
            shape(volumes, row_tiles, vectors, side),
            jax.ShapeDtypeStruct((vectors, 2 * volumes * vectors), jnp.float32),
        ],
        in_specs=[SMEM] * 2 + [VMEM] * 7,
        out_specs=[VMEM] * 2,
        scratch_shapes=[pltpu.VMEM((volumes, slab_size + 2 * ghosts, vectors, side), bf16)],
        compiler_params=params,
        name="apply_second",
    )(ints, coefs, base, slab, pair, cross, tiles, first, gram_one)

    near_pair = jnp.stack([second, lax.ppermute(second, "help", [(i, i ^ 1) for i in range(helpers)])])
    near = [
        [at(z, y, c, x) for y in range(SIDE_CHIPS) for x in range(helpers)]
        for z in range(depth)
        for c in range(CORES)
    ]
    far = [
        [at(z, y, c, x) for z in range(depth) for c in range(CORES)]
        for y in range(SIDE_CHIPS)
        for x in range(helpers)
    ]
    gram = jnp.sum(summed_parts(gram, near).astype(jnp.float32), axis=0)
    gram, near_pair = lax.optimization_barrier((gram, near_pair))
    far_pair = lax.ppermute(near_pair, "help", [(i, i ^ 3) for i in range(helpers)])
    parts = summed_parts(gram, far)
    filtered, gram = pl.pallas_call(
        functools.partial(finish, 1.0 / (row_tiles * side * helpers * rows)),
        out_shape=[
            shape(volumes, vectors, row_tiles * side),
            jax.ShapeDtypeStruct((volumes, 2, vectors, vectors), jnp.float32),
        ],
        in_specs=[SMEM] + [VMEM] * 3,
        out_specs=[VMEM] * 2,
        scratch_shapes=[pltpu.SMEM((slab_size,), jnp.int32)],
        compiler_params=params,
        name="finish",
    )(ints, parts, near_pair, far_pair)
    return filtered, gram


def solution(mesh):
    placed = (
        P(None, ("rows", "help")),
        P(None, ("rows", "help"), None, None, None),
        P(("rows", "help"), None),
        P(("rows", "help")),
        P("rows"),
        P("rows", None, None),
        P(),
        P(),
    )
    return jax.shard_map(
        per_device,
        mesh=mesh,
        in_specs=placed,
        out_specs=(P(None, None, ("rows", "help")), P()),
        check_vma=False,
    )
```

time: 121 us -> 79.1 us (0.65)
  starting transfers between devices: 58.8 us -> 23.5 us
  waiting for transfers between devices: 42.2 us -> 19.7 us
  blocking collectives: 0 us -> 19.2 us
  local copies, waits for them, and re-layouts: 8.97 us -> 5.57 us
    ppermute x28 -> x2, starting transfers between devices: 36.1 us -> 1.95 us  [the longest x1 1.25 us: per_device(): lax.ppermute(second, 'help', [(i, i ^ 1) for i in range(helpers)])]
    ppermute x28 -> x2, waiting for transfers between devices: 19.4 us -> 0.01 us  [the longest x1 0.01 us: per_device(): lax.ppermute(second, 'help', [(i, i ^ 1) for i in range(helpers)])]
    all_to_all x0 -> x1, blocking collectives: none -> 19.2 us  [summed_parts(): lax.all_to_all(parts, ('rows', 'help'), 0, 0, axis_index_groups=groups)]
    ppermute x9 -> x6, waiting for transfers between devices: 13.6 us -> 3.76 us  [gathered(): lax.ppermute(shard, 'help', [(i, i ^ d) for i in range(helpers)])]
    all_to_all x0 -> x1, waiting for transfers between devices: none -> 5.56 us  [summed_parts(): lax.all_to_all(parts, ('rows', 'help'), 0, 0, axis_index_groups=groups)]
    ppermute x9 -> x6, starting transfers between devices: 12.7 us -> 7.85 us  [gathered(): lax.ppermute(shard, 'help', [(i, i ^ d) for i in range(helpers)])]
    all_to_all x0 -> x1, starting transfers between devices: none -> 3.51 us  [summed_parts(): lax.all_to_all(parts, ('rows', 'help'), 0, 0, axis_index_groups=groups)]
    unnamed x26 -> x18, local copies, waits for them, and re-layouts: 8.22 us -> 4.88 us
  transfers between devices with their start and end apart: 41 -> 13, of which waited for: 23 -> 7; matrix products, arithmetic and copies ran while one was open for 1% -> 0% of each run, Pallas kernels for 0% -> 0%
where the time goes in v2:
time: 79.1 us; the launch traced here: 78.8 us
  starting transfers between devices  23.5 us (30%)
  waiting for transfers between devices  19.7 us (25%)
  blocking collectives  19.2 us (24%)
  Pallas kernels  9.9 us (13%)
  local copies, waits for them, and re-layouts  5.57 us (7%)
    all_to_all x1, blocking collectives, summed_parts(): lax.all_to_all(parts, ('rows', 'help'), 0, 0, axis_index_groups=groups)  19.2 us
    ppermute x2, starting transfers between devices, exchanged(): pair = lax.ppermute(to_pair, 'rows', [(s, s ^ 1) for s in range(rows)])  10.2 us
    ppermute x2, waiting for transfers between devices, exchanged(): cross = lax.ppermute(to_cross, 'rows', cross_pairs)  8.34 us
    ppermute x6, starting transfers between devices, gathered(): lax.ppermute(shard, 'help', [(i, i ^ d) for i in range(helpers)])  7.85 us
    all_to_all x1, waiting for transfers between devices, summed_parts(): lax.all_to_all(parts, ('rows', 'help'), 0, 0, axis_index_groups=groups)  5.56 us
    unnamed x18, local copies, waits for them, and re-layouts  4.88 us
    ppermute x6, waiting for transfers between devices, gathered(): lax.ppermute(shard, 'help', [(i, i ^ d) for i in range(helpers)])  3.76 us
    pallas_call x1, Pallas kernels, per_device(): pl.pallas_call(apply_second, out_shape=[shape(volumes, row_tiles, vectors...  3.53 us
  transfers between devices with their start and end apart: 13, of which 7 were waited for; matrix products, arithmetic and copies ran while one was open for 0% of the time, Pallas kernels for 0%

profile of v2, /device:TPU:1, one launch (start us, length us, event | category | flops | bytes accessed | tf_op | source)
XLA Modules:
  0.0 78.8 jit_solution(18280005770913710901)
XLA Ops:
  0.6 2.1 %collective-permute-start = (bf16[32,1024]{1,0:T(8,128)(2,1)}, bf16[32,1024]{1,0:T(8,128)(2,1)S(1)}, u32[]{:S(2)}, u32[]{:S(2)}) collective-permute-start(bf16[32,1024]{1,0:T(8,128)(2,1)} %panel.1), channel_id=1, source_target_pairs={{0,1},{1,0},{2,3},{3,2},{4,5},{5,4},{6,7},{7,6},{8,9},{9,8},{10,11... | collective-permute-start | bytes 196616 | tf_op jit(solution)/shard_map/ppermute | solution.py:172
  2.8 1.8 %collective-permute-start.2 = (bf16[32,1024]{1,0:T(8,128)(2,1)}, bf16[32,1024]{1,0:T(8,128)(2,1)S(1)}, u32[]{:S(2)}, u32[]{:S(2)}) collective-permute-start(bf16[32,1024]{1,0:T(8,128)(2,1)} %panel.1), channel_id=1, source_target_pairs={{0,3},{1,2},{2,1},{3,0},{4,7},{5,6},{6,5},{7,4},{8,11},{9,10},{10,... | collective-permute-start | bytes 196616 | tf_op jit(solution)/shard_map/ppermute | solution.py:172
  4.6 0.6 collective-permute-start.1
  5.2 0.0 copy-start
  5.2 3.4 %copy-done = bf16[2,8,16,128,128]{4,3,2,1,0:T(8,128)(2,1)S(1)} copy-done((bf16[2,8,16,128,128]{4,3,2,1,0:T(8,128)(2,1)S(1)}, bf16[2,8,16,128,128]{4,3,2,1,0:T(8,128)(2,1)}, u32[]{:S(2)}) %copy-start) | copy-done | bytes 8388632
  8.6 0.0 copy-start.2
  8.6 0.8 %copy-done.2 = bf16[32,1024]{1,0:T(8,128)(2,1)S(1)} copy-done((bf16[32,1024]{1,0:T(8,128)(2,1)S(1)}, bf16[32,1024]{1,0:T(8,128)(2,1)}, u32[]{:S(2)}) %copy-start.2) | copy-done | bytes 65560
  9.4 0.0 copy-start.3
  9.4 0.0 copy-start.4
  9.4 0.0 copy-start.5
  9.4 0.0 copy-start.6
  9.4 0.0 copy-start.7
  9.5 0.0 copy-start.8
  9.5 0.0 copy-start.1
  9.5 0.6 copy-done.3
  10.1 0.0 copy-done.4
  10.1 0.0 copy-done.5
  10.1 0.0 copy-done.6
  10.2 0.0 collective-permute-done.refs_1_
  10.2 0.0 collective-permute-done.2.refs_3_
  10.2 0.0 collective-permute-done.1.refs_2_
  10.2 0.7 spread_panel.1
  10.9 2.9 %collective-permute-start.3 = (bf16[16,32,128]{2,1,0:T(8,128)(2,1)S(1)}, bf16[16,32,128]{2,1,0:T(8,128)(2,1)S(1)}, u32[]{:S(2)}, u32[]{:S(2)}) collective-permute-start(bf16[16,32,128]{2,1,0:T(8,128)(2,1)S(1)} %get-tuple-element.15), channel_id=1, source_target_pairs={{0,4},{4,0},{8,12},{12,8},{16,20},{20,16},{24,28},{28,24},{32,36},... | collective-permute-start | bytes 393224 | tf_op jit(solution)/shard_map/ppermute | solution.py:179
  13.9 0.0 collective-permute-start.4
  13.9 0.0 copy-done.7
  13.9 0.0 copy-done.8
  13.9 0.1 pad_maximum_fusion.1.coefs
  14.0 0.9 %collective-permute-done.3.pair = bf16[16,32,128]{2,1,0:T(8,128)(2,1)S(1)} collective-permute-done((bf16[16,32,128]{2,1,0:T(8,128)(2,1)S(1)}, bf16[16,32,128]{2,1,0:T(8,128)(2,1)S(1)}, u32[]{:S(2)}, u32[]{:S(2)}) %collective-permute-start.3) | collective-permute-done | bytes 131104 | tf_op jit(solution)/shard_map/ppermute | solution.py:179
  14.8 3.4 %collective-permute-done.4.cross = bf16[16,32,128]{2,1,0:T(8,128)(2,1)S(1)} collective-permute-done((bf16[16,32,128]{2,1,0:T(8,128)(2,1)S(1)}, bf16[16,32,128]{2,1,0:T(8,128)(2,1)S(1)}, u32[]{:S(2)}, u32[]{:S(2)}) %collective-permute-start.4) | collective-permute-done | bytes 131104 | tf_op jit(solution)/shard_map/ppermute | solution.py:178
  18.3 0.0 copy-done.1
  18.3 3.3 %apply_first.1 = (bf16[2,8,32,128]{3,2,1,0:T(8,128)(2,1)S(1)}, f32[2,32,32]{2,1,0:T(8,128)S(1)}) custom-call(s32[12,128]{1,0:T(8,128)S(1)} %pad_add_fusion.ints, f32[4]{0:T(128)S(1)} %pad_maximum_fusion.1.coefs, bf16[32,32,128]{2,1,0:T(8,128)(2,1)S(1)} %get-tuple-element.14.slab.base, bf16[16,32,128]{2,1,0:T(8,128)(2,1)S(1)} %collective-permute-done.3.pair, ...), custom_call_target="tpu_custom_call" | custom-call | tf_op jit(solution)/shard_map/apply_first/pallas_call | solution.py:211
  21.6 0.8 collective-permute-start.7
  22.4 0.9 %collective-permute-start.6 = (bf16[2,8,32,128]{3,2,1,0:T(8,128)(2,1)S(1)}, bf16[2,8,32,128]{3,2,1,0:T(8,128)(2,1)S(1)}, u32[]{:S(2)}, u32[]{:S(2)}) collective-permute-start(bf16[2,8,32,128]{3,2,1,0:T(8,128)(2,1)S(1)} %get-tuple-element.17.refs_0_.first), channel_id=1, source_target_pairs={{0,2},{1,3},{2,0},{3,1},{4,6},{5,7},{6,4},{7,5},{8,10},{9,11},{10,... | collective-permute-start | bytes 393224 | tf_op jit(solution)/shard_map/ppermute | solution.py:172
  23.2 1.6 %collective-permute-start.5 = (bf16[2,8,32,128]{3,2,1,0:T(8,128)(2,1)S(1)}, bf16[2,8,32,128]{3,2,1,0:T(8,128)(2,1)S(1)}, u32[]{:S(2)}, u32[]{:S(2)}) collective-permute-start(bf16[2,8,32,128]{3,2,1,0:T(8,128)(2,1)S(1)} %get-tuple-element.17.refs_0_.first), channel_id=1, source_target_pairs={{0,1},{1,0},{2,3},{3,2},{4,5},{5,4},{6,7},{7,6},{8,9},{9,8},{10,11... | collective-permute-start | bytes 393224 | tf_op jit(solution)/shard_map/ppermute | solution.py:172
  24.9 3.2 %collective-permute-done.7.refs_3_ = bf16[2,8,32,128]{3,2,1,0:T(8,128)(2,1)S(1)} collective-permute-done((bf16[2,8,32,128]{3,2,1,0:T(8,128)(2,1)S(1)}, bf16[2,8,32,128]{3,2,1,0:T(8,128)(2,1)S(1)}, u32[]{:S(2)}, u32[]{:S(2)}) %collective-permute-start.7) | collective-permute-done | bytes 131104 | tf_op jit(solution)/shard_map/ppermute | solution.py:172
  28.1 0.0 collective-permute-done.6.refs_2_
  28.1 0.6 collective-permute-done.5.refs_1_
  28.6 0.8 %spread_field.1 = (bf16[2,32,32,128]{3,2,1,0:T(8,128)(2,1)S(1)}, bf16[2,16,32,128]{3,2,1,0:T(8,128)(2,1)S(1)}, bf16[2,16,32,128]{3,2,1,0:T(8,128)(2,1)S(1)}) custom-call(s32[12,128]{1,0:T(8,128)S(1)} %pad_add_fusion.ints, bf16[2,8,32,128]{3,2,1,0:T(8,128)(2,1)S(1)} %get-tuple-element.17.refs_0_.first, ...), custom_call_target="tpu_custom_call" | custom-call | tf_op jit(solution)/shard_map/spread_field/pallas_call | solution.py:223
  29.4 7.2 %collective-permute-start.8 = (bf16[2,16,32,128]{3,2,1,0:T(8,128)(2,1)S(1)}, bf16[2,16,32,128]{3,2,1,0:T(8,128)(2,1)S(1)}, u32[]{:S(2)}, u32[]{:S(2)}) collective-permute-start(bf16[2,16,32,128]{3,2,1,0:T(8,128)(2,1)S(1)} %get-tuple-element.19), channel_id=1, source_target_pairs={{0,4},{4,0},{8,12},{12,8},{16,20},{20,16},{24,28},{28,24},{32,36},... | collective-permute-start | bytes 786440 | tf_op jit(solution)/shard_map/ppermute | solution.py:179
  36.7 0.0 collective-permute-start.9
  36.7 1.2 %collective-permute-done.8.pair = bf16[2,16,32,128]{3,2,1,0:T(8,128)(2,1)S(1)} collective-permute-done((bf16[2,16,32,128]{3,2,1,0:T(8,128)(2,1)S(1)}, bf16[2,16,32,128]{3,2,1,0:T(8,128)(2,1)S(1)}, u32[]{:S(2)}, u32[]{:S(2)}) %collective-permute-start.8) | collective-permute-done | bytes 262176 | tf_op jit(solution)/shard_map/ppermute | solution.py:179
  37.8 4.9 %collective-permute-done.9.cross = bf16[2,16,32,128]{3,2,1,0:T(8,128)(2,1)S(1)} collective-permute-done((bf16[2,16,32,128]{3,2,1,0:T(8,128)(2,1)S(1)}, bf16[2,16,32,128]{3,2,1,0:T(8,128)(2,1)S(1)}, u32[]{:S(2)}, u32[]{:S(2)}) %collective-permute-start.9) | collective-permute-done | bytes 262176 | tf_op jit(solution)/shard_map/ppermute | solution.py:178
  42.8 3.5 %apply_second.1 = (bf16[2,8,32,128]{3,2,1,0:T(8,128)(2,1)S(1)}, f32[32,128]{1,0:T(8,128)S(1)}) custom-call(s32[12,128]{1,0:T(8,128)S(1)} %pad_add_fusion.ints, f32[4]{0:T(128)S(1)} %pad_maximum_fusion.1.coefs, bf16[32,32,128]{2,1,0:T(8,128)(2,1)S(1)} %get-tuple-element.14.slab.base, bf16[2,32,32,128]{3,2,1,0:T(8,128)(2,1)S(1)} %get-tuple-element.18.slab, ...), custom_call_target="tpu_custom_call" | custom-call | tf_op jit(solution)/shard_map/apply_second/pallas_call | solution.py:232
  46.3 0.7 broadcast_in_dim.20
  47.0 3.5 %all-to-all-start = ((bf16[16,32,128]{2,1,0:T(8,128)(2,1)}), bf16[16,32,128]{2,1,0:T(8,128)(2,1)S(1)}, u32[]{:S(2)}, u32[]{:S(2)}) async-start(bf16[16,32,128]{2,1,0:T(8,128)(2,1)} %broadcast_in_dim.20), calls=%async_computation | async-start | bytes 262144 | tf_op jit(solution)/shard_map/all_to_all | solution.py:151
  50.5 1.2 %collective-permute-start.10 = (bf16[2,8,32,128]{3,2,1,0:T(8,128)(2,1)S(1)}, bf16[2,8,32,128]{3,2,1,0:T(8,128)(2,1)S(1)}, u32[]{:S(2)}, u32[]{:S(2)}) collective-permute-start(bf16[2,8,32,128]{3,2,1,0:T(8,128)(2,1)S(1)} %get-tuple-element.23), channel_id=1, source_target_pairs={{0,1},{1,0},{2,3},{3,2},{4,5},{5,4},{6,7},{7,6},{8,9},{9,8},{10,11... | collective-permute-start | bytes 393224 | tf_op jit(solution)/shard_map/ppermute | solution.py:245
  51.8 5.6 %all-to-all-done = bf16[16,32,128]{2,1,0:T(8,128)(2,1)S(1)} async-done(((bf16[16,32,128]{2,1,0:T(8,128)(2,1)}), bf16[16,32,128]{2,1,0:T(8,128)(2,1)S(1)}, u32[]{:S(2)}, u32[]{:S(2)}) %all-to-all-start) | async-done | bytes 131104 | tf_op jit(solution)/shard_map/all_to_all | solution.py:151
  57.3 0.0 collective-permute-done.10
  57.4 0.7 collective-permute-start.11
  58.1 19.2 %all_to_all.10.parts = bf16[16,32,128]{2,1,0:T(8,128)(2,1)S(1)} all-to-all(bf16[16,32,128]{2,1,0:T(8,128)(2,1)S(1)} %broadcast_in_dim.21), channel_id=1, replica_groups={{0,4,32,36,64,68,96,100,128,132,160,164,192,196,224,228},{1,5,33,37,65,..., dimensions={0} | all-to-all | bytes 262144 | tf_op jit(solution)/shard_map/all_to_all | solution.py:151
  77.3 0.0 collective-permute-done.11.far
  77.3 1.5 %finish.1 = (bf16[2,32,1024]{2,1,0:T(8,128)(2,1)}, f32[2,2,32,32]{3,2,1,0:T(8,128)}) custom-call(s32[12,128]{1,0:T(8,128)S(1)} %pad_add_fusion.ints, bf16[16,32,128]{2,1,0:T(8,128)(2,1)S(1)} %all_to_all.10.parts, bf16[2,2,8,32,128]{4,3,2,1,0:T(8,128)(2,1)S(1)} %pad_maximum_fusion.near, bf16[2,2,8,32,128]{4,3,2,1,0:T(8,128)(2,1)S(1)} %collective-permute-done.11.far), custom_call_target="tpu_custom_call" | custom-call | tf_op jit(solution)/shard_map/finish/pallas_call | solution.py:260
  (6 shorter events, 0.1 us)
Async XLA Ops:
  0.6 9.5 %collective-permute-start = (bf16[32,1024]{1,0:T(8,128)(2,1)}, bf16[32,1024]{1,0:T(8,128)(2,1)S(1)}, u32[]{:S(2)}, u32[]{:S(2)}) collective-permute-start(bf16[32,1024]{1,0:T(8,128)(2,1)} %panel.1), channel_id=1, source_target_pairs={{0,1},{1,0},{2,3},{3,2},{4,5},{5,4},{6,7},{7,6},{8,9},{9,8},{10,11... | collective-permute-start | bytes 196616 | tf_op jit(solution)/shard_map/ppermute | solution.py:172
  2.8 7.4 %collective-permute-start.2 = (bf16[32,1024]{1,0:T(8,128)(2,1)}, bf16[32,1024]{1,0:T(8,128)(2,1)S(1)}, u32[]{:S(2)}, u32[]{:S(2)}) collective-permute-start(bf16[32,1024]{1,0:T(8,128)(2,1)} %panel.1), channel_id=1, source_target_pairs={{0,3},{1,2},{2,1},{3,0},{4,7},{5,6},{6,5},{7,4},{8,11},{9,10},{10,... | collective-permute-start | bytes 196616 | tf_op jit(solution)/shard_map/ppermute | solution.py:172
  4.6 5.6 %collective-permute-start.1 = (bf16[32,1024]{1,0:T(8,128)(2,1)}, bf16[32,1024]{1,0:T(8,128)(2,1)S(1)}, u32[]{:S(2)}, u32[]{:S(2)}) collective-permute-start(bf16[32,1024]{1,0:T(8,128)(2,1)} %panel.1), channel_id=1, source_target_pairs={{0,2},{1,3},{2,0},{3,1},{4,6},{5,7},{6,4},{7,5},{8,10},{9,11},{10,... | collective-permute-start | bytes 196616 | tf_op jit(solution)/shard_map/ppermute | solution.py:172
  5.2 3.4 %copy-start = (bf16[2,8,16,128,128]{4,3,2,1,0:T(8,128)(2,1)S(1)}, bf16[2,8,16,128,128]{4,3,2,1,0:T(8,128)(2,1)}, u32[]{:S(2)}) copy-start(bf16[2,8,16,128,128]{4,3,2,1,0:T(8,128)(2,1)} %tiles.5) | copy-start | bytes 25165828
  8.6 0.8 %copy-start.2 = (bf16[32,1024]{1,0:T(8,128)(2,1)S(1)}, bf16[32,1024]{1,0:T(8,128)(2,1)}, u32[]{:S(2)}) copy-start(bf16[32,1024]{1,0:T(8,128)(2,1)} %panel.1) | copy-start | bytes 196612
  9.4 0.7 copy-start.3
  9.4 0.7 copy-start.4
  9.4 0.7 copy-start.5
  9.4 0.7 copy-start.6
  9.4 4.5 %copy-start.7 = (f32[2]{0:T(128)S(1)}, f32[2]{0:T(128)}, u32[]{:S(2)}) copy-start(f32[2]{0:T(128)} %param.15) | copy-start | bytes 28
  9.5 4.5 %copy-start.8 = (f32[2]{0:T(128)S(1)}, f32[2]{0:T(128)}, u32[]{:S(2)}) copy-start(f32[2]{0:T(128)} %param.14) | copy-start | bytes 28
  9.5 8.8 %copy-start.1 = (bf16[2,8,16,128,128]{4,3,2,1,0:T(8,128)(2,1)S(1)}, bf16[2,8,16,128,128]{4,3,2,1,0:T(8,128)(2,1)}, u32[]{:S(2)}) copy-start(bf16[2,8,16,128,128]{4,3,2,1,0:T(8,128)(2,1)} %tiles.5) | copy-start | bytes 25165828
  10.9 3.9 %collective-permute-start.3 = (bf16[16,32,128]{2,1,0:T(8,128)(2,1)S(1)}, bf16[16,32,128]{2,1,0:T(8,128)(2,1)S(1)}, u32[]{:S(2)}, u32[]{:S(2)}) collective-permute-start(bf16[16,32,128]{2,1,0:T(8,128)(2,1)S(1)} %get-tuple-element.15), channel_id=1, source_target_pairs={{0,4},{4,0},{8,12},{12,8},{16,20},{20,16},{24,28},{28,24},{32,36},... | collective-permute-start | bytes 393224 | tf_op jit(solution)/shard_map/ppermute | solution.py:179
  13.9 4.4 %collective-permute-start.4 = (bf16[16,32,128]{2,1,0:T(8,128)(2,1)S(1)}, bf16[16,32,128]{2,1,0:T(8,128)(2,1)S(1)}, u32[]{:S(2)}, u32[]{:S(2)}) collective-permute-start(bf16[16,32,128]{2,1,0:T(8,128)(2,1)S(1)} %get-tuple-element.16), channel_id=1, source_target_pairs={{0,252},{4,8},{8,4},{12,16},{16,12},{20,24},{24,20},{28,32},{32,28... | collective-permute-start | bytes 393224 | tf_op jit(solution)/shard_map/ppermute | solution.py:178
  21.6 6.4 %collective-permute-start.7 = (bf16[2,8,32,128]{3,2,1,0:T(8,128)(2,1)S(1)}, bf16[2,8,32,128]{3,2,1,0:T(8,128)(2,1)S(1)}, u32[]{:S(2)}, u32[]{:S(2)}) collective-permute-start(bf16[2,8,32,128]{3,2,1,0:T(8,128)(2,1)S(1)} %get-tuple-element.17.refs_0_.first), channel_id=1, source_target_pairs={{0,3},{1,2},{2,1},{3,0},{4,7},{5,6},{6,5},{7,4},{8,11},{9,10},{10,... | collective-permute-start | bytes 393224 | tf_op jit(solution)/shard_map/ppermute | solution.py:172
  22.4 5.7 %collective-permute-start.6 = (bf16[2,8,32,128]{3,2,1,0:T(8,128)(2,1)S(1)}, bf16[2,8,32,128]{3,2,1,0:T(8,128)(2,1)S(1)}, u32[]{:S(2)}, u32[]{:S(2)}) collective-permute-start(bf16[2,8,32,128]{3,2,1,0:T(8,128)(2,1)S(1)} %get-tuple-element.17.refs_0_.first), channel_id=1, source_target_pairs={{0,2},{1,3},{2,0},{3,1},{4,6},{5,7},{6,4},{7,5},{8,10},{9,11},{10,... | collective-permute-start | bytes 393224 | tf_op jit(solution)/shard_map/ppermute | solution.py:172
  23.2 5.4 %collective-permute-start.5 = (bf16[2,8,32,128]{3,2,1,0:T(8,128)(2,1)S(1)}, bf16[2,8,32,128]{3,2,1,0:T(8,128)(2,1)S(1)}, u32[]{:S(2)}, u32[]{:S(2)}) collective-permute-start(bf16[2,8,32,128]{3,2,1,0:T(8,128)(2,1)S(1)} %get-tuple-element.17.refs_0_.first), channel_id=1, source_target_pairs={{0,1},{1,0},{2,3},{3,2},{4,5},{5,4},{6,7},{7,6},{8,9},{9,8},{10,11... | collective-permute-start | bytes 393224 | tf_op jit(solution)/shard_map/ppermute | solution.py:172
  29.4 8.4 %collective-permute-start.8 = (bf16[2,16,32,128]{3,2,1,0:T(8,128)(2,1)S(1)}, bf16[2,16,32,128]{3,2,1,0:T(8,128)(2,1)S(1)}, u32[]{:S(2)}, u32[]{:S(2)}) collective-permute-start(bf16[2,16,32,128]{3,2,1,0:T(8,128)(2,1)S(1)} %get-tuple-element.19), channel_id=1, source_target_pairs={{0,4},{4,0},{8,12},{12,8},{16,20},{20,16},{24,28},{28,24},{32,36},... | collective-permute-start | bytes 786440 | tf_op jit(solution)/shard_map/ppermute | solution.py:179
  36.7 6.1 %collective-permute-start.9 = (bf16[2,16,32,128]{3,2,1,0:T(8,128)(2,1)S(1)}, bf16[2,16,32,128]{3,2,1,0:T(8,128)(2,1)S(1)}, u32[]{:S(2)}, u32[]{:S(2)}) collective-permute-start(bf16[2,16,32,128]{3,2,1,0:T(8,128)(2,1)S(1)} %get-tuple-element.20), channel_id=1, source_target_pairs={{0,252},{4,8},{8,4},{12,16},{16,12},{20,24},{24,20},{28,32},{32,28... | collective-permute-start | bytes 786440 | tf_op jit(solution)/shard_map/ppermute | solution.py:178
  47.0 10.3 %all-to-all-start = ((bf16[16,32,128]{2,1,0:T(8,128)(2,1)}), bf16[16,32,128]{2,1,0:T(8,128)(2,1)S(1)}, u32[]{:S(2)}, u32[]{:S(2)}) async-start(bf16[16,32,128]{2,1,0:T(8,128)(2,1)} %broadcast_in_dim.20), calls=%async_computation | async-start | bytes 262144 | tf_op jit(solution)/shard_map/all_to_all | solution.py:151
  50.5 6.8 %collective-permute-start.10 = (bf16[2,8,32,128]{3,2,1,0:T(8,128)(2,1)S(1)}, bf16[2,8,32,128]{3,2,1,0:T(8,128)(2,1)S(1)}, u32[]{:S(2)}, u32[]{:S(2)}) collective-permute-start(bf16[2,8,32,128]{3,2,1,0:T(8,128)(2,1)S(1)} %get-tuple-element.23), channel_id=1, source_target_pairs={{0,1},{1,0},{2,3},{3,2},{4,5},{5,4},{6,7},{7,6},{8,9},{9,8},{10,11... | collective-permute-start | bytes 393224 | tf_op jit(solution)/shard_map/ppermute | solution.py:245
  57.4 19.9 %collective-permute-start.11 = (bf16[2,2,8,32,128]{4,3,2,1,0:T(8,128)(2,1)S(1)}, bf16[2,2,8,32,128]{4,3,2,1,0:T(8,128)(2,1)S(1)}, u32[]{:S(2)}, u32[]{:S(2)}) collective-permute-start(bf16[2,2,8,32,128]{4,3,2,1,0:T(8,128)(2,1)S(1)} %pad_maximum_fusion.near), channel_id=1, source_target_pairs={{0,3},{1,2},{2,1},{3,0},{4,7},{5,6},{6,5},{7,4},{8,11},{9,10},{10,... | collective-permute-start | bytes 786440 | tf_op jit(solution)/shard_map/ppermute | solution.py:258

commit v3 on v2

--- a/solution.py
+++ b/solution.py
@@ -9,6 +9,7 @@
 
 CORES = 2
 LANES = 128
+CHUNK = 8
 SIDE_CHIPS = 4
 NT = (((1,), (1,)), ((), ()))
 VMEM = pl.BlockSpec(memory_space=pltpu.VMEM)
@@ -79,44 +80,50 @@
     )
 
 
-def apply_first(ints, coefs, slab, pair, cross, tiles, first, gram, ext):
+def list_cross(ints, listed, row_tiles, slots, slab_size, ghosts, odd):
+    found = jnp.int32(0)
+    for j in range(row_tiles):
+        for k in range(slots):
+            col = ints[j, k]
+            side = jnp.where(col >= slab_size + ghosts, 1, 0)
+            crosses = jnp.logical_and(col >= slab_size, side == odd)
+            listed[found] = j * slots + k
+            found += jnp.where(jnp.logical_and(crosses, k < ints[row_tiles, j]), 1, 0)
+    listed[row_tiles * slots + 1] = found
+
+
+def near_block(ints, ext, j, k, slab_size, ghosts, row_tiles, odd, lead):
+    col = ints[j, k]
+    side = jnp.where(col >= slab_size + ghosts, 1, 0)
+    near = jnp.logical_or(col < slab_size, side != odd)
+    used = jnp.logical_and(near, k < ints[row_tiles, j])
+    return jnp.where(used, ext[lead + (col,)], 0).astype(ext.dtype)
+
+
+def near_first(ints, slab, pair, tiles, part, listed, ext):
     volumes, row_tiles, slots, side, _ = tiles.shape
-    slab_size = slab.shape[0]
-    ghosts = pair.shape[0]
-    vectors = slab.shape[1]
-    me = lax.axis_index("help")
+    slab_size, ghosts, vectors = slab.shape[0], pair.shape[0], slab.shape[1]
     odd = lax.rem(lax.axis_index("rows"), 2)
     ext[pl.ds(0, slab_size)] = slab[...]
     ext[pl.ds(slab_size + (1 - odd) * ghosts, ghosts)] = pair[...]
-    ext[pl.ds(slab_size + odd * ghosts, ghosts)] = cross[...]
     for j in range(row_tiles):
         total = jnp.zeros((vectors, volumes * side), jnp.float32)
         for k in range(0, slots, 2):
             left = jnp.concatenate(
-                [jnp.where(q < ints[row_tiles, j], ext[ints[j, q]], 0).astype(ext.dtype) for q in (k, k + 1)], axis=1
+                [near_block(ints, ext, j, q, slab_size, ghosts, row_tiles, odd, ()) for q in (k, k + 1)], axis=1
             )
             total += lax.dot_general(left, tile_pair(tiles, j, k), NT, preferred_element_type=jnp.float32)
-        stored = slab[ints[row_tiles + 1, me * row_tiles + j]].astype(jnp.float32)
-        for v in range(volumes):
-            h = total[:, v * side:(v + 1) * side]
-            first[v, j] = ((h - coefs[v] * stored) / coefs[volumes + v]).astype(first.dtype)
-    for v in range(volumes):
-        field = jnp.concatenate([first[v, j] for j in range(row_tiles)], axis=1)
-        gram[v] = lax.dot_general(field, field, NT, preferred_element_type=jnp.float32)
-
-
-def apply_second(
-    ints, coefs, base, slab, pair, cross, tiles, first, gram_one, second, gram, ext
-):
+        for v in range(volumes):
+            part[v, j] = total[:, v * side:(v + 1) * side]
+    list_cross(ints, listed, row_tiles, slots, slab_size, ghosts, odd)
+
+
+def near_second(ints, slab, pair, tiles, part, ext):
     volumes, row_tiles, slots, side, _ = tiles.shape
-    slab_size = slab.shape[1]
-    ghosts = pair.shape[1]
-    vectors = slab.shape[2]
-    me = lax.axis_index("help")
+    slab_size, ghosts, vectors = slab.shape[1], pair.shape[1], slab.shape[2]
     odd = lax.rem(lax.axis_index("rows"), 2)
     ext[:, pl.ds(0, slab_size)] = slab[...]
     ext[:, pl.ds(slab_size + (1 - odd) * ghosts, ghosts)] = pair[...]
-    ext[:, pl.ds(slab_size + odd * ghosts, ghosts)] = cross[...]
     for j in range(row_tiles):
         total = jnp.zeros((volumes * vectors, volumes * side), jnp.float32)
         for k in range(0, slots, 2):
@@ -124,7 +131,7 @@
                 [
                     jnp.concatenate(
                         [
-                            jnp.where(q < ints[row_tiles, j], ext[v, ints[j, q]], 0).astype(ext.dtype)
+                            near_block(ints, ext, j, q, slab_size, ghosts, row_tiles, odd, (v,))
                             for q in (k, k + 1)
                         ],
                         axis=1,
@@ -134,11 +141,70 @@
                 axis=0,
             )
             total += lax.dot_general(left, tile_pair(tiles, j, k), NT, preferred_element_type=jnp.float32)
+        for v in range(volumes):
+            part[v, j] = total[v * vectors:(v + 1) * vectors, v * side:(v + 1) * side]
+
+
+def add_cross(ints, listed, cross, tiles, acc, lead):
+    volumes, row_tiles, slots, side, _ = tiles.shape
+    ghosts = cross.shape[len(lead)]
+    helpers = lax.axis_size("help")
+    odd = lax.rem(lax.axis_index("rows"), 2)
+    start = row_tiles * helpers + odd * ghosts
+    found = listed[row_tiles * slots + 1]
+
+    def chunk(i, carry):
+        products = []
+        for u in range(CHUNK):
+            at = i * CHUNK + u
+            used = at < found
+            item = jnp.where(used, listed[at], 0)
+            j = lax.div(item, slots)
+            k = lax.rem(item, slots)
+            g = jnp.where(used, ints[j, k] - start, 0)
+            if lead:
+                blocks = jnp.concatenate([cross[v, g] for v in range(volumes)], axis=0)
+            else:
+                blocks = cross[g]
+            blocks = jnp.where(used, blocks, 0).astype(cross.dtype)
+            weights = jnp.concatenate([tiles[v, j, k] for v in range(volumes)], axis=0)
+            products.append((j, lax.dot_general(blocks, weights, NT, preferred_element_type=jnp.float32)))
+        for j, product in products:
+            for v in range(volumes):
+                rows = product.shape[0] // volumes if lead else product.shape[0]
+                low = v * rows if lead else 0
+                acc[v, j] += product[low:low + rows, v * side:(v + 1) * side]
+        return carry
+
+    lax.fori_loop(0, lax.div(found + CHUNK - 1, CHUNK), chunk, 0)
+
+
+def apply_first(ints, coefs, listed, slab, cross, tiles, part, first, gram, acc):
+    volumes, row_tiles = first.shape[:2]
+    me = lax.axis_index("help")
+    acc[...] = part[...]
+    scales = [1.0 / jnp.full(acc.shape[2:], coefs[volumes + v]) for v in range(volumes)]
+    add_cross(ints, listed, cross, tiles, acc, ())
+    for j in range(row_tiles):
+        stored = slab[ints[row_tiles + 1, me * row_tiles + j]].astype(jnp.float32)
+        for v in range(volumes):
+            first[v, j] = ((acc[v, j] - coefs[v] * stored) * scales[v]).astype(first.dtype)
+    for v in range(volumes):
+        field = jnp.concatenate([first[v, j] for j in range(row_tiles)], axis=1)
+        gram[v] = lax.dot_general(field, field, NT, preferred_element_type=jnp.float32)
+
+
+def apply_second(ints, coefs, listed, base, cross, tiles, part, first, gram_one, second, gram, acc):
+    volumes, row_tiles = first.shape[:2]
+    me = lax.axis_index("help")
+    acc[...] = part[...]
+    scales = [1.0 / jnp.full(acc.shape[2:], coefs[volumes + v]) for v in range(volumes)]
+    add_cross(ints, listed, cross, tiles, acc, (0,))
+    for j in range(row_tiles):
         stored = base[ints[row_tiles + 1, me * row_tiles + j]].astype(jnp.float32)
         for v in range(volumes):
-            h = total[v * vectors:(v + 1) * vectors, v * side:(v + 1) * side]
-            inner = h - coefs[v] * first[v, j].astype(jnp.float32)
-            second[v, j] = (2.0 * inner / coefs[volumes + v] - stored).astype(second.dtype)
+            inner = acc[v, j] - coefs[v] * first[v, j].astype(jnp.float32)
+            second[v, j] = (2.0 * inner * scales[v] - stored).astype(second.dtype)
     parts = [gram_one[v] for v in range(volumes)]
     for v in range(volumes):
         field = jnp.concatenate([second[v, j] for j in range(row_tiles)], axis=1)
@@ -208,18 +274,35 @@
         name="spread_panel",
     )(ints, own_panel, *gathered(panel)[1:])
     pair, cross = exchanged(to_pair, to_cross)
+    part_shape = jax.ShapeDtypeStruct((volumes, row_tiles, vectors, side), jnp.float32)
+    listed_size = row_tiles * slots + 2
+    product_cost = pl.CostEstimate(
+        flops=4 * volumes * row_tiles * slots * side * side * vectors,
+        bytes_accessed=2 * tiles.size,
+        transcendentals=0,
+    )
+    part, listed = pl.pallas_call(
+        near_first,
+        out_shape=[part_shape, jax.ShapeDtypeStruct((listed_size,), jnp.int32)],
+        in_specs=[SMEM] + [VMEM] * 3,
+        out_specs=[VMEM, SMEM],
+        scratch_shapes=[pltpu.VMEM((slab_size + 2 * ghosts, vectors, side), bf16)],
+        compiler_params=params,
+        cost_estimate=product_cost,
+        name="near_first",
+    )(ints, base, pair, tiles)
     first, gram_one = pl.pallas_call(
         apply_first,
         out_shape=[
             shape(volumes, row_tiles, vectors, side),
             jax.ShapeDtypeStruct((volumes, vectors, vectors), jnp.float32),
         ],
-        in_specs=[SMEM] * 2 + [VMEM] * 4,
+        in_specs=[SMEM] * 3 + [VMEM] * 4,
         out_specs=[VMEM] * 2,
-        scratch_shapes=[pltpu.VMEM((slab_size + 2 * ghosts, vectors, side), bf16)],
+        scratch_shapes=[pltpu.VMEM(part_shape.shape, jnp.float32)],
         compiler_params=params,
         name="apply_first",
-    )(ints, coefs, base, pair, cross, tiles)
+    )(ints, coefs, listed, base, cross, tiles, part)
     slab, to_pair, to_cross = pl.pallas_call(
         functools.partial(spread_field, helpers),
         out_shape=[shape(volumes, slab_size, vectors, side)] + [shape(volumes, ghosts, vectors, side)] * 2,
@@ -229,18 +312,28 @@
         name="spread_field",
     )(ints, *gathered(first))
     pair, cross = exchanged(to_pair, to_cross)
+    part = pl.pallas_call(
+        near_second,
+        out_shape=part_shape,
+        in_specs=[SMEM] + [VMEM] * 3,
+        out_specs=VMEM,
+        scratch_shapes=[pltpu.VMEM((volumes, slab_size + 2 * ghosts, vectors, side), bf16)],
+        compiler_params=params,
+        cost_estimate=product_cost,
+        name="near_second",
+    )(ints, slab, pair, tiles)
     second, gram = pl.pallas_call(
         apply_second,
         out_shape=[
             shape(volumes, row_tiles, vectors, side),
             jax.ShapeDtypeStruct((vectors, 2 * volumes * vectors), jnp.float32),
         ],
-        in_specs=[SMEM] * 2 + [VMEM] * 7,
+        in_specs=[SMEM] * 3 + [VMEM] * 6,
         out_specs=[VMEM] * 2,
-        scratch_shapes=[pltpu.VMEM((volumes, slab_size + 2 * ghosts, vectors, side), bf16)],
+        scratch_shapes=[pltpu.VMEM(part_shape.shape, jnp.float32)],
         compiler_params=params,
         name="apply_second",
-    )(ints, coefs, base, slab, pair, cross, tiles, first, gram_one)
+    )(ints, coefs, listed, base, cross, tiles, part, first, gram_one)
 
     near_pair = jnp.stack([second, lax.ppermute(second, "help", [(i, i ^ 1) for i in range(helpers)])])
     near = [

time: 79.1 us -> 76.7 us (0.970)
  waiting for transfers between devices: 19.7 us -> 12.9 us
  Pallas kernels: 9.9 us -> 13.5 us
  starting transfers between devices: 23.5 us -> 25.1 us
  blocking collectives: 19.2 us -> 18.4 us
    pallas_call x0 -> x2, Pallas kernels: none -> 7.43 us  [the longest x1 4.14 us: per_device(): pl.pallas_call(near_first, out_shape=[part_shape, jax.ShapeDtypeStruct((l...]
    ppermute x2, waiting for transfers between devices: 8.34 us -> 1.63 us  [exchanged(): cross = lax.ppermute(to_cross, 'rows', cross_pairs)]
    pallas_call x1, Pallas kernels: 3.53 us -> 1.62 us  [per_device(): pl.pallas_call(apply_second, out_shape=[shape(volumes, row_tiles, vectors...]
    pallas_call x1, Pallas kernels: 3.34 us -> 1.45 us  [per_device(): pl.pallas_call(apply_first, out_shape=[shape(volumes, row_tiles, vectors,...]
    ppermute x2, starting transfers between devices: 10.2 us -> 11.3 us  [exchanged(): pair = lax.ppermute(to_pair, 'rows', [(s, s ^ 1) for s in range(rows)])]
    all_to_all x1, blocking collectives: 19.2 us -> 18.4 us  [summed_parts(): lax.all_to_all(parts, ('rows', 'help'), 0, 0, axis_index_groups=groups)]
  transfers between devices with their start and end apart: 13 -> 13, of which waited for: 7 -> 6; matrix products, arithmetic and copies ran while one was open for 0% -> 0% of each run, Pallas kernels for 0% -> 10%
where the time goes in v3:
time: 76.7 us; the launch traced here: 76.4 us
  starting transfers between devices  25.1 us (33%)
  blocking collectives  18.4 us (24%)
  Pallas kernels  13.5 us (18%)
  waiting for transfers between devices  12.9 us (17%)
  local copies, waits for them, and re-layouts  5.57 us (7%)
  between operations  0.8 us (1%)
    all_to_all x1, blocking collectives, summed_parts(): lax.all_to_all(parts, ('rows', 'help'), 0, 0, axis_index_groups=groups)  18.4 us
    ppermute x2, starting transfers between devices, exchanged(): pair = lax.ppermute(to_pair, 'rows', [(s, s ^ 1) for s in range(rows)])  11.3 us
    ppermute x6, starting transfers between devices, gathered(): lax.ppermute(shard, 'help', [(i, i ^ d) for i in range(helpers)])  7.85 us
    all_to_all x1, waiting for transfers between devices, summed_parts(): lax.all_to_all(parts, ('rows', 'help'), 0, 0, axis_index_groups=groups)  5.47 us
    unnamed x18, local copies, waits for them, and re-layouts  4.88 us
    pallas_call x1, Pallas kernels, per_device(): pl.pallas_call(near_first, out_shape=[part_shape, jax.ShapeDtypeStruct((l...  4.14 us
    all_to_all x1, starting transfers between devices, summed_parts(): lax.all_to_all(parts, ('rows', 'help'), 0, 0, axis_index_groups=groups)  3.81 us
    ppermute x6, waiting for transfers between devices, gathered(): lax.ppermute(shard, 'help', [(i, i ^ d) for i in range(helpers)])  3.81 us
  transfers between devices with their start and end apart: 13, of which 6 were waited for; matrix products, arithmetic and copies ran while one was open for 0% of the time, Pallas kernels for 10%

profile of v3, /device:TPU:1, one launch (start us, length us, event | category | flops | bytes accessed | tf_op | source)
XLA Modules:
  0.0 76.4 jit_solution(17193113062423382387)
XLA Ops:
  0.6 2.1 %collective-permute-start = (bf16[32,1024]{1,0:T(8,128)(2,1)}, bf16[32,1024]{1,0:T(8,128)(2,1)S(1)}, u32[]{:S(2)}, u32[]{:S(2)}) collective-permute-start(bf16[32,1024]{1,0:T(8,128)(2,1)} %panel.1), channel_id=1, source_target_pairs={{0,1},{1,0},{2,3},{3,2},{4,5},{5,4},{6,7},{7,6},{8,9},{9,8},{10,11... | collective-permute-start | bytes 196616 | tf_op jit(solution)/shard_map/ppermute | solution.py:238
  2.8 1.8 %collective-permute-start.2 = (bf16[32,1024]{1,0:T(8,128)(2,1)}, bf16[32,1024]{1,0:T(8,128)(2,1)S(1)}, u32[]{:S(2)}, u32[]{:S(2)}) collective-permute-start(bf16[32,1024]{1,0:T(8,128)(2,1)} %panel.1), channel_id=1, source_target_pairs={{0,3},{1,2},{2,1},{3,0},{4,7},{5,6},{6,5},{7,4},{8,11},{9,10},{10,... | collective-permute-start | bytes 196616 | tf_op jit(solution)/shard_map/ppermute | solution.py:238
  4.6 0.6 collective-permute-start.1
  5.2 0.0 copy-start
  5.2 3.4 %copy-done = bf16[2,8,16,128,128]{4,3,2,1,0:T(8,128)(2,1)S(1)} copy-done((bf16[2,8,16,128,128]{4,3,2,1,0:T(8,128)(2,1)S(1)}, bf16[2,8,16,128,128]{4,3,2,1,0:T(8,128)(2,1)}, u32[]{:S(2)}) %copy-start) | copy-done | bytes 8388632
  8.6 0.0 copy-start.2
  8.6 0.8 %copy-done.2 = bf16[32,1024]{1,0:T(8,128)(2,1)S(1)} copy-done((bf16[32,1024]{1,0:T(8,128)(2,1)S(1)}, bf16[32,1024]{1,0:T(8,128)(2,1)}, u32[]{:S(2)}) %copy-start.2) | copy-done | bytes 65560
  9.4 0.0 copy-start.3
  9.4 0.0 copy-start.4
  9.4 0.0 copy-start.5
  9.4 0.0 copy-start.6
  9.4 0.0 copy-start.7
  9.5 0.0 copy-start.8
  9.5 0.0 copy-start.1
  9.5 0.6 copy-done.3
  10.1 0.0 copy-done.4
  10.1 0.0 copy-done.5
  10.1 0.0 copy-done.6
  10.2 0.0 collective-permute-done.refs_1_
  10.2 0.0 collective-permute-done.2.refs_3_
  10.2 0.0 collective-permute-done.1.refs_2_
  10.2 0.7 spread_panel.1
  10.9 2.9 %collective-permute-start.3 = (bf16[16,32,128]{2,1,0:T(8,128)(2,1)S(1)}, bf16[16,32,128]{2,1,0:T(8,128)(2,1)S(1)}, u32[]{:S(2)}, u32[]{:S(2)}) collective-permute-start(bf16[16,32,128]{2,1,0:T(8,128)(2,1)S(1)} %get-tuple-element.17), channel_id=1, source_target_pairs={{0,4},{4,0},{8,12},{12,8},{16,20},{20,16},{24,28},{28,24},{32,36},... | collective-permute-start | bytes 393224 | tf_op jit(solution)/shard_map/ppermute | solution.py:245
  13.9 0.0 collective-permute-start.4
  13.9 0.0 copy-done.7
  13.9 0.0 copy-done.8
  13.9 0.1 pad_maximum_fusion.1.coefs
  14.0 0.9 %collective-permute-done.3.pair = bf16[16,32,128]{2,1,0:T(8,128)(2,1)S(1)} collective-permute-done((bf16[16,32,128]{2,1,0:T(8,128)(2,1)S(1)}, bf16[16,32,128]{2,1,0:T(8,128)(2,1)S(1)}, u32[]{:S(2)}, u32[]{:S(2)}) %collective-permute-start.3) | collective-permute-done | bytes 131104 | tf_op jit(solution)/shard_map/ppermute | solution.py:245
  14.8 0.0 copy-done.1
  14.9 4.1 %near_first.1 = (f32[2,8,32,128]{3,2,1,0:T(8,128)S(1)}, s32[130]{0:T(256)S(1)}) custom-call(s32[12,128]{1,0:T(8,128)S(1)} %pad_add_fusion.ints, bf16[32,32,128]{2,1,0:T(8,128)(2,1)S(1)} %get-tuple-element.16.slab.base, bf16[16,32,128]{2,1,0:T(8,128)(2,1)S(1)} %collective-permute-done.3.pair, bf16[2,8,16,128,128]{4,3,2,1,0:T(8,128)(2,1)S(1)} %copy-done.1), custom_call_target="tpu_custom_call" | custom-call | flops 536870912 | bytes 8388608 | tf_op jit(solution)/shard_map/near_first/pallas_call | solution.py:284
  19.0 0.0 collective-permute-done.4.cross
  19.0 1.5 %apply_first.1 = (bf16[2,8,32,128]{3,2,1,0:T(8,128)(2,1)S(1)}, f32[2,32,32]{2,1,0:T(8,128)S(1)}) custom-call(s32[12,128]{1,0:T(8,128)S(1)} %pad_add_fusion.ints, f32[4]{0:T(128)S(1)} %pad_maximum_fusion.1.coefs, s32[130]{0:T(256)S(1)} %get-tuple-element.18.listed, bf16[32,32,128]{2,1,0:T(8,128)(2,1)S(1)} %get-tuple-element.16.slab.base, ...), custom_call_target="tpu_custom_call" | custom-call | tf_op jit(solution)/shard_map/apply_first/pallas_call | solution.py:294
  20.5 1.7 %collective-permute-start.7 = (bf16[2,8,32,128]{3,2,1,0:T(8,128)(2,1)S(1)}, bf16[2,8,32,128]{3,2,1,0:T(8,128)(2,1)S(1)}, u32[]{:S(2)}, u32[]{:S(2)}) collective-permute-start(bf16[2,8,32,128]{3,2,1,0:T(8,128)(2,1)S(1)} %get-tuple-element.21.refs_0_.first), channel_id=1, source_target_pairs={{0,3},{1,2},{2,1},{3,0},{4,7},{5,6},{6,5},{7,4},{8,11},{9,10},{10,... | collective-permute-start | bytes 393224 | tf_op jit(solution)/shard_map/ppermute | solution.py:238
  22.2 0.2 collective-permute-start.6
  22.4 1.3 %collective-permute-start.5 = (bf16[2,8,32,128]{3,2,1,0:T(8,128)(2,1)S(1)}, bf16[2,8,32,128]{3,2,1,0:T(8,128)(2,1)S(1)}, u32[]{:S(2)}, u32[]{:S(2)}) collective-permute-start(bf16[2,8,32,128]{3,2,1,0:T(8,128)(2,1)S(1)} %get-tuple-element.21.refs_0_.first), channel_id=1, source_target_pairs={{0,1},{1,0},{2,3},{3,2},{4,5},{5,4},{6,7},{7,6},{8,9},{9,8},{10,11... | collective-permute-start | bytes 393224 | tf_op jit(solution)/shard_map/ppermute | solution.py:238
  23.7 1.8 %collective-permute-done.7.refs_3_ = bf16[2,8,32,128]{3,2,1,0:T(8,128)(2,1)S(1)} collective-permute-done((bf16[2,8,32,128]{3,2,1,0:T(8,128)(2,1)S(1)}, bf16[2,8,32,128]{3,2,1,0:T(8,128)(2,1)S(1)}, u32[]{:S(2)}, u32[]{:S(2)}) %collective-permute-start.7) | collective-permute-done | bytes 131104 | tf_op jit(solution)/shard_map/ppermute | solution.py:238
  25.5 2.0 %collective-permute-done.6.refs_2_ = bf16[2,8,32,128]{3,2,1,0:T(8,128)(2,1)S(1)} collective-permute-done((bf16[2,8,32,128]{3,2,1,0:T(8,128)(2,1)S(1)}, bf16[2,8,32,128]{3,2,1,0:T(8,128)(2,1)S(1)}, u32[]{:S(2)}, u32[]{:S(2)}) %collective-permute-start.6) | collective-permute-done | bytes 131104 | tf_op jit(solution)/shard_map/ppermute | solution.py:238
  27.5 0.0 collective-permute-done.5.refs_1_
  27.5 0.8 %spread_field.1 = (bf16[2,32,32,128]{3,2,1,0:T(8,128)(2,1)S(1)}, bf16[2,16,32,128]{3,2,1,0:T(8,128)(2,1)S(1)}, bf16[2,16,32,128]{3,2,1,0:T(8,128)(2,1)S(1)}) custom-call(s32[12,128]{1,0:T(8,128)S(1)} %pad_add_fusion.ints, bf16[2,8,32,128]{3,2,1,0:T(8,128)(2,1)S(1)} %get-tuple-element.21.refs_0_.first, ...), custom_call_target="tpu_custom_call" | custom-call | tf_op jit(solution)/shard_map/spread_field/pallas_call | solution.py:306
  28.3 8.3 %collective-permute-start.9 = (bf16[2,16,32,128]{3,2,1,0:T(8,128)(2,1)S(1)}, bf16[2,16,32,128]{3,2,1,0:T(8,128)(2,1)S(1)}, u32[]{:S(2)}, u32[]{:S(2)}) collective-permute-start(bf16[2,16,32,128]{3,2,1,0:T(8,128)(2,1)S(1)} %get-tuple-element.24), channel_id=1, source_target_pairs={{0,4},{4,0},{8,12},{12,8},{16,20},{20,16},{24,28},{28,24},{32,36},... | collective-permute-start | bytes 786440 | tf_op jit(solution)/shard_map/ppermute | solution.py:245
  36.7 0.0 collective-permute-start.8
  36.7 1.2 %collective-permute-done.9.pair = bf16[2,16,32,128]{3,2,1,0:T(8,128)(2,1)S(1)} collective-permute-done((bf16[2,16,32,128]{3,2,1,0:T(8,128)(2,1)S(1)}, bf16[2,16,32,128]{3,2,1,0:T(8,128)(2,1)S(1)}, u32[]{:S(2)}, u32[]{:S(2)}) %collective-permute-start.9) | collective-permute-done | bytes 262176 | tf_op jit(solution)/shard_map/ppermute | solution.py:245
  37.8 3.3 %near_second.1.part = f32[2,8,32,128]{3,2,1,0:T(8,128)S(1)} custom-call(s32[12,128]{1,0:T(8,128)S(1)} %pad_add_fusion.ints, bf16[2,32,32,128]{3,2,1,0:T(8,128)(2,1)S(1)} %get-tuple-element.23.slab, bf16[2,16,32,128]{3,2,1,0:T(8,128)(2,1)S(1)} %collective-permute-done.9.pair, bf16[2,8,16,128,128]{4,3,2,1,0:T(8,128)(2,1)S(1)} %copy-done.1), custom_call_target="tpu_custom_call" | custom-call | flops 536870912 | bytes 8388608 | tf_op jit(solution)/shard_map/near_second/pallas_call | solution.py:315
  41.1 1.6 %collective-permute-done.8.cross = bf16[2,16,32,128]{3,2,1,0:T(8,128)(2,1)S(1)} collective-permute-done((bf16[2,16,32,128]{3,2,1,0:T(8,128)(2,1)S(1)}, bf16[2,16,32,128]{3,2,1,0:T(8,128)(2,1)S(1)}, u32[]{:S(2)}, u32[]{:S(2)}) %collective-permute-start.8) | collective-permute-done | bytes 262176 | tf_op jit(solution)/shard_map/ppermute | solution.py:244
  42.8 1.6 %apply_second.1 = (bf16[2,8,32,128]{3,2,1,0:T(8,128)(2,1)S(1)}, f32[32,128]{1,0:T(8,128)S(1)}) custom-call(s32[12,128]{1,0:T(8,128)S(1)} %pad_add_fusion.ints, f32[4]{0:T(128)S(1)} %pad_maximum_fusion.1.coefs, s32[130]{0:T(256)S(1)} %get-tuple-element.18.listed, bf16[32,32,128]{2,1,0:T(8,128)(2,1)S(1)} %get-tuple-element.16.slab.base, ...), custom_call_target="tpu_custom_call" | custom-call | tf_op jit(solution)/shard_map/apply_second/pallas_call | solution.py:325
  44.4 0.7 broadcast_in_dim.20
  45.1 3.8 %all-to-all-start = ((bf16[16,32,128]{2,1,0:T(8,128)(2,1)}), bf16[16,32,128]{2,1,0:T(8,128)(2,1)S(1)}, u32[]{:S(2)}, u32[]{:S(2)}) async-start(bf16[16,32,128]{2,1,0:T(8,128)(2,1)} %broadcast_in_dim.20), calls=%async_computation | async-start | bytes 262144 | tf_op jit(solution)/shard_map/all_to_all | solution.py:217
  48.9 1.4 %collective-permute-start.10 = (bf16[2,8,32,128]{3,2,1,0:T(8,128)(2,1)S(1)}, bf16[2,8,32,128]{3,2,1,0:T(8,128)(2,1)S(1)}, u32[]{:S(2)}, u32[]{:S(2)}) collective-permute-start(bf16[2,8,32,128]{3,2,1,0:T(8,128)(2,1)S(1)} %get-tuple-element.27), channel_id=1, source_target_pairs={{0,1},{1,0},{2,3},{3,2},{4,5},{5,4},{6,7},{7,6},{8,9},{9,8},{10,11... | collective-permute-start | bytes 393224 | tf_op jit(solution)/shard_map/ppermute | solution.py:338
  50.3 5.5 %all-to-all-done = bf16[16,32,128]{2,1,0:T(8,128)(2,1)S(1)} async-done(((bf16[16,32,128]{2,1,0:T(8,128)(2,1)}), bf16[16,32,128]{2,1,0:T(8,128)(2,1)S(1)}, u32[]{:S(2)}, u32[]{:S(2)}) %all-to-all-start) | async-done | bytes 131104 | tf_op jit(solution)/shard_map/all_to_all | solution.py:217
  55.8 0.0 collective-permute-done.10
  55.8 0.7 collective-permute-start.11
  56.6 18.4 %all_to_all.10.parts = bf16[16,32,128]{2,1,0:T(8,128)(2,1)S(1)} all-to-all(bf16[16,32,128]{2,1,0:T(8,128)(2,1)S(1)} %broadcast_in_dim.21), channel_id=1, replica_groups={{0,4,32,36,64,68,96,100,128,132,160,164,192,196,224,228},{1,5,33,37,65,..., dimensions={0} | all-to-all | bytes 262144 | tf_op jit(solution)/shard_map/all_to_all | solution.py:217
  75.0 0.0 collective-permute-done.11.far
  75.0 1.5 %finish.1 = (bf16[2,32,1024]{2,1,0:T(8,128)(2,1)}, f32[2,2,32,32]{3,2,1,0:T(8,128)}) custom-call(s32[12,128]{1,0:T(8,128)S(1)} %pad_add_fusion.ints, bf16[16,32,128]{2,1,0:T(8,128)(2,1)S(1)} %all_to_all.10.parts, bf16[2,2,8,32,128]{4,3,2,1,0:T(8,128)(2,1)S(1)} %pad_maximum_fusion.near, bf16[2,2,8,32,128]{4,3,2,1,0:T(8,128)(2,1)S(1)} %collective-permute-done.11.far), custom_call_target="tpu_custom_call" | custom-call | tf_op jit(solution)/shard_map/finish/pallas_call | solution.py:353
  (6 shorter events, 0.1 us)
Async XLA Ops:
  0.6 9.5 %collective-permute-start = (bf16[32,1024]{1,0:T(8,128)(2,1)}, bf16[32,1024]{1,0:T(8,128)(2,1)S(1)}, u32[]{:S(2)}, u32[]{:S(2)}) collective-permute-start(bf16[32,1024]{1,0:T(8,128)(2,1)} %panel.1), channel_id=1, source_target_pairs={{0,1},{1,0},{2,3},{3,2},{4,5},{5,4},{6,7},{7,6},{8,9},{9,8},{10,11... | collective-permute-start | bytes 196616 | tf_op jit(solution)/shard_map/ppermute | solution.py:238
  2.8 7.4 %collective-permute-start.2 = (bf16[32,1024]{1,0:T(8,128)(2,1)}, bf16[32,1024]{1,0:T(8,128)(2,1)S(1)}, u32[]{:S(2)}, u32[]{:S(2)}) collective-permute-start(bf16[32,1024]{1,0:T(8,128)(2,1)} %panel.1), channel_id=1, source_target_pairs={{0,3},{1,2},{2,1},{3,0},{4,7},{5,6},{6,5},{7,4},{8,11},{9,10},{10,... | collective-permute-start | bytes 196616 | tf_op jit(solution)/shard_map/ppermute | solution.py:238
  4.6 5.6 %collective-permute-start.1 = (bf16[32,1024]{1,0:T(8,128)(2,1)}, bf16[32,1024]{1,0:T(8,128)(2,1)S(1)}, u32[]{:S(2)}, u32[]{:S(2)}) collective-permute-start(bf16[32,1024]{1,0:T(8,128)(2,1)} %panel.1), channel_id=1, source_target_pairs={{0,2},{1,3},{2,0},{3,1},{4,6},{5,7},{6,4},{7,5},{8,10},{9,11},{10,... | collective-permute-start | bytes 196616 | tf_op jit(solution)/shard_map/ppermute | solution.py:238
  5.2 3.4 %copy-start = (bf16[2,8,16,128,128]{4,3,2,1,0:T(8,128)(2,1)S(1)}, bf16[2,8,16,128,128]{4,3,2,1,0:T(8,128)(2,1)}, u32[]{:S(2)}) copy-start(bf16[2,8,16,128,128]{4,3,2,1,0:T(8,128)(2,1)} %tiles.9) | copy-start | bytes 25165828
  8.6 0.8 %copy-start.2 = (bf16[32,1024]{1,0:T(8,128)(2,1)S(1)}, bf16[32,1024]{1,0:T(8,128)(2,1)}, u32[]{:S(2)}) copy-start(bf16[32,1024]{1,0:T(8,128)(2,1)} %panel.1) | copy-start | bytes 196612
  9.4 0.7 copy-start.3
  9.4 0.7 copy-start.4
  9.4 0.7 copy-start.5
  9.4 0.7 copy-start.6
  9.4 4.5 %copy-start.7 = (f32[2]{0:T(128)S(1)}, f32[2]{0:T(128)}, u32[]{:S(2)}) copy-start(f32[2]{0:T(128)} %param.15) | copy-start | bytes 28
  9.5 4.5 %copy-start.8 = (f32[2]{0:T(128)S(1)}, f32[2]{0:T(128)}, u32[]{:S(2)}) copy-start(f32[2]{0:T(128)} %param.14) | copy-start | bytes 28
  9.5 5.4 %copy-start.1 = (bf16[2,8,16,128,128]{4,3,2,1,0:T(8,128)(2,1)S(1)}, bf16[2,8,16,128,128]{4,3,2,1,0:T(8,128)(2,1)}, u32[]{:S(2)}) copy-start(bf16[2,8,16,128,128]{4,3,2,1,0:T(8,128)(2,1)} %tiles.9) | copy-start | bytes 25165828
  10.9 3.9 %collective-permute-start.3 = (bf16[16,32,128]{2,1,0:T(8,128)(2,1)S(1)}, bf16[16,32,128]{2,1,0:T(8,128)(2,1)S(1)}, u32[]{:S(2)}, u32[]{:S(2)}) collective-permute-start(bf16[16,32,128]{2,1,0:T(8,128)(2,1)S(1)} %get-tuple-element.17), channel_id=1, source_target_pairs={{0,4},{4,0},{8,12},{12,8},{16,20},{20,16},{24,28},{28,24},{32,36},... | collective-permute-start | bytes 393224 | tf_op jit(solution)/shard_map/ppermute | solution.py:245
  13.9 5.1 %collective-permute-start.4 = (bf16[16,32,128]{2,1,0:T(8,128)(2,1)S(1)}, bf16[16,32,128]{2,1,0:T(8,128)(2,1)S(1)}, u32[]{:S(2)}, u32[]{:S(2)}) collective-permute-start(bf16[16,32,128]{2,1,0:T(8,128)(2,1)S(1)} %get-tuple-element.19), channel_id=1, source_target_pairs={{0,252},{4,8},{8,4},{12,16},{16,12},{20,24},{24,20},{28,32},{32,28... | collective-permute-start | bytes 393224 | tf_op jit(solution)/shard_map/ppermute | solution.py:244
  20.5 5.0 %collective-permute-start.7 = (bf16[2,8,32,128]{3,2,1,0:T(8,128)(2,1)S(1)}, bf16[2,8,32,128]{3,2,1,0:T(8,128)(2,1)S(1)}, u32[]{:S(2)}, u32[]{:S(2)}) collective-permute-start(bf16[2,8,32,128]{3,2,1,0:T(8,128)(2,1)S(1)} %get-tuple-element.21.refs_0_.first), channel_id=1, source_target_pairs={{0,3},{1,2},{2,1},{3,0},{4,7},{5,6},{6,5},{7,4},{8,11},{9,10},{10,... | collective-permute-start | bytes 393224 | tf_op jit(solution)/shard_map/ppermute | solution.py:238
  22.2 5.3 %collective-permute-start.6 = (bf16[2,8,32,128]{3,2,1,0:T(8,128)(2,1)S(1)}, bf16[2,8,32,128]{3,2,1,0:T(8,128)(2,1)S(1)}, u32[]{:S(2)}, u32[]{:S(2)}) collective-permute-start(bf16[2,8,32,128]{3,2,1,0:T(8,128)(2,1)S(1)} %get-tuple-element.21.refs_0_.first), channel_id=1, source_target_pairs={{0,2},{1,3},{2,0},{3,1},{4,6},{5,7},{6,4},{7,5},{8,10},{9,11},{10,... | collective-permute-start | bytes 393224 | tf_op jit(solution)/shard_map/ppermute | solution.py:238
  22.4 5.1 %collective-permute-start.5 = (bf16[2,8,32,128]{3,2,1,0:T(8,128)(2,1)S(1)}, bf16[2,8,32,128]{3,2,1,0:T(8,128)(2,1)S(1)}, u32[]{:S(2)}, u32[]{:S(2)}) collective-permute-start(bf16[2,8,32,128]{3,2,1,0:T(8,128)(2,1)S(1)} %get-tuple-element.21.refs_0_.first), channel_id=1, source_target_pairs={{0,1},{1,0},{2,3},{3,2},{4,5},{5,4},{6,7},{7,6},{8,9},{9,8},{10,11... | collective-permute-start | bytes 393224 | tf_op jit(solution)/shard_map/ppermute | solution.py:238
  28.3 9.5 %collective-permute-start.9 = (bf16[2,16,32,128]{3,2,1,0:T(8,128)(2,1)S(1)}, bf16[2,16,32,128]{3,2,1,0:T(8,128)(2,1)S(1)}, u32[]{:S(2)}, u32[]{:S(2)}) collective-permute-start(bf16[2,16,32,128]{3,2,1,0:T(8,128)(2,1)S(1)} %get-tuple-element.24), channel_id=1, source_target_pairs={{0,4},{4,0},{8,12},{12,8},{16,20},{20,16},{24,28},{28,24},{32,36},... | collective-permute-start | bytes 786440 | tf_op jit(solution)/shard_map/ppermute | solution.py:245
  36.7 6.1 %collective-permute-start.8 = (bf16[2,16,32,128]{3,2,1,0:T(8,128)(2,1)S(1)}, bf16[2,16,32,128]{3,2,1,0:T(8,128)(2,1)S(1)}, u32[]{:S(2)}, u32[]{:S(2)}) collective-permute-start(bf16[2,16,32,128]{3,2,1,0:T(8,128)(2,1)S(1)} %get-tuple-element.22), channel_id=1, source_target_pairs={{0,252},{4,8},{8,4},{12,16},{16,12},{20,24},{24,20},{28,32},{32,28... | collective-permute-start | bytes 786440 | tf_op jit(solution)/shard_map/ppermute | solution.py:244
  45.1 10.7 %all-to-all-start = ((bf16[16,32,128]{2,1,0:T(8,128)(2,1)}), bf16[16,32,128]{2,1,0:T(8,128)(2,1)S(1)}, u32[]{:S(2)}, u32[]{:S(2)}) async-start(bf16[16,32,128]{2,1,0:T(8,128)(2,1)} %broadcast_in_dim.20), calls=%async_computation | async-start | bytes 262144 | tf_op jit(solution)/shard_map/all_to_all | solution.py:217
  48.9 6.9 %collective-permute-start.10 = (bf16[2,8,32,128]{3,2,1,0:T(8,128)(2,1)S(1)}, bf16[2,8,32,128]{3,2,1,0:T(8,128)(2,1)S(1)}, u32[]{:S(2)}, u32[]{:S(2)}) collective-permute-start(bf16[2,8,32,128]{3,2,1,0:T(8,128)(2,1)S(1)} %get-tuple-element.27), channel_id=1, source_target_pairs={{0,1},{1,0},{2,3},{3,2},{4,5},{5,4},{6,7},{7,6},{8,9},{9,8},{10,11... | collective-permute-start | bytes 393224 | tf_op jit(solution)/shard_map/ppermute | solution.py:338
  55.8 19.2 %collective-permute-start.11 = (bf16[2,2,8,32,128]{4,3,2,1,0:T(8,128)(2,1)S(1)}, bf16[2,2,8,32,128]{4,3,2,1,0:T(8,128)(2,1)S(1)}, u32[]{:S(2)}, u32[]{:S(2)}) collective-permute-start(bf16[2,2,8,32,128]{4,3,2,1,0:T(8,128)(2,1)S(1)} %pad_maximum_fusion.near), channel_id=1, source_target_pairs={{0,3},{1,2},{2,1},{3,0},{4,7},{5,6},{6,5},{7,4},{8,11},{9,10},{10,... | collective-permute-start | bytes 786440 | tf_op jit(solution)/shard_map/ppermute | solution.py:351

commit v4 on v3

v4 whole, which is shorter than its diff:
```python
import functools

import jax
import jax.numpy as jnp
from jax import lax
from jax.experimental import pallas as pl
from jax.experimental.pallas import tpu as pltpu
from jax.sharding import PartitionSpec as P

CORES = 2
LANES = 128
CHUNK = 8
SIDE_CHIPS = 4
NT = (((1,), (1,)), ((), ()))
VMEM = pl.BlockSpec(memory_space=pltpu.VMEM)


def own_blocks(panel, tiles, blocks):
    side = blocks.shape[2]
    for j in range(blocks.shape[0]):
        blocks[j] = panel[:, j * side:(j + 1) * side]


def rolled(row, first):
    return pltpu.roll(row, lax.rem(row.shape[1] - first, row.shape[1]), 1)


def ghost_rows(ints, row_tiles, odd):
    to_prev = ints[row_tiles + 2:row_tiles + 3, :]
    to_next = ints[row_tiles + 3:row_tiles + 4, :]
    return jnp.where(odd == 1, to_prev, to_next), jnp.where(odd == 1, to_next, to_prev)


def spread_panel(helpers, ints, *refs):
    shards, (slab, to_pair, to_cross) = refs[:helpers], refs[helpers:]
    me = lax.axis_index("help")
    odd = lax.rem(lax.axis_index("rows"), 2)
    side = slab.shape[2]
    row_tiles = slab.shape[0] // helpers
    for d in range(helpers):
        base = (me ^ d) * row_tiles
        for j in range(row_tiles):
            slab[base + j] = shards[d][:, j * side:(j + 1) * side] if d else shards[0][j]
    pair_rows, cross_rows = ghost_rows(ints, row_tiles, odd)
    for g in range(to_pair.shape[0]):
        to_cross[g] = slab[cross_rows[0, g]]
        to_pair[g] = slab[pair_rows[0, g]]


def spread_field(helpers, table, *refs):
    shards, (slab, to_pair, to_cross) = refs[:helpers], refs[helpers:]
    me = lax.axis_index("help")
    row_tiles = slab.shape[1] // helpers
    for d in range(helpers):
        slab[:, pl.ds((me ^ d) * row_tiles, row_tiles)] = shards[d][...]
    for g in range(to_pair.shape[1]):
        to_cross[:, g] = slab[:, table[3, g]]
        to_pair[:, g] = slab[:, table[2, g]]


def place_field(helpers, table, *refs):
    shards, out = refs[:helpers], refs[helpers]
    me = lax.axis_index("help")
    row_tiles, side = shards[0].shape[1], shards[0].shape[3]
    slots = rolled(table[4:5, :], me * row_tiles)
    for j in range(row_tiles):
        slot = slots[0, j]
        held = lax.rem(slot, row_tiles)
        step = lax.div(slot, row_tiles) ^ me
        block = shards[0][:, held]
        for d in range(1, helpers):
            block = jnp.where(step == d, shards[d][:, held], block)
        out[:, :, j * side:(j + 1) * side] = block


def finish_gram(scale, parts, gram):
    volumes, steps, vectors, _ = gram.shape
    total = jnp.sum(parts[...].astype(jnp.float32), axis=0) * scale
    for step in range(steps):
        for v in range(volumes):
            at = (step * volumes + v) * vectors
            gram[v, step] = total[:, at:at + vectors]


def tile_pair(tiles, j, k):
    return jnp.concatenate(
        [jnp.concatenate([tiles[v, j, k], tiles[v, j, k + 1]], axis=1) for v in range(tiles.shape[0])],
        axis=0,
    )


def near_block(ints, ext, j, k, slab_size, ghosts, row_tiles, odd, lead):
    col = ints[j, k]
    side = jnp.where(col >= slab_size + ghosts, 1, 0)
    near = jnp.logical_or(col < slab_size, side != odd)
    used = jnp.logical_and(near, k < ints[row_tiles, j])
    return jnp.where(used, ext[lead + (col,)], 0).astype(ext.dtype)


def make_table(ints, built, row_tiles, slots, slab_size, ghosts, odd):
    low = slab_size + odd * ghosts
    found = jnp.int32(0)
    for j in range(row_tiles):
        live = ints[row_tiles, j]
        for k in range(slots):
            ghost = ints[j, k] - low
            built[0, found] = (j * slots + k) * ghosts + ghost
            crosses = jnp.logical_and(jnp.logical_and(ghost >= 0, ghost < ghosts), k < live)
            found += jnp.where(crosses, 1, 0)
    built[1, 0] = found
    for q in range(slab_size):
        built[4, ints[row_tiles + 1, q]] = q
    pair_rows, cross_rows = ghost_rows(ints, row_tiles, odd)
    for g in range(ghosts):
        built[2, g] = built[4, pair_rows[0, g]]
        built[3, g] = built[4, cross_rows[0, g]]


def near_first(ints, slab, pair, tiles, part, stored, table, ext, built, done):
    volumes, row_tiles, slots, side, _ = tiles.shape
    slab_size, ghosts, vectors = slab.shape[0], pair.shape[0], slab.shape[1]
    me = lax.axis_index("help")
    odd = lax.rem(lax.axis_index("rows"), 2)
    make_table(ints, built, row_tiles, slots, slab_size, ghosts, odd)
    hand_over = pltpu.make_async_copy(built, table, done)
    hand_over.start()
    ext[pl.ds(0, slab_size)] = slab[...]
    ext[pl.ds(slab_size + (1 - odd) * ghosts, ghosts)] = pair[...]
    mine = rolled(ints[row_tiles + 1:row_tiles + 2, :], me * row_tiles)
    for j in range(row_tiles):
        total = jnp.zeros((vectors, volumes * side), jnp.float32)
        for k in range(0, slots, 2):
            left = jnp.concatenate(
                [near_block(ints, ext, j, q, slab_size, ghosts, row_tiles, odd, ()) for q in (k, k + 1)], axis=1
            )
            total += lax.dot_general(left, tile_pair(tiles, j, k), NT, preferred_element_type=jnp.float32)
        for v in range(volumes):
            part[v, j] = total[:, v * side:(v + 1) * side]
        stored[j] = slab[mine[0, j]]
    hand_over.wait()


def near_second(ints, slab, pair, tiles, part, ext):
    volumes, row_tiles, slots, side, _ = tiles.shape
    slab_size, ghosts, vectors = slab.shape[1], pair.shape[1], slab.shape[2]
    odd = lax.rem(lax.axis_index("rows"), 2)
    for q in range(slab_size):
        ext[:, ints[row_tiles + 1, q]] = slab[:, q]
    ext[:, pl.ds(slab_size + (1 - odd) * ghosts, ghosts)] = pair[...]
    for j in range(row_tiles):
        total = jnp.zeros((volumes * vectors, volumes * side), jnp.float32)
        for k in range(0, slots, 2):
            left = jnp.concatenate(
                [
                    jnp.concatenate(
                        [
                            near_block(ints, ext, j, q, slab_size, ghosts, row_tiles, odd, (v,))
                            for q in (k, k + 1)
                        ],
                        axis=1,
                    )
                    for v in range(volumes)
                ],
                axis=0,
            )
            total += lax.dot_general(left, tile_pair(tiles, j, k), NT, preferred_element_type=jnp.float32)
        for v in range(volumes):
            part[v, j] = total[v * vectors:(v + 1) * vectors, v * side:(v + 1) * side]


def add_cross(table, cross, tiles, acc, lead):
    volumes, row_tiles, slots, side, _ = tiles.shape
    ghosts = cross.shape[len(lead)]
    items = table[0:1, :]
    found = table[1, 0]

    def chunk_items(i):
        row = rolled(items, lax.rem(i * CHUNK, LANES))
        return tuple(row[0, u] for u in range(CHUNK))

    def chunk(i, held):
        products = []
        for u in range(CHUNK):
            used = i * CHUNK + u < found
            item = jnp.where(used, held[u], 0)
            tile = lax.div(item, ghosts)
            g = lax.rem(item, ghosts)
            j = lax.div(tile, slots)
            k = lax.rem(tile, slots)
            if lead:
                blocks = jnp.concatenate([cross[v, g] for v in range(volumes)], axis=0)
            else:
                blocks = cross[g]
            blocks = jnp.where(used, blocks, 0).astype(cross.dtype)
            weights = jnp.concatenate([tiles[v, j, k] for v in range(volumes)], axis=0)
            products.append((j, lax.dot_general(blocks, weights, NT, preferred_element_type=jnp.float32)))
        following = chunk_items(i + 1)
        for j, product in products:
            for v in range(volumes):
                rows = product.shape[0] // volumes if lead else product.shape[0]
                low = v * rows if lead else 0
                acc[v, j] += product[low:low + rows, v * side:(v + 1) * side]
        return following

    lax.fori_loop(0, lax.div(found + CHUNK - 1, CHUNK), chunk, chunk_items(jnp.int32(0)))


def apply_first(coefs, table, stored, cross, tiles, part, first, gram, acc):
    volumes, row_tiles = first.shape[:2]
    acc[...] = part[...]
    add_cross(table, cross, tiles, acc, ())
    for v in range(volumes):
        centre = coefs[v:v + 1, :]
        scale = 1.0 / coefs[volumes + v:volumes + v + 1, :]
        for j in range(row_tiles):
            first[v, j] = ((acc[v, j] - centre * stored[j].astype(jnp.float32)) * scale).astype(first.dtype)
        field = jnp.concatenate([first[v, j] for j in range(row_tiles)], axis=1)
        gram[v] = lax.dot_general(field, field, NT, preferred_element_type=jnp.float32)


def apply_second(coefs, table, stored, cross, tiles, part, first, gram_one, second, gram, acc):
    volumes, row_tiles = first.shape[:2]
    acc[...] = part[...]
    add_cross(table, cross, tiles, acc, (0,))
    parts = [gram_one[v] for v in range(volumes)]
    for v in range(volumes):
        centre = coefs[v:v + 1, :]
        scale = 2.0 / coefs[volumes + v:volumes + v + 1, :]
        for j in range(row_tiles):
            inner = acc[v, j] - centre * first[v, j].astype(jnp.float32)
            second[v, j] = (inner * scale - stored[j].astype(jnp.float32)).astype(second.dtype)
        field = jnp.concatenate([second[v, j] for j in range(row_tiles)], axis=1)
        parts.append(lax.dot_general(field, field, NT, preferred_element_type=jnp.float32))
    gram[...] = jnp.concatenate(parts, axis=1)


def summed_parts(value, groups):
    parts = jnp.broadcast_to(value.astype(jnp.bfloat16)[None], (len(groups[0]),) + value.shape)
    return lax.all_to_all(parts, ("rows", "help"), 0, 0, axis_index_groups=groups)


def per_device(panel, tiles, tile_cols, tile_count, row_assign, send_lists, centers, half_widths):
    helpers = lax.axis_size("help")
    rows = lax.axis_size("rows")
    volumes, row_tiles, slots, side, _ = tiles.shape
    vectors = panel.shape[0]
    ghosts = send_lists.shape[2]
    slab_size = row_tiles * helpers
    bf16 = panel.dtype
    depth = rows // (SIDE_CHIPS * CORES)

    def at(z, y, core, x):
        return ((z * SIDE_CHIPS + y) * CORES + core) * helpers + x

    def shape(*dims):
        return jax.ShapeDtypeStruct(dims, bf16)

    def gathered(shard):
        others = [
            lax.ppermute(shard, "help", [(i, i ^ d) for i in range(helpers)]) for d in range(1, helpers)
        ]
        return [shard] + others

    def exchanged(to_pair, to_cross):
        cross_pairs = [(s, (s + 1) % rows if s % 2 else (s - 1) % rows) for s in range(rows)]
        cross = lax.ppermute(to_cross, "rows", cross_pairs)
        pair = lax.ppermute(to_pair, "rows", [(s, s ^ 1) for s in range(rows)])
        return pair, cross

    params = pltpu.CompilerParams(vmem_limit_bytes=24 * 1024 * 1024)

    ints = jnp.concatenate(
        [
            jnp.pad(tile_cols, ((0, 0), (0, LANES - slots))),
            jnp.pad(tile_count[None], ((0, 0), (0, LANES - row_tiles))),
            jnp.pad(row_assign[None], ((0, 0), (0, LANES - slab_size))),
            jnp.pad(send_lists[0], ((0, 0), (0, LANES - ghosts))),
        ],
        axis=0,
    )
    coefs = jnp.broadcast_to(jnp.concatenate([centers, half_widths])[:, None], (2 * volumes, LANES))
    own_panel = pl.pallas_call(
        own_blocks,
        out_shape=shape(row_tiles, vectors, side),
        in_specs=[VMEM] * 2,
        out_specs=VMEM,
        compiler_params=params,
        name="own_blocks",
    )(panel, tiles)
    base, to_pair, to_cross = pl.pallas_call(
        functools.partial(spread_panel, helpers),
        out_shape=[shape(slab_size, vectors, side)] + [shape(ghosts, vectors, side)] * 2,
        in_specs=[VMEM] * (1 + helpers),
        out_specs=[VMEM] * 3,
        compiler_params=params,
        name="spread_panel",
    )(ints, own_panel, *gathered(panel)[1:])
    pair, cross = exchanged(to_pair, to_cross)
    part_shape = jax.ShapeDtypeStruct((volumes, row_tiles, vectors, side), jnp.float32)
    product_cost = pl.CostEstimate(
        flops=4 * volumes * row_tiles * slots * side * side * vectors,
        bytes_accessed=2 * tiles.size,
        transcendentals=0,
    )
    table_shape = (5, LANES)
    part, stored, table = pl.pallas_call(
        near_first,
        out_shape=[
            part_shape,
            shape(row_tiles, vectors, side),
            jax.ShapeDtypeStruct(table_shape, jnp.int32),
        ],
        in_specs=[VMEM] * 4,
        out_specs=[VMEM] * 3,
        scratch_shapes=[
            pltpu.VMEM((slab_size + 2 * ghosts, vectors, side), bf16),
            pltpu.SMEM(table_shape, jnp.int32),
            pltpu.SemaphoreType.DMA,
        ],
        compiler_params=params,
        cost_estimate=product_cost,
        name="near_first",
    )(ints, base, pair, tiles)
    first, gram_one = pl.pallas_call(
        apply_first,
        out_shape=[
            shape(volumes, row_tiles, vectors, side),
            jax.ShapeDtypeStruct((volumes, vectors, vectors), jnp.float32),
        ],
        in_specs=[VMEM] * 6,
        out_specs=[VMEM] * 2,
        scratch_shapes=[pltpu.VMEM(part_shape.shape, jnp.float32)],
        compiler_params=params,
        name="apply_first",
    )(coefs, table, stored, cross, tiles, part)
    slab, to_pair, to_cross = pl.pallas_call(
        functools.partial(spread_field, helpers),
        out_shape=[shape(volumes, slab_size, vectors, side)] + [shape(volumes, ghosts, vectors, side)] * 2,
        in_specs=[VMEM] * (1 + helpers),
        out_specs=[VMEM] * 3,
        compiler_params=params,
        name="spread_field",
    )(table, *gathered(first))
    pair, cross = exchanged(to_pair, to_cross)
    part = pl.pallas_call(
        near_second,
        out_shape=part_shape,
        in_specs=[VMEM] * 4,
        out_specs=VMEM,
        scratch_shapes=[pltpu.VMEM((volumes, slab_size + 2 * ghosts, vectors, side), bf16)],
        compiler_params=params,
        cost_estimate=product_cost,
        name="near_second",
    )(ints, slab, pair, tiles)
    second, gram = pl.pallas_call(
        apply_second,
        out_shape=[
            shape(volumes, row_tiles, vectors, side),
            jax.ShapeDtypeStruct((vectors, 2 * volumes * vectors), jnp.float32),
        ],
        in_specs=[VMEM] * 8,
        out_specs=[VMEM] * 2,
        scratch_shapes=[pltpu.VMEM(part_shape.shape, jnp.float32)],
        compiler_params=params,
        name="apply_second",
    )(coefs, table, stored, cross, tiles, part, first, gram_one)

    shards = gathered(second)
    near = [
        [at(z, y, c, x) for y in range(SIDE_CHIPS) for x in range(helpers)]
        for z in range(depth)
        for c in range(CORES)
    ]
    far = [
        [at(z, y, c, x) for z in range(depth) for c in range(CORES)]
        for y in range(SIDE_CHIPS)
        for x in range(helpers)
    ]
    gram = jnp.sum(summed_parts(gram, near).astype(jnp.float32), axis=0)
    gram, shards[1], shards[3] = lax.optimization_barrier((gram, shards[1], shards[3]))
    parts = summed_parts(gram, far)
    filtered = pl.pallas_call(
        functools.partial(place_field, helpers),
        out_shape=shape(volumes, vectors, row_tiles * side),
        in_specs=[VMEM] * (1 + helpers),
        out_specs=VMEM,
        compiler_params=params,
        name="place_field",
    )(table, *shards)
    gram = pl.pallas_call(
        functools.partial(finish_gram, 1.0 / (row_tiles * side * helpers * rows)),
        out_shape=jax.ShapeDtypeStruct((volumes, 2, vectors, vectors), jnp.float32),
        in_specs=[VMEM],
        out_specs=VMEM,
        compiler_params=params,
        name="finish_gram",
    )(parts)
    return filtered, gram


def solution(mesh):
    placed = (
        P(None, ("rows", "help")),
        P(None, ("rows", "help"), None, None, None),
        P(("rows", "help"), None),
        P(("rows", "help")),
        P("rows"),
        P("rows", None, None),
        P(),
        P(),
    )
    return jax.shard_map(
        per_device,
        mesh=mesh,
        in_specs=placed,
        out_specs=(P(None, None, ("rows", "help")), P()),
        check_vma=False,
    )
```

time: 76.7 us -> 74.3 us (0.969)
  blocking collectives: 18.4 us -> 0 us
  starting transfers between devices: 25.1 us -> 36.9 us
  waiting for transfers between devices: 12.9 us -> 19.5 us
  Pallas kernels: 13.5 us -> 10.4 us
    all_to_all x1 -> x0, blocking collectives: 18.4 us -> none  [summed_parts(): lax.all_to_all(parts, ('rows', 'help'), 0, 0, axis_index_groups=groups)]
    all_to_all x1 -> x2, starting transfers between devices: 3.81 us -> 13.9 us  [summed_parts(): lax.all_to_all(parts, ('rows', 'help'), 0, 0, axis_index_groups=groups)]
    ppermute x6 -> x9, waiting for transfers between devices: 3.81 us -> 9.02 us  [gathered(): lax.ppermute(shard, 'help', [(i, i ^ d) for i in range(helpers)])]
    ppermute x6 -> x9, starting transfers between devices: 7.85 us -> 11.6 us  [gathered(): lax.ppermute(shard, 'help', [(i, i ^ d) for i in range(helpers)])]
    ppermute x2 -> x0, starting transfers between devices: 2.11 us -> none  [the longest x1 1.37 us: per_device(): lax.ppermute(second, 'help', [(i, i ^ 1) for i in range(helpers)])]
    pallas_call x3 -> x4, Pallas kernels: 8.9 us -> 7.63 us  [the longest x1 3.44 us: per_device(): pl.pallas_call(near_first, out_shape=[part_shape, shape(row_tiles, vector...]
    all_to_all x1 -> x2, waiting for transfers between devices: 5.47 us -> 6.11 us  [summed_parts(): lax.all_to_all(parts, ('rows', 'help'), 0, 0, axis_index_groups=groups)]
  transfers between devices with their start and end apart: 13 -> 15, of which waited for: 6 -> 9; matrix products, arithmetic and copies ran while one was open for 0% -> 0% of each run, Pallas kernels for 10% -> 9%
where the time goes in v4:
time: 74.3 us; the launch traced here: 74 us
  starting transfers between devices  36.9 us (50%)
  waiting for transfers between devices  19.5 us (26%)
  Pallas kernels  10.4 us (14%)
  local copies, waits for them, and re-layouts  6.31 us (8%)
  between operations  0.79 us (1%)
    all_to_all x2, starting transfers between devices, summed_parts(): lax.all_to_all(parts, ('rows', 'help'), 0, 0, axis_index_groups=groups)  13.9 us
    ppermute x9, starting transfers between devices, gathered(): lax.ppermute(shard, 'help', [(i, i ^ d) for i in range(helpers)])  11.6 us
    ppermute x2, starting transfers between devices, exchanged(): pair = lax.ppermute(to_pair, 'rows', [(s, s ^ 1) for s in range(rows)])  11.3 us
    ppermute x9, waiting for transfers between devices, gathered(): lax.ppermute(shard, 'help', [(i, i ^ d) for i in range(helpers)])  9.02 us
    all_to_all x2, waiting for transfers between devices, summed_parts(): lax.all_to_all(parts, ('rows', 'help'), 0, 0, axis_index_groups=groups)  6.11 us
    unnamed x18, local copies, waits for them, and re-layouts  4.88 us
    pallas_call x1, Pallas kernels, per_device(): pl.pallas_call(near_first, out_shape=[part_shape, shape(row_tiles, vector...  3.44 us
    pallas_call x1, Pallas kernels, per_device(): pl.pallas_call(near_second, out_shape=part_shape, in_specs=[VMEM] * 4, ou...  2.56 us
  transfers between devices with their start and end apart: 15, of which 9 were waited for; matrix products, arithmetic and copies ran while one was open for 0% of the time, Pallas kernels for 9%

profile of v4, /device:TPU:1, one launch (start us, length us, event | category | flops | bytes accessed | tf_op | source)
XLA Modules:
  0.0 74.0 jit_solution(16777891766813899734)
XLA Ops:
  0.6 2.1 %collective-permute-start = (bf16[32,1024]{1,0:T(8,128)(2,1)}, bf16[32,1024]{1,0:T(8,128)(2,1)S(1)}, u32[]{:S(2)}, u32[]{:S(2)}) collective-permute-start(bf16[32,1024]{1,0:T(8,128)(2,1)} %panel.1), channel_id=1, source_target_pairs={{0,1},{1,0},{2,3},{3,2},{4,5},{5,4},{6,7},{7,6},{8,9},{9,8},{10,11... | collective-permute-start | bytes 196616 | tf_op jit(solution)/shard_map/ppermute | solution.py:260
  2.8 1.8 %collective-permute-start.2 = (bf16[32,1024]{1,0:T(8,128)(2,1)}, bf16[32,1024]{1,0:T(8,128)(2,1)S(1)}, u32[]{:S(2)}, u32[]{:S(2)}) collective-permute-start(bf16[32,1024]{1,0:T(8,128)(2,1)} %panel.1), channel_id=1, source_target_pairs={{0,3},{1,2},{2,1},{3,0},{4,7},{5,6},{6,5},{7,4},{8,11},{9,10},{10,... | collective-permute-start | bytes 196616 | tf_op jit(solution)/shard_map/ppermute | solution.py:260
  4.6 0.6 collective-permute-start.1
  5.2 0.0 copy-start
  5.2 3.4 %copy-done = bf16[2,8,16,128,128]{4,3,2,1,0:T(8,128)(2,1)S(1)} copy-done((bf16[2,8,16,128,128]{4,3,2,1,0:T(8,128)(2,1)S(1)}, bf16[2,8,16,128,128]{4,3,2,1,0:T(8,128)(2,1)}, u32[]{:S(2)}) %copy-start) | copy-done | bytes 8388632
  8.6 0.0 copy-start.2
  8.6 0.8 %copy-done.2 = bf16[32,1024]{1,0:T(8,128)(2,1)S(1)} copy-done((bf16[32,1024]{1,0:T(8,128)(2,1)S(1)}, bf16[32,1024]{1,0:T(8,128)(2,1)}, u32[]{:S(2)}) %copy-start.2) | copy-done | bytes 65560
  9.4 0.0 copy-start.3
  9.4 0.0 copy-start.4
  9.4 0.0 copy-start.5
  9.4 0.0 copy-start.6
  9.4 0.0 copy-start.7
  9.5 0.0 copy-start.8
  9.5 0.0 copy-start.1
  9.5 0.6 copy-done.3
  10.1 0.0 copy-done.4
  10.1 0.0 copy-done.5
  10.1 0.0 copy-done.6
  10.2 0.0 collective-permute-done.refs_1_
  10.2 0.0 collective-permute-done.2.refs_3_
  10.2 0.0 collective-permute-done.1.refs_2_
  10.2 0.2 spread_panel.1
  10.4 2.9 %collective-permute-start.3 = (bf16[16,32,128]{2,1,0:T(8,128)(2,1)S(1)}, bf16[16,32,128]{2,1,0:T(8,128)(2,1)S(1)}, u32[]{:S(2)}, u32[]{:S(2)}) collective-permute-start(bf16[16,32,128]{2,1,0:T(8,128)(2,1)S(1)} %get-tuple-element.19), channel_id=1, source_target_pairs={{0,4},{4,0},{8,12},{12,8},{16,20},{20,16},{24,28},{28,24},{32,36},... | collective-permute-start | bytes 393224 | tf_op jit(solution)/shard_map/ppermute | solution.py:267
  13.3 0.0 collective-permute-start.4
  13.4 0.0 copy-done.7
  13.4 0.0 copy-done.8
  13.4 0.1 pad_maximum_fusion
  13.4 0.9 %collective-permute-done.3.pair = bf16[16,32,128]{2,1,0:T(8,128)(2,1)S(1)} collective-permute-done((bf16[16,32,128]{2,1,0:T(8,128)(2,1)S(1)}, bf16[16,32,128]{2,1,0:T(8,128)(2,1)S(1)}, u32[]{:S(2)}, u32[]{:S(2)}) %collective-permute-start.3) | collective-permute-done | bytes 131104 | tf_op jit(solution)/shard_map/ppermute | solution.py:267
  14.3 0.0 copy-done.1
  14.3 3.4 %near_first.1 = (f32[2,8,32,128]{3,2,1,0:T(8,128)S(1)}, bf16[8,32,128]{2,1,0:T(8,128)(2,1)S(1)}, s32[5,128]{1,0:T(8,128)S(1)}) custom-call(s32[12,128]{1,0:T(8,128)S(1)} %pad_add_fusion.ints, bf16[32,32,128]{2,1,0:T(8,128)(2,1)S(1)} %get-tuple-element.18.slab, bf16[16,32,128]{2,1,0:T(8,128)(2,1)S(1)} %collective-permute-done.3.pair, ...), custom_call_target="tpu_custom_call" | custom-call | flops 536870912 | bytes 8388608 | tf_op jit(solution)/shard_map/near_first/pallas_call | solution.py:306
  17.7 0.0 collective-permute-done.4.cross
  17.8 0.1 broadcast_in_dim.12.coefs
  17.8 1.1 %apply_first.1 = (bf16[2,8,32,128]{3,2,1,0:T(8,128)(2,1)S(1)}, f32[2,32,32]{2,1,0:T(8,128)S(1)}) custom-call(f32[4,128]{1,0:T(4,128)S(1)} %broadcast_in_dim.12.coefs, s32[5,128]{1,0:T(8,128)S(1)} %get-tuple-element.20.table, bf16[8,32,128]{2,1,0:T(8,128)(2,1)S(1)} %get-tuple-element.21.stored, bf16[16,32,128]{2,1,0:T(8,128)(2,1)S(1)} %collective-permute-done.4.cross, ...), custom_call_target="tpu_custom_call" | custom-call | tf_op jit(solution)/shard_map/apply_first/pallas_call | solution.py:324
  19.0 1.4 %collective-permute-start.7 = (bf16[2,8,32,128]{3,2,1,0:T(8,128)(2,1)S(1)}, bf16[2,8,32,128]{3,2,1,0:T(8,128)(2,1)S(1)}, u32[]{:S(2)}, u32[]{:S(2)}) collective-permute-start(bf16[2,8,32,128]{3,2,1,0:T(8,128)(2,1)S(1)} %get-tuple-element.24.refs_0_.first), channel_id=1, source_target_pairs={{0,3},{1,2},{2,1},{3,0},{4,7},{5,6},{6,5},{7,4},{8,11},{9,10},{10,... | collective-permute-start | bytes 393224 | tf_op jit(solution)/shard_map/ppermute | solution.py:260
  20.4 0.2 collective-permute-start.6
  20.6 1.6 %collective-permute-start.5 = (bf16[2,8,32,128]{3,2,1,0:T(8,128)(2,1)S(1)}, bf16[2,8,32,128]{3,2,1,0:T(8,128)(2,1)S(1)}, u32[]{:S(2)}, u32[]{:S(2)}) collective-permute-start(bf16[2,8,32,128]{3,2,1,0:T(8,128)(2,1)S(1)} %get-tuple-element.24.refs_0_.first), channel_id=1, source_target_pairs={{0,1},{1,0},{2,3},{3,2},{4,5},{5,4},{6,7},{7,6},{8,9},{9,8},{10,11... | collective-permute-start | bytes 393224 | tf_op jit(solution)/shard_map/ppermute | solution.py:260
  22.2 1.8 %collective-permute-done.7.refs_3_ = bf16[2,8,32,128]{3,2,1,0:T(8,128)(2,1)S(1)} collective-permute-done((bf16[2,8,32,128]{3,2,1,0:T(8,128)(2,1)S(1)}, bf16[2,8,32,128]{3,2,1,0:T(8,128)(2,1)S(1)}, u32[]{:S(2)}, u32[]{:S(2)}) %collective-permute-start.7) | collective-permute-done | bytes 131104 | tf_op jit(solution)/shard_map/ppermute | solution.py:260
  24.0 1.7 %collective-permute-done.6.refs_2_ = bf16[2,8,32,128]{3,2,1,0:T(8,128)(2,1)S(1)} collective-permute-done((bf16[2,8,32,128]{3,2,1,0:T(8,128)(2,1)S(1)}, bf16[2,8,32,128]{3,2,1,0:T(8,128)(2,1)S(1)}, u32[]{:S(2)}, u32[]{:S(2)}) %collective-permute-start.6) | collective-permute-done | bytes 131104 | tf_op jit(solution)/shard_map/ppermute | solution.py:260
  25.7 0.3 collective-permute-done.5.refs_1_
  26.0 0.1 spread_field.1
  26.1 8.4 %collective-permute-start.9 = (bf16[2,16,32,128]{3,2,1,0:T(8,128)(2,1)S(1)}, bf16[2,16,32,128]{3,2,1,0:T(8,128)(2,1)S(1)}, u32[]{:S(2)}, u32[]{:S(2)}) collective-permute-start(bf16[2,16,32,128]{3,2,1,0:T(8,128)(2,1)S(1)} %get-tuple-element.27), channel_id=1, source_target_pairs={{0,4},{4,0},{8,12},{12,8},{16,20},{20,16},{24,28},{28,24},{32,36},... | collective-permute-start | bytes 786440 | tf_op jit(solution)/shard_map/ppermute | solution.py:267
  34.5 0.0 collective-permute-start.8
  34.5 1.2 %collective-permute-done.9.pair = bf16[2,16,32,128]{3,2,1,0:T(8,128)(2,1)S(1)} collective-permute-done((bf16[2,16,32,128]{3,2,1,0:T(8,128)(2,1)S(1)}, bf16[2,16,32,128]{3,2,1,0:T(8,128)(2,1)S(1)}, u32[]{:S(2)}, u32[]{:S(2)}) %collective-permute-start.9) | collective-permute-done | bytes 262176 | tf_op jit(solution)/shard_map/ppermute | solution.py:267
  35.7 2.6 %near_second.1.part = f32[2,8,32,128]{3,2,1,0:T(8,128)S(1)} custom-call(s32[12,128]{1,0:T(8,128)S(1)} %pad_add_fusion.ints, bf16[2,32,32,128]{3,2,1,0:T(8,128)(2,1)S(1)} %get-tuple-element.26.slab, bf16[2,16,32,128]{3,2,1,0:T(8,128)(2,1)S(1)} %collective-permute-done.9.pair, bf16[2,8,16,128,128]{4,3,2,1,0:T(8,128)(2,1)S(1)} %copy-done.1), custom_call_target="tpu_custom_call" | custom-call | flops 536870912 | bytes 8388608 | tf_op jit(solution)/shard_map/near_second/pallas_call | solution.py:345
  38.3 2.4 %collective-permute-done.8.cross = bf16[2,16,32,128]{3,2,1,0:T(8,128)(2,1)S(1)} collective-permute-done((bf16[2,16,32,128]{3,2,1,0:T(8,128)(2,1)S(1)}, bf16[2,16,32,128]{3,2,1,0:T(8,128)(2,1)S(1)}, u32[]{:S(2)}, u32[]{:S(2)}) %collective-permute-start.8) | collective-permute-done | bytes 262176 | tf_op jit(solution)/shard_map/ppermute | solution.py:266
  40.6 1.3 %apply_second.1 = (bf16[2,8,32,128]{3,2,1,0:T(8,128)(2,1)S(1)}, f32[32,128]{1,0:T(8,128)S(1)}) custom-call(f32[4,128]{1,0:T(4,128)S(1)} %broadcast_in_dim.12.coefs, s32[5,128]{1,0:T(8,128)S(1)} %get-tuple-element.20.table, bf16[8,32,128]{2,1,0:T(8,128)(2,1)S(1)} %get-tuple-element.21.stored, bf16[2,16,32,128]{3,2,1,0:T(8,128)(2,1)S(1)} %collective-permute-done.8.cross, ...), custom_call_target="tpu_custom_call" | custom-call | tf_op jit(solution)/shard_map/apply_second/pallas_call | solution.py:355
  42.0 0.7 broadcast_in_dim.13
  42.6 3.7 %all-to-all-start = ((bf16[16,32,128]{2,1,0:T(8,128)(2,1)}), bf16[16,32,128]{2,1,0:T(8,128)(2,1)S(1)}, u32[]{:S(2)}, u32[]{:S(2)}) async-start(bf16[16,32,128]{2,1,0:T(8,128)(2,1)} %broadcast_in_dim.13), calls=%async_computation | async-start | bytes 262144 | tf_op jit(solution)/shard_map/all_to_all | solution.py:239
  46.3 2.6 %collective-permute-start.11 = (bf16[2,8,32,128]{3,2,1,0:T(8,128)(2,1)S(1)}, bf16[2,8,32,128]{3,2,1,0:T(8,128)(2,1)S(1)}, u32[]{:S(2)}, u32[]{:S(2)}) collective-permute-start(bf16[2,8,32,128]{3,2,1,0:T(8,128)(2,1)S(1)} %get-tuple-element.29.refs_0_), channel_id=1, source_target_pairs={{0,3},{1,2},{2,1},{3,0},{4,7},{5,6},{6,5},{7,4},{8,11},{9,10},{10,... | collective-permute-start | bytes 393224 | tf_op jit(solution)/shard_map/ppermute | solution.py:260
  48.9 0.0 collective-permute-start.10
  48.9 4.3 %all-to-all-done = bf16[16,32,128]{2,1,0:T(8,128)(2,1)S(1)} async-done(((bf16[16,32,128]{2,1,0:T(8,128)(2,1)}), bf16[16,32,128]{2,1,0:T(8,128)(2,1)S(1)}, u32[]{:S(2)}, u32[]{:S(2)}) %all-to-all-start) | async-done | bytes 131104 | tf_op jit(solution)/shard_map/all_to_all | solution.py:239
  53.2 0.0 collective-permute-done.11.refs_3_
  53.2 0.0 collective-permute-done.10.refs_1_
  53.2 0.7 broadcast_in_dim.28
  53.9 10.2 %all-to-all-start.1 = ((bf16[16,32,128]{2,1,0:T(8,128)(2,1)}), bf16[16,32,128]{2,1,0:T(8,128)(2,1)S(1)}, u32[]{:S(2)}, u32[]{:S(2)}) async-start(bf16[16,32,128]{2,1,0:T(8,128)(2,1)} %broadcast_in_dim.28), calls=%async_computation.1 | async-start | bytes 262144 | tf_op jit(solution)/shard_map/all_to_all | solution.py:239
  64.1 1.2 %collective-permute-start.12 = (bf16[2,8,32,128]{3,2,1,0:T(8,128)(2,1)S(1)}, bf16[2,8,32,128]{3,2,1,0:T(8,128)(2,1)S(1)}, u32[]{:S(2)}, u32[]{:S(2)}) collective-permute-start(bf16[2,8,32,128]{3,2,1,0:T(8,128)(2,1)S(1)} %get-tuple-element.29.refs_0_), channel_id=1, source_target_pairs={{0,2},{1,3},{2,0},{3,1},{4,6},{5,7},{6,4},{7,5},{8,10},{9,11},{10,... | collective-permute-start | bytes 393224 | tf_op jit(solution)/shard_map/ppermute | solution.py:260
  65.3 5.2 %collective-permute-done.12.refs_2_ = bf16[2,8,32,128]{3,2,1,0:T(8,128)(2,1)S(1)} collective-permute-done((bf16[2,8,32,128]{3,2,1,0:T(8,128)(2,1)S(1)}, bf16[2,8,32,128]{3,2,1,0:T(8,128)(2,1)S(1)}, u32[]{:S(2)}, u32[]{:S(2)}) %collective-permute-start.12) | collective-permute-done | bytes 131104 | tf_op jit(solution)/shard_map/ppermute | solution.py:260
  70.6 0.9 %place_field.1 = bf16[2,32,1024]{2,1,0:T(8,128)(2,1)} custom-call(s32[5,128]{1,0:T(8,128)S(1)} %get-tuple-element.20.table, bf16[2,8,32,128]{3,2,1,0:T(8,128)(2,1)S(1)} %get-tuple-element.29.refs_0_, bf16[2,8,32,128]{3,2,1,0:T(8,128)(2,1)S(1)} %collective-permute-done.10.refs_1_, bf16[2,8,32,128]{3,2,1,0:T(8,128)(2,1)S(1)} %collective-permute-done.12.refs_2_, ...), custom_call_target="tpu_custom_call" | custom-call | tf_op jit(solution)/shard_map/place_field/pallas_call | solution.py:382
  71.4 1.8 %all-to-all-done.1.parts = bf16[16,32,128]{2,1,0:T(8,128)(2,1)S(1)} async-done(((bf16[16,32,128]{2,1,0:T(8,128)(2,1)}), bf16[16,32,128]{2,1,0:T(8,128)(2,1)S(1)}, u32[]{:S(2)}, u32[]{:S(2)}) %all-to-all-start.1) | async-done | bytes 131104 | tf_op jit(solution)/shard_map/all_to_all | solution.py:239
  73.3 0.7 finish_gram.1
  (4 shorter events, 0.1 us)
Async XLA Ops:
  0.6 9.5 %collective-permute-start = (bf16[32,1024]{1,0:T(8,128)(2,1)}, bf16[32,1024]{1,0:T(8,128)(2,1)S(1)}, u32[]{:S(2)}, u32[]{:S(2)}) collective-permute-start(bf16[32,1024]{1,0:T(8,128)(2,1)} %panel.1), channel_id=1, source_target_pairs={{0,1},{1,0},{2,3},{3,2},{4,5},{5,4},{6,7},{7,6},{8,9},{9,8},{10,11... | collective-permute-start | bytes 196616 | tf_op jit(solution)/shard_map/ppermute | solution.py:260
  2.8 7.4 %collective-permute-start.2 = (bf16[32,1024]{1,0:T(8,128)(2,1)}, bf16[32,1024]{1,0:T(8,128)(2,1)S(1)}, u32[]{:S(2)}, u32[]{:S(2)}) collective-permute-start(bf16[32,1024]{1,0:T(8,128)(2,1)} %panel.1), channel_id=1, source_target_pairs={{0,3},{1,2},{2,1},{3,0},{4,7},{5,6},{6,5},{7,4},{8,11},{9,10},{10,... | collective-permute-start | bytes 196616 | tf_op jit(solution)/shard_map/ppermute | solution.py:260
  4.6 5.6 %collective-permute-start.1 = (bf16[32,1024]{1,0:T(8,128)(2,1)}, bf16[32,1024]{1,0:T(8,128)(2,1)S(1)}, u32[]{:S(2)}, u32[]{:S(2)}) collective-permute-start(bf16[32,1024]{1,0:T(8,128)(2,1)} %panel.1), channel_id=1, source_target_pairs={{0,2},{1,3},{2,0},{3,1},{4,6},{5,7},{6,4},{7,5},{8,10},{9,11},{10,... | collective-permute-start | bytes 196616 | tf_op jit(solution)/shard_map/ppermute | solution.py:260
  5.2 3.4 %copy-start = (bf16[2,8,16,128,128]{4,3,2,1,0:T(8,128)(2,1)S(1)}, bf16[2,8,16,128,128]{4,3,2,1,0:T(8,128)(2,1)}, u32[]{:S(2)}) copy-start(bf16[2,8,16,128,128]{4,3,2,1,0:T(8,128)(2,1)} %tiles.9) | copy-start | bytes 25165828
  8.6 0.8 %copy-start.2 = (bf16[32,1024]{1,0:T(8,128)(2,1)S(1)}, bf16[32,1024]{1,0:T(8,128)(2,1)}, u32[]{:S(2)}) copy-start(bf16[32,1024]{1,0:T(8,128)(2,1)} %panel.1) | copy-start | bytes 196612
  9.4 0.7 copy-start.3
  9.4 0.7 copy-start.4
  9.4 0.7 copy-start.5
  9.4 0.7 copy-start.6
  9.4 3.9 %copy-start.7 = (f32[2]{0:T(128)S(1)}, f32[2]{0:T(128)}, u32[]{:S(2)}) copy-start(f32[2]{0:T(128)} %param.15) | copy-start | bytes 28
  9.5 3.9 %copy-start.8 = (f32[2]{0:T(128)S(1)}, f32[2]{0:T(128)}, u32[]{:S(2)}) copy-start(f32[2]{0:T(128)} %param.14) | copy-start | bytes 28
  9.5 4.8 %copy-start.1 = (bf16[2,8,16,128,128]{4,3,2,1,0:T(8,128)(2,1)S(1)}, bf16[2,8,16,128,128]{4,3,2,1,0:T(8,128)(2,1)}, u32[]{:S(2)}) copy-start(bf16[2,8,16,128,128]{4,3,2,1,0:T(8,128)(2,1)} %tiles.9) | copy-start | bytes 25165828
  10.4 3.9 %collective-permute-start.3 = (bf16[16,32,128]{2,1,0:T(8,128)(2,1)S(1)}, bf16[16,32,128]{2,1,0:T(8,128)(2,1)S(1)}, u32[]{:S(2)}, u32[]{:S(2)}) collective-permute-start(bf16[16,32,128]{2,1,0:T(8,128)(2,1)S(1)} %get-tuple-element.19), channel_id=1, source_target_pairs={{0,4},{4,0},{8,12},{12,8},{16,20},{20,16},{24,28},{28,24},{32,36},... | collective-permute-start | bytes 393224 | tf_op jit(solution)/shard_map/ppermute | solution.py:267
  13.3 4.4 %collective-permute-start.4 = (bf16[16,32,128]{2,1,0:T(8,128)(2,1)S(1)}, bf16[16,32,128]{2,1,0:T(8,128)(2,1)S(1)}, u32[]{:S(2)}, u32[]{:S(2)}) collective-permute-start(bf16[16,32,128]{2,1,0:T(8,128)(2,1)S(1)} %get-tuple-element.22), channel_id=1, source_target_pairs={{0,252},{4,8},{8,4},{12,16},{16,12},{20,24},{24,20},{28,32},{32,28... | collective-permute-start | bytes 393224 | tf_op jit(solution)/shard_map/ppermute | solution.py:266
  19.0 5.0 %collective-permute-start.7 = (bf16[2,8,32,128]{3,2,1,0:T(8,128)(2,1)S(1)}, bf16[2,8,32,128]{3,2,1,0:T(8,128)(2,1)S(1)}, u32[]{:S(2)}, u32[]{:S(2)}) collective-permute-start(bf16[2,8,32,128]{3,2,1,0:T(8,128)(2,1)S(1)} %get-tuple-element.24.refs_0_.first), channel_id=1, source_target_pairs={{0,3},{1,2},{2,1},{3,0},{4,7},{5,6},{6,5},{7,4},{8,11},{9,10},{10,... | collective-permute-start | bytes 393224 | tf_op jit(solution)/shard_map/ppermute | solution.py:260
  20.4 5.3 %collective-permute-start.6 = (bf16[2,8,32,128]{3,2,1,0:T(8,128)(2,1)S(1)}, bf16[2,8,32,128]{3,2,1,0:T(8,128)(2,1)S(1)}, u32[]{:S(2)}, u32[]{:S(2)}) collective-permute-start(bf16[2,8,32,128]{3,2,1,0:T(8,128)(2,1)S(1)} %get-tuple-element.24.refs_0_.first), channel_id=1, source_target_pairs={{0,2},{1,3},{2,0},{3,1},{4,6},{5,7},{6,4},{7,5},{8,10},{9,11},{10,... | collective-permute-start | bytes 393224 | tf_op jit(solution)/shard_map/ppermute | solution.py:260
  20.6 5.4 %collective-permute-start.5 = (bf16[2,8,32,128]{3,2,1,0:T(8,128)(2,1)S(1)}, bf16[2,8,32,128]{3,2,1,0:T(8,128)(2,1)S(1)}, u32[]{:S(2)}, u32[]{:S(2)}) collective-permute-start(bf16[2,8,32,128]{3,2,1,0:T(8,128)(2,1)S(1)} %get-tuple-element.24.refs_0_.first), channel_id=1, source_target_pairs={{0,1},{1,0},{2,3},{3,2},{4,5},{5,4},{6,7},{7,6},{8,9},{9,8},{10,11... | collective-permute-start | bytes 393224 | tf_op jit(solution)/shard_map/ppermute | solution.py:260
  26.1 9.5 %collective-permute-start.9 = (bf16[2,16,32,128]{3,2,1,0:T(8,128)(2,1)S(1)}, bf16[2,16,32,128]{3,2,1,0:T(8,128)(2,1)S(1)}, u32[]{:S(2)}, u32[]{:S(2)}) collective-permute-start(bf16[2,16,32,128]{3,2,1,0:T(8,128)(2,1)S(1)} %get-tuple-element.27), channel_id=1, source_target_pairs={{0,4},{4,0},{8,12},{12,8},{16,20},{20,16},{24,28},{28,24},{32,36},... | collective-permute-start | bytes 786440 | tf_op jit(solution)/shard_map/ppermute | solution.py:267
  34.5 6.1 %collective-permute-start.8 = (bf16[2,16,32,128]{3,2,1,0:T(8,128)(2,1)S(1)}, bf16[2,16,32,128]{3,2,1,0:T(8,128)(2,1)S(1)}, u32[]{:S(2)}, u32[]{:S(2)}) collective-permute-start(bf16[2,16,32,128]{3,2,1,0:T(8,128)(2,1)S(1)} %get-tuple-element.25), channel_id=1, source_target_pairs={{0,252},{4,8},{8,4},{12,16},{16,12},{20,24},{24,20},{28,32},{32,28... | collective-permute-start | bytes 786440 | tf_op jit(solution)/shard_map/ppermute | solution.py:266
  42.6 10.5 %all-to-all-start = ((bf16[16,32,128]{2,1,0:T(8,128)(2,1)}), bf16[16,32,128]{2,1,0:T(8,128)(2,1)S(1)}, u32[]{:S(2)}, u32[]{:S(2)}) async-start(bf16[16,32,128]{2,1,0:T(8,128)(2,1)} %broadcast_in_dim.13), calls=%async_computation | async-start | bytes 262144 | tf_op jit(solution)/shard_map/all_to_all | solution.py:239
  46.3 6.9 %collective-permute-start.11 = (bf16[2,8,32,128]{3,2,1,0:T(8,128)(2,1)S(1)}, bf16[2,8,32,128]{3,2,1,0:T(8,128)(2,1)S(1)}, u32[]{:S(2)}, u32[]{:S(2)}) collective-permute-start(bf16[2,8,32,128]{3,2,1,0:T(8,128)(2,1)S(1)} %get-tuple-element.29.refs_0_), channel_id=1, source_target_pairs={{0,3},{1,2},{2,1},{3,0},{4,7},{5,6},{6,5},{7,4},{8,11},{9,10},{10,... | collective-permute-start | bytes 393224 | tf_op jit(solution)/shard_map/ppermute | solution.py:260
  48.9 4.3 %collective-permute-start.10 = (bf16[2,8,32,128]{3,2,1,0:T(8,128)(2,1)S(1)}, bf16[2,8,32,128]{3,2,1,0:T(8,128)(2,1)S(1)}, u32[]{:S(2)}, u32[]{:S(2)}) collective-permute-start(bf16[2,8,32,128]{3,2,1,0:T(8,128)(2,1)S(1)} %get-tuple-element.29.refs_0_), channel_id=1, source_target_pairs={{0,1},{1,0},{2,3},{3,2},{4,5},{5,4},{6,7},{7,6},{8,9},{9,8},{10,11... | collective-permute-start | bytes 393224 | tf_op jit(solution)/shard_map/ppermute | solution.py:260
  53.9 19.4 %all-to-all-start.1 = ((bf16[16,32,128]{2,1,0:T(8,128)(2,1)}), bf16[16,32,128]{2,1,0:T(8,128)(2,1)S(1)}, u32[]{:S(2)}, u32[]{:S(2)}) async-start(bf16[16,32,128]{2,1,0:T(8,128)(2,1)} %broadcast_in_dim.28), calls=%async_computation.1 | async-start | bytes 262144 | tf_op jit(solution)/shard_map/all_to_all | solution.py:239
  64.1 6.4 %collective-permute-start.12 = (bf16[2,8,32,128]{3,2,1,0:T(8,128)(2,1)S(1)}, bf16[2,8,32,128]{3,2,1,0:T(8,128)(2,1)S(1)}, u32[]{:S(2)}, u32[]{:S(2)}) collective-permute-start(bf16[2,8,32,128]{3,2,1,0:T(8,128)(2,1)S(1)} %get-tuple-element.29.refs_0_), channel_id=1, source_target_pairs={{0,2},{1,3},{2,0},{3,1},{4,6},{5,7},{6,4},{7,5},{8,10},{9,11},{10,... | collective-permute-start | bytes 393224 | tf_op jit(solution)/shard_map/ppermute | solution.py:260

commit v5 on v4

--- a/solution.py
+++ b/solution.py
@@ -58,8 +58,8 @@
         to_pair[:, g] = slab[:, table[2, g]]
 
 
-def place_field(helpers, table, *refs):
-    shards, out = refs[:helpers], refs[helpers]
+def finish(helpers, scale, table, parts, *refs):
+    shards, (out, gram) = refs[:helpers], refs[helpers:]
     me = lax.axis_index("help")
     row_tiles, side = shards[0].shape[1], shards[0].shape[3]
     slots = rolled(table[4:5, :], me * row_tiles)
@@ -71,9 +71,6 @@
         for d in range(1, helpers):
             block = jnp.where(step == d, shards[d][:, held], block)
         out[:, :, j * side:(j + 1) * side] = block
-
-
-def finish_gram(scale, parts, gram):
     volumes, steps, vectors, _ = gram.shape
     total = jnp.sum(parts[...].astype(jnp.float32), axis=0) * scale
     for step in range(steps):
@@ -365,7 +362,6 @@
         name="apply_second",
     )(coefs, table, stored, cross, tiles, part, first, gram_one)
 
-    shards = gathered(second)
     near = [
         [at(z, y, c, x) for y in range(SIDE_CHIPS) for x in range(helpers)]
         for z in range(depth)
@@ -377,24 +373,20 @@
         for x in range(helpers)
     ]
     gram = jnp.sum(summed_parts(gram, near).astype(jnp.float32), axis=0)
-    gram, shards[1], shards[3] = lax.optimization_barrier((gram, shards[1], shards[3]))
+    gram, late = lax.optimization_barrier((gram, second))
+    shards = gathered(late)
     parts = summed_parts(gram, far)
-    filtered = pl.pallas_call(
-        functools.partial(place_field, helpers),
-        out_shape=shape(volumes, vectors, row_tiles * side),
-        in_specs=[VMEM] * (1 + helpers),
-        out_specs=VMEM,
-        compiler_params=params,
-        name="place_field",
-    )(table, *shards)
-    gram = pl.pallas_call(
-        functools.partial(finish_gram, 1.0 / (row_tiles * side * helpers * rows)),
-        out_shape=jax.ShapeDtypeStruct((volumes, 2, vectors, vectors), jnp.float32),
-        in_specs=[VMEM],
-        out_specs=VMEM,
-        compiler_params=params,
-        name="finish_gram",
-    )(parts)
+    filtered, gram = pl.pallas_call(
+        functools.partial(finish, helpers, 1.0 / (row_tiles * side * helpers * rows)),
+        out_shape=[
+            shape(volumes, vectors, row_tiles * side),
+            jax.ShapeDtypeStruct((volumes, 2, vectors, vectors), jnp.float32),
+        ],
+        in_specs=[VMEM] * (2 + helpers),
+        out_specs=[VMEM] * 2,
+        compiler_params=params,
+        name="finish",
+    )(table, parts, *shards)
     return filtered, gram
 
 

time: 74.3 us -> 72.4 us (0.974)
  blocking collectives: 0 us -> 11.5 us
  starting transfers between devices: 36.9 us -> 30.3 us
  waiting for transfers between devices: 19.5 us -> 14.1 us
    all_to_all x0 -> x1, blocking collectives: none -> 11.5 us  [summed_parts(): lax.all_to_all(parts, ('rows', 'help'), 0, 0, axis_index_groups=groups)]
    all_to_all x2 -> x1, waiting for transfers between devices: 6.11 us -> 0.01 us  [summed_parts(): lax.all_to_all(parts, ('rows', 'help'), 0, 0, axis_index_groups=groups)]
    all_to_all x2 -> x1, starting transfers between devices: 13.9 us -> 8.37 us  [summed_parts(): lax.all_to_all(parts, ('rows', 'help'), 0, 0, axis_index_groups=groups)]
    pallas_call x2 -> x1, Pallas kernels: 1.63 us -> 0.93 us  [per_device(): pl.pallas_call(functools.partial(finish, helpers, 1.0 / (row_tiles * side...]
  transfers between devices with their start and end apart: 15 -> 14, of which waited for: 9 -> 8; matrix products, arithmetic and copies ran while one was open for 0% -> 0% of each run, Pallas kernels for 9% -> 8%
where the time goes in v5:
time: 72.4 us; the launch traced here: 72.2 us
  starting transfers between devices  30.3 us (42%)
  waiting for transfers between devices  14.1 us (19%)
  blocking collectives  11.5 us (16%)
  Pallas kernels  9.74 us (13%)
  local copies, waits for them, and re-layouts  5.64 us (8%)
  between operations  0.77 us (1%)
    all_to_all x1, blocking collectives, summed_parts(): lax.all_to_all(parts, ('rows', 'help'), 0, 0, axis_index_groups=groups)  11.5 us
    ppermute x9, starting transfers between devices, gathered(): lax.ppermute(shard, 'help', [(i, i ^ d) for i in range(helpers)])  11.1 us
    ppermute x2, starting transfers between devices, exchanged(): pair = lax.ppermute(to_pair, 'rows', [(s, s ^ 1) for s in range(rows)])  10.7 us
    ppermute x9, waiting for transfers between devices, gathered(): lax.ppermute(shard, 'help', [(i, i ^ d) for i in range(helpers)])  9.75 us
    all_to_all x1, starting transfers between devices, summed_parts(): lax.all_to_all(parts, ('rows', 'help'), 0, 0, axis_index_groups=groups)  8.37 us
    unnamed x18, local copies, waits for them, and re-layouts  4.88 us
    pallas_call x1, Pallas kernels, per_device(): pl.pallas_call(near_first, out_shape=[part_shape, shape(row_tiles, vector...  3.44 us
    pallas_call x1, Pallas kernels, per_device(): pl.pallas_call(near_second, out_shape=part_shape, in_specs=[VMEM] * 4, ou...  2.57 us
  transfers between devices with their start and end apart: 14, of which 8 were waited for; matrix products, arithmetic and copies ran while one was open for 0% of the time, Pallas kernels for 8%

profile of v5, /device:TPU:1, one launch (start us, length us, event | category | flops | bytes accessed | tf_op | source)
XLA Modules:
  0.0 72.2 jit_solution(14179432578200728657)
XLA Ops:
  0.6 2.1 %collective-permute-start = (bf16[32,1024]{1,0:T(8,128)(2,1)}, bf16[32,1024]{1,0:T(8,128)(2,1)S(1)}, u32[]{:S(2)}, u32[]{:S(2)}) collective-permute-start(bf16[32,1024]{1,0:T(8,128)(2,1)} %panel.1), channel_id=1, source_target_pairs={{0,1},{1,0},{2,3},{3,2},{4,5},{5,4},{6,7},{7,6},{8,9},{9,8},{10,11... | collective-permute-start | bytes 196616 | tf_op jit(solution)/shard_map/ppermute | solution.py:257
  2.8 1.8 %collective-permute-start.2 = (bf16[32,1024]{1,0:T(8,128)(2,1)}, bf16[32,1024]{1,0:T(8,128)(2,1)S(1)}, u32[]{:S(2)}, u32[]{:S(2)}) collective-permute-start(bf16[32,1024]{1,0:T(8,128)(2,1)} %panel.1), channel_id=1, source_target_pairs={{0,3},{1,2},{2,1},{3,0},{4,7},{5,6},{6,5},{7,4},{8,11},{9,10},{10,... | collective-permute-start | bytes 196616 | tf_op jit(solution)/shard_map/ppermute | solution.py:257
  4.6 0.6 collective-permute-start.1
  5.2 0.0 copy-start
  5.2 3.4 %copy-done = bf16[2,8,16,128,128]{4,3,2,1,0:T(8,128)(2,1)S(1)} copy-done((bf16[2,8,16,128,128]{4,3,2,1,0:T(8,128)(2,1)S(1)}, bf16[2,8,16,128,128]{4,3,2,1,0:T(8,128)(2,1)}, u32[]{:S(2)}) %copy-start) | copy-done | bytes 8388632
  8.6 0.0 copy-start.2
  8.6 0.8 %copy-done.2 = bf16[32,1024]{1,0:T(8,128)(2,1)S(1)} copy-done((bf16[32,1024]{1,0:T(8,128)(2,1)S(1)}, bf16[32,1024]{1,0:T(8,128)(2,1)}, u32[]{:S(2)}) %copy-start.2) | copy-done | bytes 65560
  9.4 0.0 copy-start.3
  9.4 0.0 copy-start.4
  9.4 0.0 copy-start.5
  9.4 0.0 copy-start.6
  9.4 0.0 copy-start.7
  9.5 0.0 copy-start.8
  9.5 0.0 copy-start.1
  9.5 0.6 copy-done.3
  10.1 0.0 copy-done.4
  10.1 0.0 copy-done.5
  10.1 0.0 copy-done.6
  10.2 0.0 collective-permute-done.refs_1_
  10.2 0.0 collective-permute-done.2.refs_3_
  10.2 0.0 collective-permute-done.1.refs_2_
  10.2 0.2 spread_panel.1
  10.4 2.9 %collective-permute-start.3 = (bf16[16,32,128]{2,1,0:T(8,128)(2,1)S(1)}, bf16[16,32,128]{2,1,0:T(8,128)(2,1)S(1)}, u32[]{:S(2)}, u32[]{:S(2)}) collective-permute-start(bf16[16,32,128]{2,1,0:T(8,128)(2,1)S(1)} %get-tuple-element.18), channel_id=1, source_target_pairs={{0,4},{4,0},{8,12},{12,8},{16,20},{20,16},{24,28},{28,24},{32,36},... | collective-permute-start | bytes 393224 | tf_op jit(solution)/shard_map/ppermute | solution.py:264
  13.3 0.0 collective-permute-start.4
  13.4 0.0 copy-done.7
  13.4 0.0 copy-done.8
  13.4 0.1 pad_maximum_fusion
  13.4 0.9 %collective-permute-done.3.pair = bf16[16,32,128]{2,1,0:T(8,128)(2,1)S(1)} collective-permute-done((bf16[16,32,128]{2,1,0:T(8,128)(2,1)S(1)}, bf16[16,32,128]{2,1,0:T(8,128)(2,1)S(1)}, u32[]{:S(2)}, u32[]{:S(2)}) %collective-permute-start.3) | collective-permute-done | bytes 131104 | tf_op jit(solution)/shard_map/ppermute | solution.py:264
  14.3 0.0 copy-done.1
  14.3 3.4 %near_first.1 = (f32[2,8,32,128]{3,2,1,0:T(8,128)S(1)}, bf16[8,32,128]{2,1,0:T(8,128)(2,1)S(1)}, s32[5,128]{1,0:T(8,128)S(1)}) custom-call(s32[12,128]{1,0:T(8,128)S(1)} %pad_add_fusion.ints, bf16[32,32,128]{2,1,0:T(8,128)(2,1)S(1)} %get-tuple-element.17.slab, bf16[16,32,128]{2,1,0:T(8,128)(2,1)S(1)} %collective-permute-done.3.pair, ...), custom_call_target="tpu_custom_call" | custom-call | flops 536870912 | bytes 8388608 | tf_op jit(solution)/shard_map/near_first/pallas_call | solution.py:303
  17.7 0.0 collective-permute-done.4.cross
  17.8 0.1 broadcast_in_dim.12.coefs
  17.8 1.1 %apply_first.1 = (bf16[2,8,32,128]{3,2,1,0:T(8,128)(2,1)S(1)}, f32[2,32,32]{2,1,0:T(8,128)S(1)}) custom-call(f32[4,128]{1,0:T(4,128)S(1)} %broadcast_in_dim.12.coefs, s32[5,128]{1,0:T(8,128)S(1)} %get-tuple-element.19.table, bf16[8,32,128]{2,1,0:T(8,128)(2,1)S(1)} %get-tuple-element.20.stored, bf16[16,32,128]{2,1,0:T(8,128)(2,1)S(1)} %collective-permute-done.4.cross, ...), custom_call_target="tpu_custom_call" | custom-call | tf_op jit(solution)/shard_map/apply_first/pallas_call | solution.py:321
  19.0 1.1 %collective-permute-start.7 = (bf16[2,8,32,128]{3,2,1,0:T(8,128)(2,1)S(1)}, bf16[2,8,32,128]{3,2,1,0:T(8,128)(2,1)S(1)}, u32[]{:S(2)}, u32[]{:S(2)}) collective-permute-start(bf16[2,8,32,128]{3,2,1,0:T(8,128)(2,1)S(1)} %get-tuple-element.23.refs_0_.first), channel_id=1, source_target_pairs={{0,3},{1,2},{2,1},{3,0},{4,7},{5,6},{6,5},{7,4},{8,11},{9,10},{10,... | collective-permute-start | bytes 393224 | tf_op jit(solution)/shard_map/ppermute | solution.py:257
  20.1 0.5 collective-permute-start.6
  20.6 1.6 %collective-permute-start.5 = (bf16[2,8,32,128]{3,2,1,0:T(8,128)(2,1)S(1)}, bf16[2,8,32,128]{3,2,1,0:T(8,128)(2,1)S(1)}, u32[]{:S(2)}, u32[]{:S(2)}) collective-permute-start(bf16[2,8,32,128]{3,2,1,0:T(8,128)(2,1)S(1)} %get-tuple-element.23.refs_0_.first), channel_id=1, source_target_pairs={{0,1},{1,0},{2,3},{3,2},{4,5},{5,4},{6,7},{7,6},{8,9},{9,8},{10,11... | collective-permute-start | bytes 393224 | tf_op jit(solution)/shard_map/ppermute | solution.py:257
  22.2 1.8 %collective-permute-done.7.refs_3_ = bf16[2,8,32,128]{3,2,1,0:T(8,128)(2,1)S(1)} collective-permute-done((bf16[2,8,32,128]{3,2,1,0:T(8,128)(2,1)S(1)}, bf16[2,8,32,128]{3,2,1,0:T(8,128)(2,1)S(1)}, u32[]{:S(2)}, u32[]{:S(2)}) %collective-permute-start.7) | collective-permute-done | bytes 131104 | tf_op jit(solution)/shard_map/ppermute | solution.py:257
  24.0 1.4 %collective-permute-done.6.refs_2_ = bf16[2,8,32,128]{3,2,1,0:T(8,128)(2,1)S(1)} collective-permute-done((bf16[2,8,32,128]{3,2,1,0:T(8,128)(2,1)S(1)}, bf16[2,8,32,128]{3,2,1,0:T(8,128)(2,1)S(1)}, u32[]{:S(2)}, u32[]{:S(2)}) %collective-permute-start.6) | collective-permute-done | bytes 131104 | tf_op jit(solution)/shard_map/ppermute | solution.py:257
  25.4 0.6 collective-permute-done.5.refs_1_
  26.0 0.1 spread_field.1
  26.1 7.8 %collective-permute-start.9 = (bf16[2,16,32,128]{3,2,1,0:T(8,128)(2,1)S(1)}, bf16[2,16,32,128]{3,2,1,0:T(8,128)(2,1)S(1)}, u32[]{:S(2)}, u32[]{:S(2)}) collective-permute-start(bf16[2,16,32,128]{3,2,1,0:T(8,128)(2,1)S(1)} %get-tuple-element.26), channel_id=1, source_target_pairs={{0,4},{4,0},{8,12},{12,8},{16,20},{20,16},{24,28},{28,24},{32,36},... | collective-permute-start | bytes 786440 | tf_op jit(solution)/shard_map/ppermute | solution.py:264
  34.0 0.0 collective-permute-start.8
  34.0 1.2 %collective-permute-done.9.pair = bf16[2,16,32,128]{3,2,1,0:T(8,128)(2,1)S(1)} collective-permute-done((bf16[2,16,32,128]{3,2,1,0:T(8,128)(2,1)S(1)}, bf16[2,16,32,128]{3,2,1,0:T(8,128)(2,1)S(1)}, u32[]{:S(2)}, u32[]{:S(2)}) %collective-permute-start.9) | collective-permute-done | bytes 262176 | tf_op jit(solution)/shard_map/ppermute | solution.py:264
  35.1 2.6 %near_second.1.part = f32[2,8,32,128]{3,2,1,0:T(8,128)S(1)} custom-call(s32[12,128]{1,0:T(8,128)S(1)} %pad_add_fusion.ints, bf16[2,32,32,128]{3,2,1,0:T(8,128)(2,1)S(1)} %get-tuple-element.25.slab, bf16[2,16,32,128]{3,2,1,0:T(8,128)(2,1)S(1)} %collective-permute-done.9.pair, bf16[2,8,16,128,128]{4,3,2,1,0:T(8,128)(2,1)S(1)} %copy-done.1), custom_call_target="tpu_custom_call" | custom-call | flops 536870912 | bytes 8388608 | tf_op jit(solution)/shard_map/near_second/pallas_call | solution.py:342
  37.7 2.4 %collective-permute-done.8.cross = bf16[2,16,32,128]{3,2,1,0:T(8,128)(2,1)S(1)} collective-permute-done((bf16[2,16,32,128]{3,2,1,0:T(8,128)(2,1)S(1)}, bf16[2,16,32,128]{3,2,1,0:T(8,128)(2,1)S(1)}, u32[]{:S(2)}, u32[]{:S(2)}) %collective-permute-start.8) | collective-permute-done | bytes 262176 | tf_op jit(solution)/shard_map/ppermute | solution.py:263
  40.1 1.3 %apply_second.1 = (bf16[2,8,32,128]{3,2,1,0:T(8,128)(2,1)S(1)}, f32[32,128]{1,0:T(8,128)S(1)}) custom-call(f32[4,128]{1,0:T(4,128)S(1)} %broadcast_in_dim.12.coefs, s32[5,128]{1,0:T(8,128)S(1)} %get-tuple-element.19.table, bf16[8,32,128]{2,1,0:T(8,128)(2,1)S(1)} %get-tuple-element.20.stored, bf16[2,16,32,128]{3,2,1,0:T(8,128)(2,1)S(1)} %collective-permute-done.8.cross, ...), custom_call_target="tpu_custom_call" | custom-call | tf_op jit(solution)/shard_map/apply_second/pallas_call | solution.py:352
  41.4 11.5 %all_to_all.10 = bf16[16,32,128]{2,1,0:T(8,128)(2,1)S(1)} all-to-all(bf16[16,32,128]{2,1,0:T(8,128)(2,1)S(1)} %broadcast_in_dim.13), channel_id=1, replica_groups={{0,1,2,3,8,9,10,11,16,17,18,19,24,25,26,27},{4,5,6,7,12,13,14,15,20,21,..., dimensions={0} | all-to-all | bytes 262144 | tf_op jit(solution)/shard_map/all_to_all | solution.py:236
  52.9 0.7 broadcast_in_dim.28
  53.6 8.4 %all-to-all-start.1 = ((bf16[16,32,128]{2,1,0:T(8,128)(2,1)}), bf16[16,32,128]{2,1,0:T(8,128)(2,1)S(1)}, u32[]{:S(2)}, u32[]{:S(2)}) async-start(bf16[16,32,128]{2,1,0:T(8,128)(2,1)} %broadcast_in_dim.28), calls=%async_computation.1 | async-start | bytes 262144 | tf_op jit(solution)/shard_map/all_to_all | solution.py:236
  62.0 0.7 collective-permute-start.12
  62.6 1.4 %collective-permute-start.11 = (bf16[2,8,32,128]{3,2,1,0:T(8,128)(2,1)S(1)}, bf16[2,8,32,128]{3,2,1,0:T(8,128)(2,1)S(1)}, u32[]{:S(2)}, u32[]{:S(2)}) collective-permute-start(bf16[2,8,32,128]{3,2,1,0:T(8,128)(2,1)S(1)} %get-tuple-element.31.refs_0_), channel_id=1, source_target_pairs={{0,2},{1,3},{2,0},{3,1},{4,6},{5,7},{6,4},{7,5},{8,10},{9,11},{10,... | collective-permute-start | bytes 393224 | tf_op jit(solution)/shard_map/ppermute | solution.py:257
  64.1 1.2 %collective-permute-start.10 = (bf16[2,8,32,128]{3,2,1,0:T(8,128)(2,1)S(1)}, bf16[2,8,32,128]{3,2,1,0:T(8,128)(2,1)S(1)}, u32[]{:S(2)}, u32[]{:S(2)}) collective-permute-start(bf16[2,8,32,128]{3,2,1,0:T(8,128)(2,1)S(1)} %get-tuple-element.31.refs_0_), channel_id=1, source_target_pairs={{0,1},{1,0},{2,3},{3,2},{4,5},{5,4},{6,7},{7,6},{8,9},{9,8},{10,11... | collective-permute-start | bytes 393224 | tf_op jit(solution)/shard_map/ppermute | solution.py:257
  65.2 5.7 %collective-permute-done.12.refs_3_ = bf16[2,8,32,128]{3,2,1,0:T(8,128)(2,1)S(1)} collective-permute-done((bf16[2,8,32,128]{3,2,1,0:T(8,128)(2,1)S(1)}, bf16[2,8,32,128]{3,2,1,0:T(8,128)(2,1)S(1)}, u32[]{:S(2)}, u32[]{:S(2)}) %collective-permute-start.12) | collective-permute-done | bytes 131104 | tf_op jit(solution)/shard_map/ppermute | solution.py:257
  70.9 0.0 collective-permute-done.11.refs_2_
  70.9 0.3 collective-permute-done.10.refs_1_
  71.2 0.0 all-to-all-done.1.parts
  71.2 0.9 %finish.1 = (bf16[2,32,1024]{2,1,0:T(8,128)(2,1)}, f32[2,2,32,32]{3,2,1,0:T(8,128)}) custom-call(s32[5,128]{1,0:T(8,128)S(1)} %get-tuple-element.19.table, bf16[16,32,128]{2,1,0:T(8,128)(2,1)S(1)} %all-to-all-done.1.parts, bf16[2,8,32,128]{3,2,1,0:T(8,128)(2,1)S(1)} %get-tuple-element.31.refs_0_, ...), custom_call_target="tpu_custom_call" | custom-call | tf_op jit(solution)/shard_map/finish/pallas_call | solution.py:379
  (5 shorter events, 0.1 us)
Async XLA Ops:
  0.6 9.5 %collective-permute-start = (bf16[32,1024]{1,0:T(8,128)(2,1)}, bf16[32,1024]{1,0:T(8,128)(2,1)S(1)}, u32[]{:S(2)}, u32[]{:S(2)}) collective-permute-start(bf16[32,1024]{1,0:T(8,128)(2,1)} %panel.1), channel_id=1, source_target_pairs={{0,1},{1,0},{2,3},{3,2},{4,5},{5,4},{6,7},{7,6},{8,9},{9,8},{10,11... | collective-permute-start | bytes 196616 | tf_op jit(solution)/shard_map/ppermute | solution.py:257
  2.8 7.4 %collective-permute-start.2 = (bf16[32,1024]{1,0:T(8,128)(2,1)}, bf16[32,1024]{1,0:T(8,128)(2,1)S(1)}, u32[]{:S(2)}, u32[]{:S(2)}) collective-permute-start(bf16[32,1024]{1,0:T(8,128)(2,1)} %panel.1), channel_id=1, source_target_pairs={{0,3},{1,2},{2,1},{3,0},{4,7},{5,6},{6,5},{7,4},{8,11},{9,10},{10,... | collective-permute-start | bytes 196616 | tf_op jit(solution)/shard_map/ppermute | solution.py:257
  4.6 5.6 %collective-permute-start.1 = (bf16[32,1024]{1,0:T(8,128)(2,1)}, bf16[32,1024]{1,0:T(8,128)(2,1)S(1)}, u32[]{:S(2)}, u32[]{:S(2)}) collective-permute-start(bf16[32,1024]{1,0:T(8,128)(2,1)} %panel.1), channel_id=1, source_target_pairs={{0,2},{1,3},{2,0},{3,1},{4,6},{5,7},{6,4},{7,5},{8,10},{9,11},{10,... | collective-permute-start | bytes 196616 | tf_op jit(solution)/shard_map/ppermute | solution.py:257
  5.2 3.4 %copy-start = (bf16[2,8,16,128,128]{4,3,2,1,0:T(8,128)(2,1)S(1)}, bf16[2,8,16,128,128]{4,3,2,1,0:T(8,128)(2,1)}, u32[]{:S(2)}) copy-start(bf16[2,8,16,128,128]{4,3,2,1,0:T(8,128)(2,1)} %tiles.9) | copy-start | bytes 25165828
  8.6 0.8 %copy-start.2 = (bf16[32,1024]{1,0:T(8,128)(2,1)S(1)}, bf16[32,1024]{1,0:T(8,128)(2,1)}, u32[]{:S(2)}) copy-start(bf16[32,1024]{1,0:T(8,128)(2,1)} %panel.1) | copy-start | bytes 196612
  9.4 0.7 copy-start.3
  9.4 0.7 copy-start.4
  9.4 0.7 copy-start.5
  9.4 0.7 copy-start.6
  9.4 3.9 %copy-start.7 = (f32[2]{0:T(128)S(1)}, f32[2]{0:T(128)}, u32[]{:S(2)}) copy-start(f32[2]{0:T(128)} %param.15) | copy-start | bytes 28
  9.5 3.9 %copy-start.8 = (f32[2]{0:T(128)S(1)}, f32[2]{0:T(128)}, u32[]{:S(2)}) copy-start(f32[2]{0:T(128)} %param.14) | copy-start | bytes 28
  9.5 4.8 %copy-start.1 = (bf16[2,8,16,128,128]{4,3,2,1,0:T(8,128)(2,1)S(1)}, bf16[2,8,16,128,128]{4,3,2,1,0:T(8,128)(2,1)}, u32[]{:S(2)}) copy-start(bf16[2,8,16,128,128]{4,3,2,1,0:T(8,128)(2,1)} %tiles.9) | copy-start | bytes 25165828
  10.4 3.9 %collective-permute-start.3 = (bf16[16,32,128]{2,1,0:T(8,128)(2,1)S(1)}, bf16[16,32,128]{2,1,0:T(8,128)(2,1)S(1)}, u32[]{:S(2)}, u32[]{:S(2)}) collective-permute-start(bf16[16,32,128]{2,1,0:T(8,128)(2,1)S(1)} %get-tuple-element.18), channel_id=1, source_target_pairs={{0,4},{4,0},{8,12},{12,8},{16,20},{20,16},{24,28},{28,24},{32,36},... | collective-permute-start | bytes 393224 | tf_op jit(solution)/shard_map/ppermute | solution.py:264
  13.3 4.4 %collective-permute-start.4 = (bf16[16,32,128]{2,1,0:T(8,128)(2,1)S(1)}, bf16[16,32,128]{2,1,0:T(8,128)(2,1)S(1)}, u32[]{:S(2)}, u32[]{:S(2)}) collective-permute-start(bf16[16,32,128]{2,1,0:T(8,128)(2,1)S(1)} %get-tuple-element.21), channel_id=1, source_target_pairs={{0,252},{4,8},{8,4},{12,16},{16,12},{20,24},{24,20},{28,32},{32,28... | collective-permute-start | bytes 393224 | tf_op jit(solution)/shard_map/ppermute | solution.py:263
  19.0 5.0 %collective-permute-start.7 = (bf16[2,8,32,128]{3,2,1,0:T(8,128)(2,1)S(1)}, bf16[2,8,32,128]{3,2,1,0:T(8,128)(2,1)S(1)}, u32[]{:S(2)}, u32[]{:S(2)}) collective-permute-start(bf16[2,8,32,128]{3,2,1,0:T(8,128)(2,1)S(1)} %get-tuple-element.23.refs_0_.first), channel_id=1, source_target_pairs={{0,3},{1,2},{2,1},{3,0},{4,7},{5,6},{6,5},{7,4},{8,11},{9,10},{10,... | collective-permute-start | bytes 393224 | tf_op jit(solution)/shard_map/ppermute | solution.py:257
  20.1 5.3 %collective-permute-start.6 = (bf16[2,8,32,128]{3,2,1,0:T(8,128)(2,1)S(1)}, bf16[2,8,32,128]{3,2,1,0:T(8,128)(2,1)S(1)}, u32[]{:S(2)}, u32[]{:S(2)}) collective-permute-start(bf16[2,8,32,128]{3,2,1,0:T(8,128)(2,1)S(1)} %get-tuple-element.23.refs_0_.first), channel_id=1, source_target_pairs={{0,2},{1,3},{2,0},{3,1},{4,6},{5,7},{6,4},{7,5},{8,10},{9,11},{10,... | collective-permute-start | bytes 393224 | tf_op jit(solution)/shard_map/ppermute | solution.py:257
  20.6 5.4 %collective-permute-start.5 = (bf16[2,8,32,128]{3,2,1,0:T(8,128)(2,1)S(1)}, bf16[2,8,32,128]{3,2,1,0:T(8,128)(2,1)S(1)}, u32[]{:S(2)}, u32[]{:S(2)}) collective-permute-start(bf16[2,8,32,128]{3,2,1,0:T(8,128)(2,1)S(1)} %get-tuple-element.23.refs_0_.first), channel_id=1, source_target_pairs={{0,1},{1,0},{2,3},{3,2},{4,5},{5,4},{6,7},{7,6},{8,9},{9,8},{10,11... | collective-permute-start | bytes 393224 | tf_op jit(solution)/shard_map/ppermute | solution.py:257
  26.1 9.0 %collective-permute-start.9 = (bf16[2,16,32,128]{3,2,1,0:T(8,128)(2,1)S(1)}, bf16[2,16,32,128]{3,2,1,0:T(8,128)(2,1)S(1)}, u32[]{:S(2)}, u32[]{:S(2)}) collective-permute-start(bf16[2,16,32,128]{3,2,1,0:T(8,128)(2,1)S(1)} %get-tuple-element.26), channel_id=1, source_target_pairs={{0,4},{4,0},{8,12},{12,8},{16,20},{20,16},{24,28},{28,24},{32,36},... | collective-permute-start | bytes 786440 | tf_op jit(solution)/shard_map/ppermute | solution.py:264
  34.0 6.1 %collective-permute-start.8 = (bf16[2,16,32,128]{3,2,1,0:T(8,128)(2,1)S(1)}, bf16[2,16,32,128]{3,2,1,0:T(8,128)(2,1)S(1)}, u32[]{:S(2)}, u32[]{:S(2)}) collective-permute-start(bf16[2,16,32,128]{3,2,1,0:T(8,128)(2,1)S(1)} %get-tuple-element.24), channel_id=1, source_target_pairs={{0,252},{4,8},{8,4},{12,16},{16,12},{20,24},{24,20},{28,32},{32,28... | collective-permute-start | bytes 786440 | tf_op jit(solution)/shard_map/ppermute | solution.py:263
  53.6 17.6 %all-to-all-start.1 = ((bf16[16,32,128]{2,1,0:T(8,128)(2,1)}), bf16[16,32,128]{2,1,0:T(8,128)(2,1)S(1)}, u32[]{:S(2)}, u32[]{:S(2)}) async-start(bf16[16,32,128]{2,1,0:T(8,128)(2,1)} %broadcast_in_dim.28), calls=%async_computation.1 | async-start | bytes 262144 | tf_op jit(solution)/shard_map/all_to_all | solution.py:236
  62.0 8.9 %collective-permute-start.12 = (bf16[2,8,32,128]{3,2,1,0:T(8,128)(2,1)S(1)}, bf16[2,8,32,128]{3,2,1,0:T(8,128)(2,1)S(1)}, u32[]{:S(2)}, u32[]{:S(2)}) collective-permute-start(bf16[2,8,32,128]{3,2,1,0:T(8,128)(2,1)S(1)} %get-tuple-element.31.refs_0_), channel_id=1, source_target_pairs={{0,3},{1,2},{2,1},{3,0},{4,7},{5,6},{6,5},{7,4},{8,11},{9,10},{10,... | collective-permute-start | bytes 393224 | tf_op jit(solution)/shard_map/ppermute | solution.py:257
  62.6 8.3 %collective-permute-start.11 = (bf16[2,8,32,128]{3,2,1,0:T(8,128)(2,1)S(1)}, bf16[2,8,32,128]{3,2,1,0:T(8,128)(2,1)S(1)}, u32[]{:S(2)}, u32[]{:S(2)}) collective-permute-start(bf16[2,8,32,128]{3,2,1,0:T(8,128)(2,1)S(1)} %get-tuple-element.31.refs_0_), channel_id=1, source_target_pairs={{0,2},{1,3},{2,0},{3,1},{4,6},{5,7},{6,4},{7,5},{8,10},{9,11},{10,... | collective-permute-start | bytes 393224 | tf_op jit(solution)/shard_map/ppermute | solution.py:257
  64.1 7.2 %collective-permute-start.10 = (bf16[2,8,32,128]{3,2,1,0:T(8,128)(2,1)S(1)}, bf16[2,8,32,128]{3,2,1,0:T(8,128)(2,1)S(1)}, u32[]{:S(2)}, u32[]{:S(2)}) collective-permute-start(bf16[2,8,32,128]{3,2,1,0:T(8,128)(2,1)S(1)} %get-tuple-element.31.refs_0_), channel_id=1, source_target_pairs={{0,1},{1,0},{2,3},{3,2},{4,5},{5,4},{6,7},{7,6},{8,9},{9,8},{10,11... | collective-permute-start | bytes 393224 | tf_op jit(solution)/shard_map/ppermute | solution.py:257

commit v6 on v5

--- a/solution.py
+++ b/solution.py
@@ -94,23 +94,15 @@
     return jnp.where(used, ext[lead + (col,)], 0).astype(ext.dtype)
 
 
-def make_table(ints, built, row_tiles, slots, slab_size, ghosts, odd):
+def list_row(ints, built, found, j, row_tiles, slots, slab_size, ghosts, odd):
     low = slab_size + odd * ghosts
-    found = jnp.int32(0)
-    for j in range(row_tiles):
-        live = ints[row_tiles, j]
-        for k in range(slots):
-            ghost = ints[j, k] - low
-            built[0, found] = (j * slots + k) * ghosts + ghost
-            crosses = jnp.logical_and(jnp.logical_and(ghost >= 0, ghost < ghosts), k < live)
-            found += jnp.where(crosses, 1, 0)
-    built[1, 0] = found
-    for q in range(slab_size):
-        built[4, ints[row_tiles + 1, q]] = q
-    pair_rows, cross_rows = ghost_rows(ints, row_tiles, odd)
-    for g in range(ghosts):
-        built[2, g] = built[4, pair_rows[0, g]]
-        built[3, g] = built[4, cross_rows[0, g]]
+    live = ints[row_tiles, j]
+    for k in range(slots):
+        ghost = ints[j, k] - low
+        built[0, found] = (j * slots + k) * ghosts + ghost
+        crosses = jnp.logical_and(jnp.logical_and(ghost >= 0, ghost < ghosts), k < live)
+        found += jnp.where(crosses, 1, 0)
+    return found
 
 
 def near_first(ints, slab, pair, tiles, part, stored, table, ext, built, done):
@@ -118,13 +110,25 @@
     slab_size, ghosts, vectors = slab.shape[0], pair.shape[0], slab.shape[1]
     me = lax.axis_index("help")
     odd = lax.rem(lax.axis_index("rows"), 2)
-    make_table(ints, built, row_tiles, slots, slab_size, ghosts, odd)
-    hand_over = pltpu.make_async_copy(built, table, done)
-    hand_over.start()
     ext[pl.ds(0, slab_size)] = slab[...]
     ext[pl.ds(slab_size + (1 - odd) * ghosts, ghosts)] = pair[...]
     mine = rolled(ints[row_tiles + 1:row_tiles + 2, :], me * row_tiles)
+    pair_rows, cross_rows = ghost_rows(ints, row_tiles, odd)
+    found = jnp.int32(0)
+    half = row_tiles // 2
+    hand_over = pltpu.make_async_copy(built, table, done)
     for j in range(row_tiles):
+        if j < half:
+            for q in range(j * slab_size // half, (j + 1) * slab_size // half):
+                built[4, ints[row_tiles + 1, q]] = q
+            for row in (2 * j, 2 * j + 1):
+                found = list_row(ints, built, found, row, row_tiles, slots, slab_size, ghosts, odd)
+        if j == half:
+            built[1, 0] = found
+            for g in range(ghosts):
+                built[2, g] = built[4, pair_rows[0, g]]
+                built[3, g] = built[4, cross_rows[0, g]]
+            hand_over.start()
         total = jnp.zeros((vectors, volumes * side), jnp.float32)
         for k in range(0, slots, 2):
             left = jnp.concatenate(

time: 72.4 us -> 72.1 us (level)
  blocking collectives: 11.5 us -> 10.7 us
    all_to_all x1, blocking collectives: 11.5 us -> 10.7 us  [summed_parts(): lax.all_to_all(parts, ('rows', 'help'), 0, 0, axis_index_groups=groups)]
  transfers between devices with their start and end apart: 14 -> 14, of which waited for: 8 -> 9; matrix products, arithmetic and copies ran while one was open for 0% -> 0% of each run, Pallas kernels for 8% -> 8%
where the time goes in v6:
time: 72.1 us; the launch traced here: 71.6 us
  starting transfers between devices  30.6 us (42%)
  waiting for transfers between devices  14.2 us (20%)
  blocking collectives  10.7 us (15%)
  Pallas kernels  9.65 us (13%)
  local copies, waits for them, and re-layouts  5.64 us (8%)
  between operations  0.77 us (1%)
    ppermute x2, starting transfers between devices, exchanged(): pair = lax.ppermute(to_pair, 'rows', [(s, s ^ 1) for s in range(rows)])  11.3 us
    ppermute x9, starting transfers between devices, gathered(): lax.ppermute(shard, 'help', [(i, i ^ d) for i in range(helpers)])  11.1 us
    all_to_all x1, blocking collectives, summed_parts(): lax.all_to_all(parts, ('rows', 'help'), 0, 0, axis_index_groups=groups)  10.7 us
    ppermute x9, waiting for transfers between devices, gathered(): lax.ppermute(shard, 'help', [(i, i ^ d) for i in range(helpers)])  9.75 us
    all_to_all x1, starting transfers between devices, summed_parts(): lax.all_to_all(parts, ('rows', 'help'), 0, 0, axis_index_groups=groups)  8.15 us
    unnamed x18, local copies, waits for them, and re-layouts  4.88 us
    pallas_call x1, Pallas kernels, per_device(): pl.pallas_call(near_first, out_shape=[part_shape, shape(row_tiles, vector...  3.34 us
    pallas_call x1, Pallas kernels, per_device(): pl.pallas_call(near_second, out_shape=part_shape, in_specs=[VMEM] * 4, ou...  2.57 us
  transfers between devices with their start and end apart: 14, of which 9 were waited for; matrix products, arithmetic and copies ran while one was open for 0% of the time, Pallas kernels for 8%

profile of v6, /device:TPU:1, one launch (start us, length us, event | category | flops | bytes accessed | tf_op | source)
XLA Modules:
  0.0 71.6 jit_solution(14607380462424402516)
XLA Ops:
  0.6 2.1 %collective-permute-start = (bf16[32,1024]{1,0:T(8,128)(2,1)}, bf16[32,1024]{1,0:T(8,128)(2,1)S(1)}, u32[]{:S(2)}, u32[]{:S(2)}) collective-permute-start(bf16[32,1024]{1,0:T(8,128)(2,1)} %panel.1), channel_id=1, source_target_pairs={{0,1},{1,0},{2,3},{3,2},{4,5},{5,4},{6,7},{7,6},{8,9},{9,8},{10,11... | collective-permute-start | bytes 196616 | tf_op jit(solution)/shard_map/ppermute | solution.py:261
  2.8 1.8 %collective-permute-start.2 = (bf16[32,1024]{1,0:T(8,128)(2,1)}, bf16[32,1024]{1,0:T(8,128)(2,1)S(1)}, u32[]{:S(2)}, u32[]{:S(2)}) collective-permute-start(bf16[32,1024]{1,0:T(8,128)(2,1)} %panel.1), channel_id=1, source_target_pairs={{0,3},{1,2},{2,1},{3,0},{4,7},{5,6},{6,5},{7,4},{8,11},{9,10},{10,... | collective-permute-start | bytes 196616 | tf_op jit(solution)/shard_map/ppermute | solution.py:261
  4.6 0.6 collective-permute-start.1
  5.2 0.0 copy-start
  5.2 3.4 %copy-done = bf16[2,8,16,128,128]{4,3,2,1,0:T(8,128)(2,1)S(1)} copy-done((bf16[2,8,16,128,128]{4,3,2,1,0:T(8,128)(2,1)S(1)}, bf16[2,8,16,128,128]{4,3,2,1,0:T(8,128)(2,1)}, u32[]{:S(2)}) %copy-start) | copy-done | bytes 8388632
  8.6 0.0 copy-start.2
  8.6 0.8 %copy-done.2 = bf16[32,1024]{1,0:T(8,128)(2,1)S(1)} copy-done((bf16[32,1024]{1,0:T(8,128)(2,1)S(1)}, bf16[32,1024]{1,0:T(8,128)(2,1)}, u32[]{:S(2)}) %copy-start.2) | copy-done | bytes 65560
  9.4 0.0 copy-start.3
  9.4 0.0 copy-start.4
  9.4 0.0 copy-start.5
  9.4 0.0 copy-start.6
  9.4 0.0 copy-start.7
  9.5 0.0 copy-start.8
  9.5 0.0 copy-start.1
  9.5 0.6 copy-done.3
  10.1 0.0 copy-done.4
  10.1 0.0 copy-done.5
  10.1 0.0 copy-done.6
  10.2 0.0 collective-permute-done.refs_1_
  10.2 0.0 collective-permute-done.2.refs_3_
  10.2 0.0 collective-permute-done.1.refs_2_
  10.2 0.2 spread_panel.1
  10.4 2.9 %collective-permute-start.3 = (bf16[16,32,128]{2,1,0:T(8,128)(2,1)S(1)}, bf16[16,32,128]{2,1,0:T(8,128)(2,1)S(1)}, u32[]{:S(2)}, u32[]{:S(2)}) collective-permute-start(bf16[16,32,128]{2,1,0:T(8,128)(2,1)S(1)} %get-tuple-element.18), channel_id=1, source_target_pairs={{0,4},{4,0},{8,12},{12,8},{16,20},{20,16},{24,28},{28,24},{32,36},... | collective-permute-start | bytes 393224 | tf_op jit(solution)/shard_map/ppermute | solution.py:268
  13.3 0.0 collective-permute-start.4
  13.4 0.0 copy-done.7
  13.4 0.0 copy-done.8
  13.4 0.1 pad_maximum_fusion
  13.4 0.9 %collective-permute-done.3.pair = bf16[16,32,128]{2,1,0:T(8,128)(2,1)S(1)} collective-permute-done((bf16[16,32,128]{2,1,0:T(8,128)(2,1)S(1)}, bf16[16,32,128]{2,1,0:T(8,128)(2,1)S(1)}, u32[]{:S(2)}, u32[]{:S(2)}) %collective-permute-start.3) | collective-permute-done | bytes 131104 | tf_op jit(solution)/shard_map/ppermute | solution.py:268
  14.3 0.0 copy-done.1
  14.3 3.3 %near_first.1 = (f32[2,8,32,128]{3,2,1,0:T(8,128)S(1)}, bf16[8,32,128]{2,1,0:T(8,128)(2,1)S(1)}, s32[5,128]{1,0:T(8,128)S(1)}) custom-call(s32[12,128]{1,0:T(8,128)S(1)} %pad_add_fusion.ints, bf16[32,32,128]{2,1,0:T(8,128)(2,1)S(1)} %get-tuple-element.17.slab, bf16[16,32,128]{2,1,0:T(8,128)(2,1)S(1)} %collective-permute-done.3.pair, ...), custom_call_target="tpu_custom_call" | custom-call | flops 536870912 | bytes 8388608 | tf_op jit(solution)/shard_map/near_first/pallas_call | solution.py:307
  17.6 0.1 collective-permute-done.4.cross
  17.7 0.1 broadcast_in_dim.12.coefs
  17.8 1.1 %apply_first.1 = (bf16[2,8,32,128]{3,2,1,0:T(8,128)(2,1)S(1)}, f32[2,32,32]{2,1,0:T(8,128)S(1)}) custom-call(f32[4,128]{1,0:T(4,128)S(1)} %broadcast_in_dim.12.coefs, s32[5,128]{1,0:T(8,128)S(1)} %get-tuple-element.19.table, bf16[8,32,128]{2,1,0:T(8,128)(2,1)S(1)} %get-tuple-element.20.stored, bf16[16,32,128]{2,1,0:T(8,128)(2,1)S(1)} %collective-permute-done.4.cross, ...), custom_call_target="tpu_custom_call" | custom-call | tf_op jit(solution)/shard_map/apply_first/pallas_call | solution.py:325
  18.9 1.1 %collective-permute-start.7 = (bf16[2,8,32,128]{3,2,1,0:T(8,128)(2,1)S(1)}, bf16[2,8,32,128]{3,2,1,0:T(8,128)(2,1)S(1)}, u32[]{:S(2)}, u32[]{:S(2)}) collective-permute-start(bf16[2,8,32,128]{3,2,1,0:T(8,128)(2,1)S(1)} %get-tuple-element.23.refs_0_.first), channel_id=1, source_target_pairs={{0,3},{1,2},{2,1},{3,0},{4,7},{5,6},{6,5},{7,4},{8,11},{9,10},{10,... | collective-permute-start | bytes 393224 | tf_op jit(solution)/shard_map/ppermute | solution.py:261
  20.0 0.8 %collective-permute-start.6 = (bf16[2,8,32,128]{3,2,1,0:T(8,128)(2,1)S(1)}, bf16[2,8,32,128]{3,2,1,0:T(8,128)(2,1)S(1)}, u32[]{:S(2)}, u32[]{:S(2)}) collective-permute-start(bf16[2,8,32,128]{3,2,1,0:T(8,128)(2,1)S(1)} %get-tuple-element.23.refs_0_.first), channel_id=1, source_target_pairs={{0,2},{1,3},{2,0},{3,1},{4,6},{5,7},{6,4},{7,5},{8,10},{9,11},{10,... | collective-permute-start | bytes 393224 | tf_op jit(solution)/shard_map/ppermute | solution.py:261
  20.8 1.4 %collective-permute-start.5 = (bf16[2,8,32,128]{3,2,1,0:T(8,128)(2,1)S(1)}, bf16[2,8,32,128]{3,2,1,0:T(8,128)(2,1)S(1)}, u32[]{:S(2)}, u32[]{:S(2)}) collective-permute-start(bf16[2,8,32,128]{3,2,1,0:T(8,128)(2,1)S(1)} %get-tuple-element.23.refs_0_.first), channel_id=1, source_target_pairs={{0,1},{1,0},{2,3},{3,2},{4,5},{5,4},{6,7},{7,6},{8,9},{9,8},{10,11... | collective-permute-start | bytes 393224 | tf_op jit(solution)/shard_map/ppermute | solution.py:261
  22.2 1.8 %collective-permute-done.7.refs_3_ = bf16[2,8,32,128]{3,2,1,0:T(8,128)(2,1)S(1)} collective-permute-done((bf16[2,8,32,128]{3,2,1,0:T(8,128)(2,1)S(1)}, bf16[2,8,32,128]{3,2,1,0:T(8,128)(2,1)S(1)}, u32[]{:S(2)}, u32[]{:S(2)}) %collective-permute-start.7) | collective-permute-done | bytes 131104 | tf_op jit(solution)/shard_map/ppermute | solution.py:261
  24.0 1.4 %collective-permute-done.6.refs_2_ = bf16[2,8,32,128]{3,2,1,0:T(8,128)(2,1)S(1)} collective-permute-done((bf16[2,8,32,128]{3,2,1,0:T(8,128)(2,1)S(1)}, bf16[2,8,32,128]{3,2,1,0:T(8,128)(2,1)S(1)}, u32[]{:S(2)}, u32[]{:S(2)}) %collective-permute-start.6) | collective-permute-done | bytes 131104 | tf_op jit(solution)/shard_map/ppermute | solution.py:261
  25.4 0.6 collective-permute-done.5.refs_1_
  25.9 0.1 spread_field.1
  26.1 8.3 %collective-permute-start.9 = (bf16[2,16,32,128]{3,2,1,0:T(8,128)(2,1)S(1)}, bf16[2,16,32,128]{3,2,1,0:T(8,128)(2,1)S(1)}, u32[]{:S(2)}, u32[]{:S(2)}) collective-permute-start(bf16[2,16,32,128]{3,2,1,0:T(8,128)(2,1)S(1)} %get-tuple-element.26), channel_id=1, source_target_pairs={{0,4},{4,0},{8,12},{12,8},{16,20},{20,16},{24,28},{28,24},{32,36},... | collective-permute-start | bytes 786440 | tf_op jit(solution)/shard_map/ppermute | solution.py:268
  34.4 0.0 collective-permute-start.8
  34.4 1.2 %collective-permute-done.9.pair = bf16[2,16,32,128]{3,2,1,0:T(8,128)(2,1)S(1)} collective-permute-done((bf16[2,16,32,128]{3,2,1,0:T(8,128)(2,1)S(1)}, bf16[2,16,32,128]{3,2,1,0:T(8,128)(2,1)S(1)}, u32[]{:S(2)}, u32[]{:S(2)}) %collective-permute-start.9) | collective-permute-done | bytes 262176 | tf_op jit(solution)/shard_map/ppermute | solution.py:268
  35.6 2.6 %near_second.1.part = f32[2,8,32,128]{3,2,1,0:T(8,128)S(1)} custom-call(s32[12,128]{1,0:T(8,128)S(1)} %pad_add_fusion.ints, bf16[2,32,32,128]{3,2,1,0:T(8,128)(2,1)S(1)} %get-tuple-element.25.slab, bf16[2,16,32,128]{3,2,1,0:T(8,128)(2,1)S(1)} %collective-permute-done.9.pair, bf16[2,8,16,128,128]{4,3,2,1,0:T(8,128)(2,1)S(1)} %copy-done.1), custom_call_target="tpu_custom_call" | custom-call | flops 536870912 | bytes 8388608 | tf_op jit(solution)/shard_map/near_second/pallas_call | solution.py:346
  38.2 2.4 %collective-permute-done.8.cross = bf16[2,16,32,128]{3,2,1,0:T(8,128)(2,1)S(1)} collective-permute-done((bf16[2,16,32,128]{3,2,1,0:T(8,128)(2,1)S(1)}, bf16[2,16,32,128]{3,2,1,0:T(8,128)(2,1)S(1)}, u32[]{:S(2)}, u32[]{:S(2)}) %collective-permute-start.8) | collective-permute-done | bytes 262176 | tf_op jit(solution)/shard_map/ppermute | solution.py:267
  40.5 1.3 %apply_second.1 = (bf16[2,8,32,128]{3,2,1,0:T(8,128)(2,1)S(1)}, f32[32,128]{1,0:T(8,128)S(1)}) custom-call(f32[4,128]{1,0:T(4,128)S(1)} %broadcast_in_dim.12.coefs, s32[5,128]{1,0:T(8,128)S(1)} %get-tuple-element.19.table, bf16[8,32,128]{2,1,0:T(8,128)(2,1)S(1)} %get-tuple-element.20.stored, bf16[2,16,32,128]{3,2,1,0:T(8,128)(2,1)S(1)} %collective-permute-done.8.cross, ...), custom_call_target="tpu_custom_call" | custom-call | tf_op jit(solution)/shard_map/apply_second/pallas_call | solution.py:356
  41.9 10.7 %all_to_all.10 = bf16[16,32,128]{2,1,0:T(8,128)(2,1)S(1)} all-to-all(bf16[16,32,128]{2,1,0:T(8,128)(2,1)S(1)} %broadcast_in_dim.13), channel_id=1, replica_groups={{0,1,2,3,8,9,10,11,16,17,18,19,24,25,26,27},{4,5,6,7,12,13,14,15,20,21,..., dimensions={0} | all-to-all | bytes 262144 | tf_op jit(solution)/shard_map/all_to_all | solution.py:240
  52.6 0.7 broadcast_in_dim.28
  53.2 8.2 %all-to-all-start.1 = ((bf16[16,32,128]{2,1,0:T(8,128)(2,1)}), bf16[16,32,128]{2,1,0:T(8,128)(2,1)S(1)}, u32[]{:S(2)}, u32[]{:S(2)}) async-start(bf16[16,32,128]{2,1,0:T(8,128)(2,1)} %broadcast_in_dim.28), calls=%async_computation.1 | async-start | bytes 262144 | tf_op jit(solution)/shard_map/all_to_all | solution.py:240
  61.4 0.7 collective-permute-start.12
  62.0 1.4 %collective-permute-start.11 = (bf16[2,8,32,128]{3,2,1,0:T(8,128)(2,1)S(1)}, bf16[2,8,32,128]{3,2,1,0:T(8,128)(2,1)S(1)}, u32[]{:S(2)}, u32[]{:S(2)}) collective-permute-start(bf16[2,8,32,128]{3,2,1,0:T(8,128)(2,1)S(1)} %get-tuple-element.31.refs_0_), channel_id=1, source_target_pairs={{0,2},{1,3},{2,0},{3,1},{4,6},{5,7},{6,4},{7,5},{8,10},{9,11},{10,... | collective-permute-start | bytes 393224 | tf_op jit(solution)/shard_map/ppermute | solution.py:261
  63.5 1.2 %collective-permute-start.10 = (bf16[2,8,32,128]{3,2,1,0:T(8,128)(2,1)S(1)}, bf16[2,8,32,128]{3,2,1,0:T(8,128)(2,1)S(1)}, u32[]{:S(2)}, u32[]{:S(2)}) collective-permute-start(bf16[2,8,32,128]{3,2,1,0:T(8,128)(2,1)S(1)} %get-tuple-element.31.refs_0_), channel_id=1, source_target_pairs={{0,1},{1,0},{2,3},{3,2},{4,5},{5,4},{6,7},{7,6},{8,9},{9,8},{10,11... | collective-permute-start | bytes 393224 | tf_op jit(solution)/shard_map/ppermute | solution.py:261
  64.6 5.7 %collective-permute-done.12.refs_3_ = bf16[2,8,32,128]{3,2,1,0:T(8,128)(2,1)S(1)} collective-permute-done((bf16[2,8,32,128]{3,2,1,0:T(8,128)(2,1)S(1)}, bf16[2,8,32,128]{3,2,1,0:T(8,128)(2,1)S(1)}, u32[]{:S(2)}, u32[]{:S(2)}) %collective-permute-start.12) | collective-permute-done | bytes 131104 | tf_op jit(solution)/shard_map/ppermute | solution.py:261
  70.3 0.0 collective-permute-done.11.refs_2_
  70.3 0.3 collective-permute-done.10.refs_1_
  70.6 0.0 all-to-all-done.1.parts
  70.6 0.9 %finish.1 = (bf16[2,32,1024]{2,1,0:T(8,128)(2,1)}, f32[2,2,32,32]{3,2,1,0:T(8,128)}) custom-call(s32[5,128]{1,0:T(8,128)S(1)} %get-tuple-element.19.table, bf16[16,32,128]{2,1,0:T(8,128)(2,1)S(1)} %all-to-all-done.1.parts, bf16[2,8,32,128]{3,2,1,0:T(8,128)(2,1)S(1)} %get-tuple-element.31.refs_0_, ...), custom_call_target="tpu_custom_call" | custom-call | tf_op jit(solution)/shard_map/finish/pallas_call | solution.py:383
  (5 shorter events, 0.1 us)
Async XLA Ops:
  0.6 9.5 %collective-permute-start = (bf16[32,1024]{1,0:T(8,128)(2,1)}, bf16[32,1024]{1,0:T(8,128)(2,1)S(1)}, u32[]{:S(2)}, u32[]{:S(2)}) collective-permute-start(bf16[32,1024]{1,0:T(8,128)(2,1)} %panel.1), channel_id=1, source_target_pairs={{0,1},{1,0},{2,3},{3,2},{4,5},{5,4},{6,7},{7,6},{8,9},{9,8},{10,11... | collective-permute-start | bytes 196616 | tf_op jit(solution)/shard_map/ppermute | solution.py:261
  2.8 7.4 %collective-permute-start.2 = (bf16[32,1024]{1,0:T(8,128)(2,1)}, bf16[32,1024]{1,0:T(8,128)(2,1)S(1)}, u32[]{:S(2)}, u32[]{:S(2)}) collective-permute-start(bf16[32,1024]{1,0:T(8,128)(2,1)} %panel.1), channel_id=1, source_target_pairs={{0,3},{1,2},{2,1},{3,0},{4,7},{5,6},{6,5},{7,4},{8,11},{9,10},{10,... | collective-permute-start | bytes 196616 | tf_op jit(solution)/shard_map/ppermute | solution.py:261
  4.6 5.6 %collective-permute-start.1 = (bf16[32,1024]{1,0:T(8,128)(2,1)}, bf16[32,1024]{1,0:T(8,128)(2,1)S(1)}, u32[]{:S(2)}, u32[]{:S(2)}) collective-permute-start(bf16[32,1024]{1,0:T(8,128)(2,1)} %panel.1), channel_id=1, source_target_pairs={{0,2},{1,3},{2,0},{3,1},{4,6},{5,7},{6,4},{7,5},{8,10},{9,11},{10,... | collective-permute-start | bytes 196616 | tf_op jit(solution)/shard_map/ppermute | solution.py:261
  5.2 3.4 %copy-start = (bf16[2,8,16,128,128]{4,3,2,1,0:T(8,128)(2,1)S(1)}, bf16[2,8,16,128,128]{4,3,2,1,0:T(8,128)(2,1)}, u32[]{:S(2)}) copy-start(bf16[2,8,16,128,128]{4,3,2,1,0:T(8,128)(2,1)} %tiles.9) | copy-start | bytes 25165828
  8.6 0.8 %copy-start.2 = (bf16[32,1024]{1,0:T(8,128)(2,1)S(1)}, bf16[32,1024]{1,0:T(8,128)(2,1)}, u32[]{:S(2)}) copy-start(bf16[32,1024]{1,0:T(8,128)(2,1)} %panel.1) | copy-start | bytes 196612
  9.4 0.7 copy-start.3
  9.4 0.7 copy-start.4
  9.4 0.7 copy-start.5
  9.4 0.7 copy-start.6
  9.4 3.9 %copy-start.7 = (f32[2]{0:T(128)S(1)}, f32[2]{0:T(128)}, u32[]{:S(2)}) copy-start(f32[2]{0:T(128)} %param.15) | copy-start | bytes 28
  9.5 3.9 %copy-start.8 = (f32[2]{0:T(128)S(1)}, f32[2]{0:T(128)}, u32[]{:S(2)}) copy-start(f32[2]{0:T(128)} %param.14) | copy-start | bytes 28
  9.5 4.8 %copy-start.1 = (bf16[2,8,16,128,128]{4,3,2,1,0:T(8,128)(2,1)S(1)}, bf16[2,8,16,128,128]{4,3,2,1,0:T(8,128)(2,1)}, u32[]{:S(2)}) copy-start(bf16[2,8,16,128,128]{4,3,2,1,0:T(8,128)(2,1)} %tiles.9) | copy-start | bytes 25165828
  10.4 3.9 %collective-permute-start.3 = (bf16[16,32,128]{2,1,0:T(8,128)(2,1)S(1)}, bf16[16,32,128]{2,1,0:T(8,128)(2,1)S(1)}, u32[]{:S(2)}, u32[]{:S(2)}) collective-permute-start(bf16[16,32,128]{2,1,0:T(8,128)(2,1)S(1)} %get-tuple-element.18), channel_id=1, source_target_pairs={{0,4},{4,0},{8,12},{12,8},{16,20},{20,16},{24,28},{28,24},{32,36},... | collective-permute-start | bytes 393224 | tf_op jit(solution)/shard_map/ppermute | solution.py:268
  13.3 4.4 %collective-permute-start.4 = (bf16[16,32,128]{2,1,0:T(8,128)(2,1)S(1)}, bf16[16,32,128]{2,1,0:T(8,128)(2,1)S(1)}, u32[]{:S(2)}, u32[]{:S(2)}) collective-permute-start(bf16[16,32,128]{2,1,0:T(8,128)(2,1)S(1)} %get-tuple-element.21), channel_id=1, source_target_pairs={{0,252},{4,8},{8,4},{12,16},{16,12},{20,24},{24,20},{28,32},{32,28... | collective-permute-start | bytes 393224 | tf_op jit(solution)/shard_map/ppermute | solution.py:267
  18.9 5.1 %collective-permute-start.7 = (bf16[2,8,32,128]{3,2,1,0:T(8,128)(2,1)S(1)}, bf16[2,8,32,128]{3,2,1,0:T(8,128)(2,1)S(1)}, u32[]{:S(2)}, u32[]{:S(2)}) collective-permute-start(bf16[2,8,32,128]{3,2,1,0:T(8,128)(2,1)S(1)} %get-tuple-element.23.refs_0_.first), channel_id=1, source_target_pairs={{0,3},{1,2},{2,1},{3,0},{4,7},{5,6},{6,5},{7,4},{8,11},{9,10},{10,... | collective-permute-start | bytes 393224 | tf_op jit(solution)/shard_map/ppermute | solution.py:261
  20.0 5.4 %collective-permute-start.6 = (bf16[2,8,32,128]{3,2,1,0:T(8,128)(2,1)S(1)}, bf16[2,8,32,128]{3,2,1,0:T(8,128)(2,1)S(1)}, u32[]{:S(2)}, u32[]{:S(2)}) collective-permute-start(bf16[2,8,32,128]{3,2,1,0:T(8,128)(2,1)S(1)} %get-tuple-element.23.refs_0_.first), channel_id=1, source_target_pairs={{0,2},{1,3},{2,0},{3,1},{4,6},{5,7},{6,4},{7,5},{8,10},{9,11},{10,... | collective-permute-start | bytes 393224 | tf_op jit(solution)/shard_map/ppermute | solution.py:261
  20.8 5.1 %collective-permute-start.5 = (bf16[2,8,32,128]{3,2,1,0:T(8,128)(2,1)S(1)}, bf16[2,8,32,128]{3,2,1,0:T(8,128)(2,1)S(1)}, u32[]{:S(2)}, u32[]{:S(2)}) collective-permute-start(bf16[2,8,32,128]{3,2,1,0:T(8,128)(2,1)S(1)} %get-tuple-element.23.refs_0_.first), channel_id=1, source_target_pairs={{0,1},{1,0},{2,3},{3,2},{4,5},{5,4},{6,7},{7,6},{8,9},{9,8},{10,11... | collective-permute-start | bytes 393224 | tf_op jit(solution)/shard_map/ppermute | solution.py:261
  26.1 9.5 %collective-permute-start.9 = (bf16[2,16,32,128]{3,2,1,0:T(8,128)(2,1)S(1)}, bf16[2,16,32,128]{3,2,1,0:T(8,128)(2,1)S(1)}, u32[]{:S(2)}, u32[]{:S(2)}) collective-permute-start(bf16[2,16,32,128]{3,2,1,0:T(8,128)(2,1)S(1)} %get-tuple-element.26), channel_id=1, source_target_pairs={{0,4},{4,0},{8,12},{12,8},{16,20},{20,16},{24,28},{28,24},{32,36},... | collective-permute-start | bytes 786440 | tf_op jit(solution)/shard_map/ppermute | solution.py:268
  34.4 6.1 %collective-permute-start.8 = (bf16[2,16,32,128]{3,2,1,0:T(8,128)(2,1)S(1)}, bf16[2,16,32,128]{3,2,1,0:T(8,128)(2,1)S(1)}, u32[]{:S(2)}, u32[]{:S(2)}) collective-permute-start(bf16[2,16,32,128]{3,2,1,0:T(8,128)(2,1)S(1)} %get-tuple-element.24), channel_id=1, source_target_pairs={{0,252},{4,8},{8,4},{12,16},{16,12},{20,24},{24,20},{28,32},{32,28... | collective-permute-start | bytes 786440 | tf_op jit(solution)/shard_map/ppermute | solution.py:267
  53.2 17.4 %all-to-all-start.1 = ((bf16[16,32,128]{2,1,0:T(8,128)(2,1)}), bf16[16,32,128]{2,1,0:T(8,128)(2,1)S(1)}, u32[]{:S(2)}, u32[]{:S(2)}) async-start(bf16[16,32,128]{2,1,0:T(8,128)(2,1)} %broadcast_in_dim.28), calls=%async_computation.1 | async-start | bytes 262144 | tf_op jit(solution)/shard_map/all_to_all | solution.py:240
  61.4 8.9 %collective-permute-start.12 = (bf16[2,8,32,128]{3,2,1,0:T(8,128)(2,1)S(1)}, bf16[2,8,32,128]{3,2,1,0:T(8,128)(2,1)S(1)}, u32[]{:S(2)}, u32[]{:S(2)}) collective-permute-start(bf16[2,8,32,128]{3,2,1,0:T(8,128)(2,1)S(1)} %get-tuple-element.31.refs_0_), channel_id=1, source_target_pairs={{0,3},{1,2},{2,1},{3,0},{4,7},{5,6},{6,5},{7,4},{8,11},{9,10},{10,... | collective-permute-start | bytes 393224 | tf_op jit(solution)/shard_map/ppermute | solution.py:261
  62.0 8.3 %collective-permute-start.11 = (bf16[2,8,32,128]{3,2,1,0:T(8,128)(2,1)S(1)}, bf16[2,8,32,128]{3,2,1,0:T(8,128)(2,1)S(1)}, u32[]{:S(2)}, u32[]{:S(2)}) collective-permute-start(bf16[2,8,32,128]{3,2,1,0:T(8,128)(2,1)S(1)} %get-tuple-element.31.refs_0_), channel_id=1, source_target_pairs={{0,2},{1,3},{2,0},{3,1},{4,6},{5,7},{6,4},{7,5},{8,10},{9,11},{10,... | collective-permute-start | bytes 393224 | tf_op jit(solution)/shard_map/ppermute | solution.py:261
  63.5 7.2 %collective-permute-start.10 = (bf16[2,8,32,128]{3,2,1,0:T(8,128)(2,1)S(1)}, bf16[2,8,32,128]{3,2,1,0:T(8,128)(2,1)S(1)}, u32[]{:S(2)}, u32[]{:S(2)}) collective-permute-start(bf16[2,8,32,128]{3,2,1,0:T(8,128)(2,1)S(1)} %get-tuple-element.31.refs_0_), channel_id=1, source_target_pairs={{0,1},{1,0},{2,3},{3,2},{4,5},{5,4},{6,7},{7,6},{8,9},{9,8},{10,11... | collective-permute-start | bytes 393224 | tf_op jit(solution)/shard_map/ppermute | solution.py:261

commit v7 on v6

--- a/solution.py
+++ b/solution.py
@@ -21,6 +21,10 @@
         blocks[j] = panel[:, j * side:(j + 1) * side]
 
 
+def distances(helpers):
+    return sorted(range(helpers), key=lambda d: min(d, helpers - d))
+
+
 def rolled(row, first):
     return pltpu.roll(row, lax.rem(row.shape[1] - first, row.shape[1]), 1)
 
@@ -37,10 +41,10 @@
     odd = lax.rem(lax.axis_index("rows"), 2)
     side = slab.shape[2]
     row_tiles = slab.shape[0] // helpers
-    for d in range(helpers):
+    for at, d in enumerate(distances(helpers)):
         base = (me ^ d) * row_tiles
         for j in range(row_tiles):
-            slab[base + j] = shards[d][:, j * side:(j + 1) * side] if d else shards[0][j]
+            slab[base + j] = shards[at][:, j * side:(j + 1) * side] if d else shards[0][j]
     pair_rows, cross_rows = ghost_rows(ints, row_tiles, odd)
     for g in range(to_pair.shape[0]):
         to_cross[g] = slab[cross_rows[0, g]]
@@ -51,8 +55,8 @@
     shards, (slab, to_pair, to_cross) = refs[:helpers], refs[helpers:]
     me = lax.axis_index("help")
     row_tiles = slab.shape[1] // helpers
-    for d in range(helpers):
-        slab[:, pl.ds((me ^ d) * row_tiles, row_tiles)] = shards[d][...]
+    for at, d in enumerate(distances(helpers)):
+        slab[:, pl.ds((me ^ d) * row_tiles, row_tiles)] = shards[at][...]
     for g in range(to_pair.shape[1]):
         to_cross[:, g] = slab[:, table[3, g]]
         to_pair[:, g] = slab[:, table[2, g]]
@@ -68,8 +72,8 @@
         held = lax.rem(slot, row_tiles)
         step = lax.div(slot, row_tiles) ^ me
         block = shards[0][:, held]
-        for d in range(1, helpers):
-            block = jnp.where(step == d, shards[d][:, held], block)
+        for at, d in enumerate(distances(helpers)):
+            block = jnp.where(step == d, shards[at][:, held], block)
         out[:, :, j * side:(j + 1) * side] = block
     volumes, steps, vectors, _ = gram.shape
     total = jnp.sum(parts[...].astype(jnp.float32), axis=0) * scale
@@ -258,7 +262,7 @@
 
     def gathered(shard):
         others = [
-            lax.ppermute(shard, "help", [(i, i ^ d) for i in range(helpers)]) for d in range(1, helpers)
+            lax.ppermute(shard, "help", [(i, i ^ d) for i in range(helpers)]) for d in distances(helpers)[1:]
         ]
         return [shard] + others
 

time: 72.1 us -> 72.2 us (level)
  starting transfers between devices: 30.6 us -> 28.8 us
  waiting for transfers between devices: 14.2 us -> 15.4 us
    ppermute x9, waiting for transfers between devices: 9.75 us -> 10.9 us  [gathered(): lax.ppermute(shard, 'help', [(i, i ^ d) for i in range(helpers)])]
    ppermute x9, starting transfers between devices: 11.1 us -> 9.95 us  [gathered(): lax.ppermute(shard, 'help', [(i, i ^ d) for i in range(helpers)])]
  transfers between devices with their start and end apart: 14 -> 14, of which waited for: 9 -> 8; matrix products, arithmetic and copies ran while one was open for 0% -> 0% of each run, Pallas kernels for 8% -> 8%
where the time goes in v7:
time: 72.2 us; the launch traced here: 72 us
  starting transfers between devices  28.8 us (40%)
  waiting for transfers between devices  15.4 us (21%)
  blocking collectives  11 us (15%)
  Pallas kernels  10.2 us (14%)
  local copies, waits for them, and re-layouts  5.64 us (8%)
  between operations  0.78 us (1%)
    all_to_all x1, blocking collectives, summed_parts(): lax.all_to_all(parts, ('rows', 'help'), 0, 0, axis_index_groups=groups)  11 us
    ppermute x9, waiting for transfers between devices, gathered(): lax.ppermute(shard, 'help', [(i, i ^ d) for i in range(helpers)])  10.9 us
    ppermute x2, starting transfers between devices, exchanged(): pair = lax.ppermute(to_pair, 'rows', [(s, s ^ 1) for s in range(rows)])  10.6 us
    ppermute x9, starting transfers between devices, gathered(): lax.ppermute(shard, 'help', [(i, i ^ d) for i in range(helpers)])  9.95 us
    all_to_all x1, starting transfers between devices, summed_parts(): lax.all_to_all(parts, ('rows', 'help'), 0, 0, axis_index_groups=groups)  8.2 us
    unnamed x18, local copies, waits for them, and re-layouts  4.88 us
    pallas_call x1, Pallas kernels, per_device(): pl.pallas_call(near_first, out_shape=[part_shape, shape(row_tiles, vector...  3.34 us
    pallas_call x1, Pallas kernels, per_device(): pl.pallas_call(near_second, out_shape=part_shape, in_specs=[VMEM] * 4, ou...  2.57 us
  transfers between devices with their start and end apart: 14, of which 8 were waited for; matrix products, arithmetic and copies ran while one was open for 0% of the time, Pallas kernels for 8%

profile of v7, /device:TPU:1, one launch (start us, length us, event | category | flops | bytes accessed | tf_op | source)
XLA Modules:
  0.0 72.0 jit_solution(14257008676919921806)
XLA Ops:
  0.6 2.1 %collective-permute-start = (bf16[32,1024]{1,0:T(8,128)(2,1)}, bf16[32,1024]{1,0:T(8,128)(2,1)S(1)}, u32[]{:S(2)}, u32[]{:S(2)}) collective-permute-start(bf16[32,1024]{1,0:T(8,128)(2,1)} %panel.1), channel_id=1, source_target_pairs={{0,1},{1,0},{2,3},{3,2},{4,5},{5,4},{6,7},{7,6},{8,9},{9,8},{10,11... | collective-permute-start | bytes 196616 | tf_op jit(solution)/shard_map/ppermute | solution.py:265
  2.8 2.5 %collective-permute-start.2 = (bf16[32,1024]{1,0:T(8,128)(2,1)}, bf16[32,1024]{1,0:T(8,128)(2,1)S(1)}, u32[]{:S(2)}, u32[]{:S(2)}) collective-permute-start(bf16[32,1024]{1,0:T(8,128)(2,1)} %panel.1), channel_id=1, source_target_pairs={{0,2},{1,3},{2,0},{3,1},{4,6},{5,7},{6,4},{7,5},{8,10},{9,11},{10,... | collective-permute-start | bytes 196616 | tf_op jit(solution)/shard_map/ppermute | solution.py:265
  5.2 0.0 collective-permute-start.1
  5.3 0.0 copy-start
  5.3 3.4 %copy-done = bf16[2,8,16,128,128]{4,3,2,1,0:T(8,128)(2,1)S(1)} copy-done((bf16[2,8,16,128,128]{4,3,2,1,0:T(8,128)(2,1)S(1)}, bf16[2,8,16,128,128]{4,3,2,1,0:T(8,128)(2,1)}, u32[]{:S(2)}) %copy-start) | copy-done | bytes 8388632
  8.6 0.0 copy-start.2
  8.6 0.8 %copy-done.2 = bf16[32,1024]{1,0:T(8,128)(2,1)S(1)} copy-done((bf16[32,1024]{1,0:T(8,128)(2,1)S(1)}, bf16[32,1024]{1,0:T(8,128)(2,1)}, u32[]{:S(2)}) %copy-start.2) | copy-done | bytes 65560
  9.5 0.0 copy-start.3
  9.5 0.0 copy-start.4
  9.5 0.0 copy-start.5
  9.5 0.0 copy-start.6
  9.5 0.0 copy-start.7
  9.5 0.0 copy-start.8
  9.5 0.0 copy-start.1
  9.5 0.6 copy-done.3
  10.2 0.0 copy-done.4
  10.2 0.0 copy-done.5
  10.2 0.0 copy-done.6
  10.2 0.0 collective-permute-done.refs_1_
  10.2 0.0 collective-permute-done.2.refs_3_
  10.2 0.0 collective-permute-done.1.refs_2_
  10.2 0.2 spread_panel.1
  10.4 3.5 %collective-permute-start.3 = (bf16[16,32,128]{2,1,0:T(8,128)(2,1)S(1)}, bf16[16,32,128]{2,1,0:T(8,128)(2,1)S(1)}, u32[]{:S(2)}, u32[]{:S(2)}) collective-permute-start(bf16[16,32,128]{2,1,0:T(8,128)(2,1)S(1)} %get-tuple-element.18), channel_id=1, source_target_pairs={{0,4},{4,0},{8,12},{12,8},{16,20},{20,16},{24,28},{28,24},{32,36},... | collective-permute-start | bytes 393224 | tf_op jit(solution)/shard_map/ppermute | solution.py:272
  13.9 0.0 collective-permute-start.4
  13.9 0.0 copy-done.7
  13.9 0.0 copy-done.8
  13.9 0.1 pad_maximum_fusion
  14.0 0.9 %collective-permute-done.3.pair = bf16[16,32,128]{2,1,0:T(8,128)(2,1)S(1)} collective-permute-done((bf16[16,32,128]{2,1,0:T(8,128)(2,1)S(1)}, bf16[16,32,128]{2,1,0:T(8,128)(2,1)S(1)}, u32[]{:S(2)}, u32[]{:S(2)}) %collective-permute-start.3) | collective-permute-done | bytes 131104 | tf_op jit(solution)/shard_map/ppermute | solution.py:272
  14.9 0.0 copy-done.1
  14.9 3.3 %near_first.1 = (f32[2,8,32,128]{3,2,1,0:T(8,128)S(1)}, bf16[8,32,128]{2,1,0:T(8,128)(2,1)S(1)}, s32[5,128]{1,0:T(8,128)S(1)}) custom-call(s32[12,128]{1,0:T(8,128)S(1)} %pad_add_fusion.ints, bf16[32,32,128]{2,1,0:T(8,128)(2,1)S(1)} %get-tuple-element.17.slab, bf16[16,32,128]{2,1,0:T(8,128)(2,1)S(1)} %collective-permute-done.3.pair, ...), custom_call_target="tpu_custom_call" | custom-call | flops 536870912 | bytes 8388608 | tf_op jit(solution)/shard_map/near_first/pallas_call | solution.py:311
  18.2 0.1 collective-permute-done.4.cross
  18.3 0.1 broadcast_in_dim.12.coefs
  18.4 1.4 %apply_first.1 = (bf16[2,8,32,128]{3,2,1,0:T(8,128)(2,1)S(1)}, f32[2,32,32]{2,1,0:T(8,128)S(1)}) custom-call(f32[4,128]{1,0:T(4,128)S(1)} %broadcast_in_dim.12.coefs, s32[5,128]{1,0:T(8,128)S(1)} %get-tuple-element.19.table, bf16[8,32,128]{2,1,0:T(8,128)(2,1)S(1)} %get-tuple-element.20.stored, bf16[16,32,128]{2,1,0:T(8,128)(2,1)S(1)} %collective-permute-done.4.cross, ...), custom_call_target="tpu_custom_call" | custom-call | tf_op jit(solution)/shard_map/apply_first/pallas_call | solution.py:329
  19.8 0.0 collective-permute-start.7
  19.8 0.9 %collective-permute-start.6 = (bf16[2,8,32,128]{3,2,1,0:T(8,128)(2,1)S(1)}, bf16[2,8,32,128]{3,2,1,0:T(8,128)(2,1)S(1)}, u32[]{:S(2)}, u32[]{:S(2)}) collective-permute-start(bf16[2,8,32,128]{3,2,1,0:T(8,128)(2,1)S(1)} %get-tuple-element.23.refs_0_.first), channel_id=1, source_target_pairs={{0,3},{1,2},{2,1},{3,0},{4,7},{5,6},{6,5},{7,4},{8,11},{9,10},{10,... | collective-permute-start | bytes 393224 | tf_op jit(solution)/shard_map/ppermute | solution.py:265
  20.7 1.8 %collective-permute-start.5 = (bf16[2,8,32,128]{3,2,1,0:T(8,128)(2,1)S(1)}, bf16[2,8,32,128]{3,2,1,0:T(8,128)(2,1)S(1)}, u32[]{:S(2)}, u32[]{:S(2)}) collective-permute-start(bf16[2,8,32,128]{3,2,1,0:T(8,128)(2,1)S(1)} %get-tuple-element.23.refs_0_.first), channel_id=1, source_target_pairs={{0,1},{1,0},{2,3},{3,2},{4,5},{5,4},{6,7},{7,6},{8,9},{9,8},{10,11... | collective-permute-start | bytes 393224 | tf_op jit(solution)/shard_map/ppermute | solution.py:265
  22.5 2.8 %collective-permute-done.7.refs_3_ = bf16[2,8,32,128]{3,2,1,0:T(8,128)(2,1)S(1)} collective-permute-done((bf16[2,8,32,128]{3,2,1,0:T(8,128)(2,1)S(1)}, bf16[2,8,32,128]{3,2,1,0:T(8,128)(2,1)S(1)}, u32[]{:S(2)}, u32[]{:S(2)}) %collective-permute-start.7) | collective-permute-done | bytes 131104 | tf_op jit(solution)/shard_map/ppermute | solution.py:265
  25.2 1.1 %collective-permute-done.6.refs_2_ = bf16[2,8,32,128]{3,2,1,0:T(8,128)(2,1)S(1)} collective-permute-done((bf16[2,8,32,128]{3,2,1,0:T(8,128)(2,1)S(1)}, bf16[2,8,32,128]{3,2,1,0:T(8,128)(2,1)S(1)}, u32[]{:S(2)}, u32[]{:S(2)}) %collective-permute-start.6) | collective-permute-done | bytes 131104 | tf_op jit(solution)/shard_map/ppermute | solution.py:265
  26.3 0.0 collective-permute-done.5.refs_1_
  26.3 0.1 spread_field.1
  26.5 7.1 %collective-permute-start.9 = (bf16[2,16,32,128]{3,2,1,0:T(8,128)(2,1)S(1)}, bf16[2,16,32,128]{3,2,1,0:T(8,128)(2,1)S(1)}, u32[]{:S(2)}, u32[]{:S(2)}) collective-permute-start(bf16[2,16,32,128]{3,2,1,0:T(8,128)(2,1)S(1)} %get-tuple-element.26), channel_id=1, source_target_pairs={{0,4},{4,0},{8,12},{12,8},{16,20},{20,16},{24,28},{28,24},{32,36},... | collective-permute-start | bytes 786440 | tf_op jit(solution)/shard_map/ppermute | solution.py:272
  33.6 0.0 collective-permute-start.8
  33.6 1.2 %collective-permute-done.9.pair = bf16[2,16,32,128]{3,2,1,0:T(8,128)(2,1)S(1)} collective-permute-done((bf16[2,16,32,128]{3,2,1,0:T(8,128)(2,1)S(1)}, bf16[2,16,32,128]{3,2,1,0:T(8,128)(2,1)S(1)}, u32[]{:S(2)}, u32[]{:S(2)}) %collective-permute-start.9) | collective-permute-done | bytes 262176 | tf_op jit(solution)/shard_map/ppermute | solution.py:272
  34.8 2.6 %near_second.1.part = f32[2,8,32,128]{3,2,1,0:T(8,128)S(1)} custom-call(s32[12,128]{1,0:T(8,128)S(1)} %pad_add_fusion.ints, bf16[2,32,32,128]{3,2,1,0:T(8,128)(2,1)S(1)} %get-tuple-element.25.slab, bf16[2,16,32,128]{3,2,1,0:T(8,128)(2,1)S(1)} %collective-permute-done.9.pair, bf16[2,8,16,128,128]{4,3,2,1,0:T(8,128)(2,1)S(1)} %copy-done.1), custom_call_target="tpu_custom_call" | custom-call | flops 536870912 | bytes 8388608 | tf_op jit(solution)/shard_map/near_second/pallas_call | solution.py:350
  37.4 2.4 %collective-permute-done.8.cross = bf16[2,16,32,128]{3,2,1,0:T(8,128)(2,1)S(1)} collective-permute-done((bf16[2,16,32,128]{3,2,1,0:T(8,128)(2,1)S(1)}, bf16[2,16,32,128]{3,2,1,0:T(8,128)(2,1)S(1)}, u32[]{:S(2)}, u32[]{:S(2)}) %collective-permute-start.8) | collective-permute-done | bytes 262176 | tf_op jit(solution)/shard_map/ppermute | solution.py:271
  39.7 1.6 %apply_second.1 = (bf16[2,8,32,128]{3,2,1,0:T(8,128)(2,1)S(1)}, f32[32,128]{1,0:T(8,128)S(1)}) custom-call(f32[4,128]{1,0:T(4,128)S(1)} %broadcast_in_dim.12.coefs, s32[5,128]{1,0:T(8,128)S(1)} %get-tuple-element.19.table, bf16[8,32,128]{2,1,0:T(8,128)(2,1)S(1)} %get-tuple-element.20.stored, bf16[2,16,32,128]{3,2,1,0:T(8,128)(2,1)S(1)} %collective-permute-done.8.cross, ...), custom_call_target="tpu_custom_call" | custom-call | tf_op jit(solution)/shard_map/apply_second/pallas_call | solution.py:360
  41.4 11.0 %all_to_all.10 = bf16[16,32,128]{2,1,0:T(8,128)(2,1)S(1)} all-to-all(bf16[16,32,128]{2,1,0:T(8,128)(2,1)S(1)} %broadcast_in_dim.13), channel_id=1, replica_groups={{0,1,2,3,8,9,10,11,16,17,18,19,24,25,26,27},{4,5,6,7,12,13,14,15,20,21,..., dimensions={0} | all-to-all | bytes 262144 | tf_op jit(solution)/shard_map/all_to_all | solution.py:244
  52.4 0.7 broadcast_in_dim.28
  53.1 8.2 %all-to-all-start.1 = ((bf16[16,32,128]{2,1,0:T(8,128)(2,1)}), bf16[16,32,128]{2,1,0:T(8,128)(2,1)S(1)}, u32[]{:S(2)}, u32[]{:S(2)}) async-start(bf16[16,32,128]{2,1,0:T(8,128)(2,1)} %broadcast_in_dim.28), calls=%async_computation.1 | async-start | bytes 262144 | tf_op jit(solution)/shard_map/all_to_all | solution.py:244
  61.3 0.9 %collective-permute-start.12 = (bf16[2,8,32,128]{3,2,1,0:T(8,128)(2,1)S(1)}, bf16[2,8,32,128]{3,2,1,0:T(8,128)(2,1)S(1)}, u32[]{:S(2)}, u32[]{:S(2)}) collective-permute-start(bf16[2,8,32,128]{3,2,1,0:T(8,128)(2,1)S(1)} %get-tuple-element.31.refs_0_), channel_id=1, source_target_pairs={{0,2},{1,3},{2,0},{3,1},{4,6},{5,7},{6,4},{7,5},{8,10},{9,11},{10,... | collective-permute-start | bytes 393224 | tf_op jit(solution)/shard_map/ppermute | solution.py:265
  62.2 1.8 %collective-permute-start.11 = (bf16[2,8,32,128]{3,2,1,0:T(8,128)(2,1)S(1)}, bf16[2,8,32,128]{3,2,1,0:T(8,128)(2,1)S(1)}, u32[]{:S(2)}, u32[]{:S(2)}) collective-permute-start(bf16[2,8,32,128]{3,2,1,0:T(8,128)(2,1)S(1)} %get-tuple-element.31.refs_0_), channel_id=1, source_target_pairs={{0,3},{1,2},{2,1},{3,0},{4,7},{5,6},{6,5},{7,4},{8,11},{9,10},{10,... | collective-permute-start | bytes 393224 | tf_op jit(solution)/shard_map/ppermute | solution.py:265
  64.0 0.0 collective-permute-start.10
  64.0 3.8 %collective-permute-done.12.refs_3_ = bf16[2,8,32,128]{3,2,1,0:T(8,128)(2,1)S(1)} collective-permute-done((bf16[2,8,32,128]{3,2,1,0:T(8,128)(2,1)S(1)}, bf16[2,8,32,128]{3,2,1,0:T(8,128)(2,1)S(1)}, u32[]{:S(2)}, u32[]{:S(2)}) %collective-permute-start.12) | collective-permute-done | bytes 131104 | tf_op jit(solution)/shard_map/ppermute | solution.py:265
  67.7 3.3 %collective-permute-done.11.refs_2_ = bf16[2,8,32,128]{3,2,1,0:T(8,128)(2,1)S(1)} collective-permute-done((bf16[2,8,32,128]{3,2,1,0:T(8,128)(2,1)S(1)}, bf16[2,8,32,128]{3,2,1,0:T(8,128)(2,1)S(1)}, u32[]{:S(2)}, u32[]{:S(2)}) %collective-permute-start.11) | collective-permute-done | bytes 131104 | tf_op jit(solution)/shard_map/ppermute | solution.py:265
  71.0 0.0 collective-permute-done.10.refs_1_
  71.0 0.0 all-to-all-done.1.parts
  71.0 0.9 %finish.1 = (bf16[2,32,1024]{2,1,0:T(8,128)(2,1)}, f32[2,2,32,32]{3,2,1,0:T(8,128)}) custom-call(s32[5,128]{1,0:T(8,128)S(1)} %get-tuple-element.19.table, bf16[16,32,128]{2,1,0:T(8,128)(2,1)S(1)} %all-to-all-done.1.parts, bf16[2,8,32,128]{3,2,1,0:T(8,128)(2,1)S(1)} %get-tuple-element.31.refs_0_, ...), custom_call_target="tpu_custom_call" | custom-call | tf_op jit(solution)/shard_map/finish/pallas_call | solution.py:387
  (5 shorter events, 0.1 us)
Async XLA Ops:
  0.6 9.6 %collective-permute-start = (bf16[32,1024]{1,0:T(8,128)(2,1)}, bf16[32,1024]{1,0:T(8,128)(2,1)S(1)}, u32[]{:S(2)}, u32[]{:S(2)}) collective-permute-start(bf16[32,1024]{1,0:T(8,128)(2,1)} %panel.1), channel_id=1, source_target_pairs={{0,1},{1,0},{2,3},{3,2},{4,5},{5,4},{6,7},{7,6},{8,9},{9,8},{10,11... | collective-permute-start | bytes 196616 | tf_op jit(solution)/shard_map/ppermute | solution.py:265
  2.8 7.4 %collective-permute-start.2 = (bf16[32,1024]{1,0:T(8,128)(2,1)}, bf16[32,1024]{1,0:T(8,128)(2,1)S(1)}, u32[]{:S(2)}, u32[]{:S(2)}) collective-permute-start(bf16[32,1024]{1,0:T(8,128)(2,1)} %panel.1), channel_id=1, source_target_pairs={{0,2},{1,3},{2,0},{3,1},{4,6},{5,7},{6,4},{7,5},{8,10},{9,11},{10,... | collective-permute-start | bytes 196616 | tf_op jit(solution)/shard_map/ppermute | solution.py:265
  5.2 5.0 %collective-permute-start.1 = (bf16[32,1024]{1,0:T(8,128)(2,1)}, bf16[32,1024]{1,0:T(8,128)(2,1)S(1)}, u32[]{:S(2)}, u32[]{:S(2)}) collective-permute-start(bf16[32,1024]{1,0:T(8,128)(2,1)} %panel.1), channel_id=1, source_target_pairs={{0,3},{1,2},{2,1},{3,0},{4,7},{5,6},{6,5},{7,4},{8,11},{9,10},{10,... | collective-permute-start | bytes 196616 | tf_op jit(solution)/shard_map/ppermute | solution.py:265
  5.3 3.4 %copy-start = (bf16[2,8,16,128,128]{4,3,2,1,0:T(8,128)(2,1)S(1)}, bf16[2,8,16,128,128]{4,3,2,1,0:T(8,128)(2,1)}, u32[]{:S(2)}) copy-start(bf16[2,8,16,128,128]{4,3,2,1,0:T(8,128)(2,1)} %tiles.9) | copy-start | bytes 25165828
  8.6 0.8 %copy-start.2 = (bf16[32,1024]{1,0:T(8,128)(2,1)S(1)}, bf16[32,1024]{1,0:T(8,128)(2,1)}, u32[]{:S(2)}) copy-start(bf16[32,1024]{1,0:T(8,128)(2,1)} %panel.1) | copy-start | bytes 196612
  9.5 0.7 copy-start.3
  9.5 0.7 copy-start.4
  9.5 0.7 copy-start.5
  9.5 0.7 copy-start.6
  9.5 4.4 %copy-start.7 = (f32[2]{0:T(128)S(1)}, f32[2]{0:T(128)}, u32[]{:S(2)}) copy-start(f32[2]{0:T(128)} %param.15) | copy-start | bytes 28
  9.5 4.4 %copy-start.8 = (f32[2]{0:T(128)S(1)}, f32[2]{0:T(128)}, u32[]{:S(2)}) copy-start(f32[2]{0:T(128)} %param.14) | copy-start | bytes 28
  9.5 5.4 %copy-start.1 = (bf16[2,8,16,128,128]{4,3,2,1,0:T(8,128)(2,1)S(1)}, bf16[2,8,16,128,128]{4,3,2,1,0:T(8,128)(2,1)}, u32[]{:S(2)}) copy-start(bf16[2,8,16,128,128]{4,3,2,1,0:T(8,128)(2,1)} %tiles.9) | copy-start | bytes 25165828
  10.4 4.5 %collective-permute-start.3 = (bf16[16,32,128]{2,1,0:T(8,128)(2,1)S(1)}, bf16[16,32,128]{2,1,0:T(8,128)(2,1)S(1)}, u32[]{:S(2)}, u32[]{:S(2)}) collective-permute-start(bf16[16,32,128]{2,1,0:T(8,128)(2,1)S(1)} %get-tuple-element.18), channel_id=1, source_target_pairs={{0,4},{4,0},{8,12},{12,8},{16,20},{20,16},{24,28},{28,24},{32,36},... | collective-permute-start | bytes 393224 | tf_op jit(solution)/shard_map/ppermute | solution.py:272
  13.9 4.4 %collective-permute-start.4 = (bf16[16,32,128]{2,1,0:T(8,128)(2,1)S(1)}, bf16[16,32,128]{2,1,0:T(8,128)(2,1)S(1)}, u32[]{:S(2)}, u32[]{:S(2)}) collective-permute-start(bf16[16,32,128]{2,1,0:T(8,128)(2,1)S(1)} %get-tuple-element.21), channel_id=1, source_target_pairs={{0,252},{4,8},{8,4},{12,16},{16,12},{20,24},{24,20},{28,32},{32,28... | collective-permute-start | bytes 393224 | tf_op jit(solution)/shard_map/ppermute | solution.py:271
  19.8 5.4 %collective-permute-start.7 = (bf16[2,8,32,128]{3,2,1,0:T(8,128)(2,1)S(1)}, bf16[2,8,32,128]{3,2,1,0:T(8,128)(2,1)S(1)}, u32[]{:S(2)}, u32[]{:S(2)}) collective-permute-start(bf16[2,8,32,128]{3,2,1,0:T(8,128)(2,1)S(1)} %get-tuple-element.23.refs_0_.first), channel_id=1, source_target_pairs={{0,2},{1,3},{2,0},{3,1},{4,6},{5,7},{6,4},{7,5},{8,10},{9,11},{10,... | collective-permute-start | bytes 393224 | tf_op jit(solution)/shard_map/ppermute | solution.py:265
  19.8 6.5 %collective-permute-start.6 = (bf16[2,8,32,128]{3,2,1,0:T(8,128)(2,1)S(1)}, bf16[2,8,32,128]{3,2,1,0:T(8,128)(2,1)S(1)}, u32[]{:S(2)}, u32[]{:S(2)}) collective-permute-start(bf16[2,8,32,128]{3,2,1,0:T(8,128)(2,1)S(1)} %get-tuple-element.23.refs_0_.first), channel_id=1, source_target_pairs={{0,3},{1,2},{2,1},{3,0},{4,7},{5,6},{6,5},{7,4},{8,11},{9,10},{10,... | collective-permute-start | bytes 393224 | tf_op jit(solution)/shard_map/ppermute | solution.py:265
  20.7 5.6 %collective-permute-start.5 = (bf16[2,8,32,128]{3,2,1,0:T(8,128)(2,1)S(1)}, bf16[2,8,32,128]{3,2,1,0:T(8,128)(2,1)S(1)}, u32[]{:S(2)}, u32[]{:S(2)}) collective-permute-start(bf16[2,8,32,128]{3,2,1,0:T(8,128)(2,1)S(1)} %get-tuple-element.23.refs_0_.first), channel_id=1, source_target_pairs={{0,1},{1,0},{2,3},{3,2},{4,5},{5,4},{6,7},{7,6},{8,9},{9,8},{10,11... | collective-permute-start | bytes 393224 | tf_op jit(solution)/shard_map/ppermute | solution.py:265
  26.5 8.3 %collective-permute-start.9 = (bf16[2,16,32,128]{3,2,1,0:T(8,128)(2,1)S(1)}, bf16[2,16,32,128]{3,2,1,0:T(8,128)(2,1)S(1)}, u32[]{:S(2)}, u32[]{:S(2)}) collective-permute-start(bf16[2,16,32,128]{3,2,1,0:T(8,128)(2,1)S(1)} %get-tuple-element.26), channel_id=1, source_target_pairs={{0,4},{4,0},{8,12},{12,8},{16,20},{20,16},{24,28},{28,24},{32,36},... | collective-permute-start | bytes 786440 | tf_op jit(solution)/shard_map/ppermute | solution.py:272
  33.6 6.1 %collective-permute-start.8 = (bf16[2,16,32,128]{3,2,1,0:T(8,128)(2,1)S(1)}, bf16[2,16,32,128]{3,2,1,0:T(8,128)(2,1)S(1)}, u32[]{:S(2)}, u32[]{:S(2)}) collective-permute-start(bf16[2,16,32,128]{3,2,1,0:T(8,128)(2,1)S(1)} %get-tuple-element.24), channel_id=1, source_target_pairs={{0,252},{4,8},{8,4},{12,16},{16,12},{20,24},{24,20},{28,32},{32,28... | collective-permute-start | bytes 786440 | tf_op jit(solution)/shard_map/ppermute | solution.py:271
  53.1 18.0 %all-to-all-start.1 = ((bf16[16,32,128]{2,1,0:T(8,128)(2,1)}), bf16[16,32,128]{2,1,0:T(8,128)(2,1)S(1)}, u32[]{:S(2)}, u32[]{:S(2)}) async-start(bf16[16,32,128]{2,1,0:T(8,128)(2,1)} %broadcast_in_dim.28), calls=%async_computation.1 | async-start | bytes 262144 | tf_op jit(solution)/shard_map/all_to_all | solution.py:244
  61.3 6.4 %collective-permute-start.12 = (bf16[2,8,32,128]{3,2,1,0:T(8,128)(2,1)S(1)}, bf16[2,8,32,128]{3,2,1,0:T(8,128)(2,1)S(1)}, u32[]{:S(2)}, u32[]{:S(2)}) collective-permute-start(bf16[2,8,32,128]{3,2,1,0:T(8,128)(2,1)S(1)} %get-tuple-element.31.refs_0_), channel_id=1, source_target_pairs={{0,2},{1,3},{2,0},{3,1},{4,6},{5,7},{6,4},{7,5},{8,10},{9,11},{10,... | collective-permute-start | bytes 393224 | tf_op jit(solution)/shard_map/ppermute | solution.py:265
  62.2 8.8 %collective-permute-start.11 = (bf16[2,8,32,128]{3,2,1,0:T(8,128)(2,1)S(1)}, bf16[2,8,32,128]{3,2,1,0:T(8,128)(2,1)S(1)}, u32[]{:S(2)}, u32[]{:S(2)}) collective-permute-start(bf16[2,8,32,128]{3,2,1,0:T(8,128)(2,1)S(1)} %get-tuple-element.31.refs_0_), channel_id=1, source_target_pairs={{0,3},{1,2},{2,1},{3,0},{4,7},{5,6},{6,5},{7,4},{8,11},{9,10},{10,... | collective-permute-start | bytes 393224 | tf_op jit(solution)/shard_map/ppermute | solution.py:265
  64.0 7.1 %collective-permute-start.10 = (bf16[2,8,32,128]{3,2,1,0:T(8,128)(2,1)S(1)}, bf16[2,8,32,128]{3,2,1,0:T(8,128)(2,1)S(1)}, u32[]{:S(2)}, u32[]{:S(2)}) collective-permute-start(bf16[2,8,32,128]{3,2,1,0:T(8,128)(2,1)S(1)} %get-tuple-element.31.refs_0_), channel_id=1, source_target_pairs={{0,1},{1,0},{2,3},{3,2},{4,5},{5,4},{6,7},{7,6},{8,9},{9,8},{10,11... | collective-permute-start | bytes 393224 | tf_op jit(solution)/shard_map/ppermute | solution.py:265
